TPU v7x, 128 devices: a whole 4x4x4 slice. The times are simulated.
128 devices in a mesh: dp: 16 (over x, z), mp: 8 (over y, core).
Axes of the slice: x: 4, y: 4, z: 4, core: 2. Of those that a mesh axis runs over, the one named last changes fastest.
Arguments:
- query: bfloat16 [4, 1280, 8192], P(None, 'dp', 'mp'), may hold values from -80 to 80
- token_keys: bfloat16 [4, 1280, 1024], P(None, 'dp', 'mp'), may hold values from -5 to 5
- token_values: bfloat16 [4, 1280, 1024], P(None, 'dp', 'mp'), may hold values from -5 to 5
- cache_keys: bfloat16 [1280, 8, 128, 128], P('dp', 'mp'), may hold values from -4 to 4
- stored_values: bfloat16 [1280, 8, 128, 128], P('dp', 'mp'), may hold values from -5 to 5
- lengths: int32 [1280], P('dp'), may hold values from 1 to 128, as said below
- talker_row: int32 [1280], P('dp'), may hold values from 0 to 1279, as said below
- residual: bfloat16 [4, 1280, 8192], P(None, 'dp', 'mp'), may hold values from -2 to 2
- embedding: bfloat16 [4, 1280, 8192], P(None, 'dp', 'mp'), may hold values from -6 to 6
- out_weight: bfloat16 [8192, 8192], P('mp'), may hold values from -0.0625 to 0.0625
- talker_proj: bfloat16 [8192, 3584], P(None, 'mp'), may hold values from -2 to 2
- talker_gain: bfloat16 [3584], P('mp'), may hold values from 0.25 to 1.75
Outputs:
- hidden: bfloat16 [4, 1280, 8192], P(None, 'dp', 'mp')
- talker_input: bfloat16 [4, 1280, 3584], P(None, 'dp', 'mp')
Inputs may be any that keep to these rules, and one draw needn't show every extreme that they name: `lengths`: some stream has all 128 slots filled. `talker_row`: A permutation of the streams. Streams of one index of dp (rows of one device) land in at most 10 rows of any one talker shard of 80 rows, and exactly 10 in every shard they reach.
All inputs are finite; a program needn't handle non-finite values.
Results may differ from a plain program's by a relative error of at most 0.015.
Values may be sent and summed in bfloat16 or wider, within the bound.
No kernel may reach another device: no remote copies, remote signals or barrier semaphores. Data moves between devices by JAX's collectives and lax.ppermute only.
A program may use at most 128 MiB of HBM per device.

v0:
```python
import jax
import jax.numpy as jnp
from jax import lax
from jax.sharding import PartitionSpec as P

epsilon = 1e-06


def local(
    query,
    token_keys,
    token_values,
    cache_keys,
    stored_values,
    lengths,
    talker_row,
    residual,
    embedding,
    out_weight,
    talker_proj,
    talker_gain,
):
    step_count, row_count, query_cols = query.shape
    head_dim = cache_keys.shape[3]
    kv_local = cache_keys.shape[1]
    slot_count = cache_keys.shape[2]
    query_groups = query_cols // (kv_local * head_dim)
    score_scale = 1.0 / head_dim**0.5
    query_rows = query.reshape(step_count, row_count, kv_local, query_groups, head_dim)
    cache_scores = (
        jnp.einsum("tskgd,skld->tskgl", query_rows, cache_keys, preferred_element_type=jnp.float32)
        * score_scale
    )
    filled = jnp.arange(slot_count, dtype=jnp.int32)[None, :] < lengths[:, None]
    cache_scores = jnp.where(filled[None, :, None, None, :], cache_scores, jnp.float32(-1e30))
    recent_keys = token_keys.reshape(step_count, row_count, kv_local, head_dim)
    fresh_scores = (
        jnp.einsum("tskgd,uskd->tskgu", query_rows, recent_keys, preferred_element_type=jnp.float32)
        * score_scale
    )
    causal = jnp.arange(step_count)[None, :] <= jnp.arange(step_count)[:, None]
    fresh_scores = jnp.where(causal[:, None, None, None, :], fresh_scores, jnp.float32(-1e30))
    highest = jnp.maximum(jnp.max(cache_scores, -1), jnp.max(fresh_scores, -1))[..., None]
    cache_exp = jnp.exp(cache_scores - highest)
    fresh_exp = jnp.exp(fresh_scores - highest)
    denominator = jnp.sum(cache_exp, -1, keepdims=True) + jnp.sum(fresh_exp, -1, keepdims=True)
    cache_weights = (cache_exp / denominator).astype(jnp.bfloat16)
    fresh_weights = (fresh_exp / denominator).astype(jnp.bfloat16)
    recent_values = token_values.reshape(step_count, row_count, kv_local, head_dim)
    context = jnp.einsum(
        "tskgl,skld->tskgd", cache_weights, stored_values, preferred_element_type=jnp.float32
    )
    context = context + jnp.einsum(
        "tskgu,uskd->tskgd", fresh_weights, recent_values, preferred_element_type=jnp.float32
    )
    context = context.astype(jnp.bfloat16).reshape(step_count * row_count, query_cols)
    head_partial = jnp.dot(context, out_weight, preferred_element_type=jnp.float32).reshape(
        step_count, row_count, -1
    )
    summed = lax.psum_scatter(
        head_partial.astype(jnp.bfloat16), "mp", scatter_dimension=2, tiled=True
    ).astype(jnp.float32)
    hidden = (residual.astype(jnp.float32) + summed).astype(jnp.bfloat16)
    own_index = lax.axis_index("dp")
    all_hidden, all_embed, all_rows = (
        lax.all_gather(hidden, "dp", axis=1, tiled=True),
        lax.all_gather(embedding, "dp", axis=1, tiled=True),
        lax.all_gather(talker_row[None, :], "dp", axis=1, tiled=True),
    )
    total_rows = all_rows.shape[1]
    inverse = (
        jnp.zeros((total_rows,), jnp.int32)
        .at[all_rows[0]]
        .set(jnp.arange(total_rows, dtype=jnp.int32))
    )
    wanted = lax.dynamic_slice_in_dim(inverse, own_index * row_count, row_count)
    mine_hidden = jnp.take(all_hidden, wanted, axis=1)
    mine_embed = jnp.take(all_embed, wanted, axis=1)
    talk_cols = talker_proj.shape[1]
    piece_hidden = lax.all_gather(mine_hidden, "mp", axis=2, tiled=True)
    piece_embed = lax.all_gather(mine_embed, "mp", axis=2, tiled=True)
    running = jnp.einsum(
        "tsd,dc->tsc", piece_hidden, talker_proj, preferred_element_type=jnp.float32
    )
    mixed = running + jnp.einsum(
        "tsd,dc->tsc", piece_embed, talker_proj, preferred_element_type=jnp.float32
    )
    squares = lax.psum(jnp.sum(mixed * mixed, -1), "mp")
    talk_width = talk_cols * lax.axis_size("mp")
    normed = (
        mixed
        * lax.rsqrt(squares / talk_width + epsilon)[..., None]
        * talker_gain.astype(jnp.float32)
    )
    return (hidden, normed.astype(jnp.bfloat16))


def solution(mesh):
    placed = (
        P(None, "dp", "mp"),
        P(None, "dp", "mp"),
        P(None, "dp", "mp"),
        P("dp", "mp", None, None),
        P("dp", "mp", None, None),
        P("dp"),
        P("dp"),
        P(None, "dp", "mp"),
        P(None, "dp", "mp"),
        P("mp", None),
        P(None, "mp"),
        P("mp"),
    )
    return jax.shard_map(
        local,
        mesh=mesh,
        in_specs=placed,
        out_specs=(P(None, "dp", "mp"), P(None, "dp", "mp")),
        check_vma=False,
    )
```

profile of v0, /device:TPU:0, one launch (start us, length us, event | category | flops | bytes accessed | tf_op | source)
XLA Modules:
  0.0 325.8 jit_solution(17148340591246658376)
XLA Ops:
  8.0 0.0 copy-start
  8.0 0.0 reduce-scatter.2.cloned.1.call-start
  8.1 1.4 copy.45
  9.4 0.0 copy-start.6
  9.4 0.8 iota_compare_fusion
  10.2 0.0 copy-done
  10.2 1.6 bitcast_reduce_fusion
  11.9 0.0 copy-done.6
  11.9 0.0 copy-start.5
  11.9 3.0 fusion.46
  15.0 0.6 fusion.38
  15.6 0.9 fusion.29
  16.5 0.0 copy-done.5
  16.5 0.0 copy-start.7
  16.6 1.1 fusion.9
  17.7 0.0 copy-done.7
  17.7 0.6 fusion.25
  18.3 0.2 dot_general.27
  18.4 13.2 %fusion.2 = bf16[4,80,8192]{2,1,0:T(8,128)(2,1)} fusion(bf16[1024,8192]{1,0:T(8,128)(2,1)} %param.23, bf16[4,80,1024]{2,0,1:T(4,128)(2,1)S(1)} %dot_general.27), kind=kOutput, calls=%fused_computation.5 | convolution fusion | flops 5371330560 | bytes 22675456 | tf_op jit(solution)/shard_map/dot_general | solution.py:57
  31.6 0.0 copy-start.2
  31.6 0.0 copy-start.3
  31.6 0.0 reduce-scatter.2.cloned.1.call-update
  31.7 0.0 copy-start.9
  31.7 0.0 copy-start.8
  31.7 0.0 all-gather.10.cloned.1.call-start
  31.7 1.0 copy-done.2
  32.7 1.4 copy.35
  34.1 0.0 all-gather.10.cloned.1.call-update
  34.1 0.0 all-gather.6.cloned.1.call-start
  34.2 40.8 %reduce-scatter.2.cloned.1.call-done = bf16[4,80,1024]{2,1,0:T(8,128)(2,1)} async-done(((bf16[4,80,8192]{2,1,0:T(8,128)(2,1)}), bf16[4,80,1024]{2,1,0:T(8,128)(2,1)}) %reduce-scatter.2.cloned.1.call-update) | async-done | bytes 655376 | tf_op jit(solution)/shard_map/reduce_scatter | solution.py:60
  74.9 0.0 copy-done.3
  75.0 2.2 add_convert_fusion
  77.1 0.0 all-gather.6.cloned.1.call-update
  77.1 0.0 all-gather.12.cloned.1.call-start
  77.2 0.0 copy-done.9
  77.2 0.6 dynamic-slice
  78.5 0.0 copy-done.8
  78.5 0.3 dynamic-update-slice
  78.7 17.1 %all-reduce = s32[1280]{0:T(1024)S(1)} all-reduce(s32[1280]{0:T(1024)S(1)} %dynamic-update-slice), channel_id=2, replica_groups=mesh['dp'=16,'mp'=8] {'dp'}, use_global_device_ids=true, to_apply=%add | all-reduce | flops 1280 | bytes 10240
  95.9 5.4 %scatter_custom_fusion = s32[1280]{0:T(1024)S(1)} fusion(s32[1280]{0:T(1024)S(1)} %fusion.43, s32[1280]{0:T(1024)S(1)} %iota.25, s32[]{:T(128)} %constant.6.clone.1), kind=kCustom, calls=%fused_computation.52 | custom fusion | bytes 5124 | tf_op jit(solution)/shard_map/scatter | solution.py:74
  101.4 0.1 compare_and_fusion
  101.4 16.3 %all-gather.10.cloned.1.call-done = bf16[4,1280,1024]{2,0,1:T(4,128)(2,1)} async-done(((bf16[4,80,1024]{2,0,1:T(4,128)(2,1)}), bf16[4,1280,1024]{2,0,1:T(4,128)(2,1)}) %all-gather.10.cloned.1.call-update) | async-done | bytes 10485776 | tf_op jit(solution)/shard_map/all_gather | solution.py:67
  117.7 5.1 %gather_fusion.1 = bf16[80,4,1024]{2,1,0:T(4,128)(2,1)S(1)} fusion(bf16[4,1280,1024]{2,0,1:T(4,128)(2,1)} %all-gather.10.cloned.1.call-done, s32[1024]{0:T(1024)S(1)} %pad_clamp_fusion), kind=kCustom, calls=%fused_computation.1.clone | custom fusion | bytes 1311040 | tf_op jit(solution)/shard_map/jit(_take)/gather | solution.py:78
  122.8 78.0 %all-gather.6.cloned.1.call-done = bf16[4,1280,1024]{2,1,0:T(8,128)(2,1)} async-done(((bf16[4,80,1024]{2,1,0:T(8,128)(2,1)}), bf16[4,1280,1024]{2,1,0:T(8,128)(2,1)}) %all-gather.6.cloned.1.call-update) | async-done | bytes 10485776 | tf_op jit(solution)/shard_map/all_gather | solution.py:66
  200.8 14.6 %copy.33 = bf16[4,1280,1024]{2,0,1:T(4,128)(2,1)} copy(bf16[4,1280,1024]{2,1,0:T(8,128)(2,1)} %all-gather.6.cloned.1.call-done) | data formatting | bytes 20971520 | tf_op jit(solution)/shard_map/all_gather | solution.py:66
  215.4 0.0 copy-start.4
  215.4 5.1 %gather_fusion = bf16[80,4,1024]{2,1,0:T(4,128)(2,1)S(1)} fusion(bf16[4,1280,1024]{2,0,1:T(4,128)(2,1)} %copy.33, s32[1024]{0:T(1024)S(1)} %pad_clamp_fusion), kind=kCustom, calls=%fused_computation.clone | custom fusion | bytes 1311040 | tf_op jit(solution)/shard_map/jit(_take)/gather | solution.py:77
  220.5 1.9 fusion.33
  222.4 0.0 all-gather.12.cloned.1.call-update
  222.4 0.0 all-gather.8.cloned.1.call-start
  222.5 0.7 all-gather.8.cloned.1.call-update
  223.2 0.0 copy-done.4
  223.2 35.5 %all-gather.12.cloned.1.call-done = bf16[4,80,8192]{2,1,0:T(8,128)(2,1)} async-done(((bf16[4,80,1024]{2,1,0:T(8,128)(2,1)}), bf16[4,80,8192]{2,1,0:T(8,128)(2,1)}) %all-gather.12.cloned.1.call-update) | async-done | bytes 5242896 | tf_op jit(solution)/shard_map/all_gather | solution.py:81
  258.7 8.4 %fusion.5 = f32[4,80,448]{2,1,0:T(8,128)} fusion(bf16[4,80,8192]{2,1,0:T(8,128)(2,1)} %all-gather.12.cloned.1.call-done, bf16[8192,448]{0,1:T(8,128)(2,1)} %param.24), kind=kOutput, calls=%fused_computation.6 | convolution fusion | flops 2348810240 | bytes 13156352 | tf_op jit(solution)/shard_map/tsd,dc->tsc/dot_general | solution.py:85
  267.1 29.9 %all-gather.8.cloned.1.call-done = bf16[4,80,8192]{2,1,0:T(8,128)(2,1)} async-done(((bf16[4,80,1024]{2,1,0:T(8,128)(2,1)}), bf16[4,80,8192]{2,1,0:T(8,128)(2,1)}) %all-gather.8.cloned.1.call-update) | async-done | bytes 5242896 | tf_op jit(solution)/shard_map/all_gather | solution.py:80
  296.9 0.0 copy-start.1
  296.9 7.8 %multiply_reduce_fusion = (f32[4,80]{1,0:T(4,128)S(1)}, f32[4,80,448]{2,1,0:T(8,128)S(1)}) fusion(f32[4,80,448]{2,1,0:T(8,128)} %fusion.5, bf16[4,80,8192]{2,1,0:T(8,128)(2,1)} %all-gather.8.cloned.1.call-done, bf16[8192,448]{0,1:T(8,128)(2,1)} %param.24), kind=kOutput, calls=%fused_computation.37 | convolution fusion | flops 2349240064 | bytes 13731072 | tf_op jit(solution)/shard_map/tsd,dc->tsc/dot_general | solution.py:82
  304.7 13.1 %psum.7 = f32[4,80]{1,0:T(4,128)S(1)} all-reduce(f32[4,80]{1,0:T(4,128)S(1)} %get-tuple-element.11), channel_id=1, replica_groups=mesh['dp'=16,'mp'=8] {'mp'}, use_global_device_ids=true, to_apply=%region_7.9 | all-reduce | flops 320 | bytes 2560 | tf_op jit(solution)/shard_map/psum | solution.py:88
  317.9 0.9 multiply_convert_fusion
  318.7 0.0 copy-done.1
  (9 shorter events, 0.1 us)
Async XLA Ops:
  8.0 2.2 copy-start
  8.0 66.9 %reduce-scatter.2.cloned.1.call-start = ((), (), s32[]{:S(2)}) async-start(), calls=%async_computation.1 | async-start | bytes 5898240 | tf_op jit(solution)/shard_map/reduce_scatter | solution.py:60
  9.4 2.4 copy-start.6
  11.9 4.7 %copy-start.5 = (bf16[80,1,128,128]{3,2,1,0:T(8,128)(2,1)S(1)}, bf16[80,1,128,128]{3,2,1,0:T(8,128)(2,1)}, u32[]{:S(2)}) copy-start(bf16[80,1,128,128]{3,2,1,0:T(8,128)(2,1)} %param.18) | copy-start | bytes 7864324
  16.5 1.1 copy-start.7
  31.6 1.1 copy-start.2
  31.6 43.3 %copy-start.3 = (bf16[4,80,1024]{2,1,0:T(8,128)(2,1)S(1)}, bf16[4,80,1024]{2,1,0:T(8,128)(2,1)}, u32[]{:S(2)}) copy-start(bf16[4,80,1024]{2,1,0:T(8,128)(2,1)} %param.21) | copy-start | bytes 1966084
  31.7 45.5 %copy-start.9 = (u32[128]{0:T(128)S(1)}, u32[128]{0:T(128)}, u32[]{:S(2)}) copy-start(u32[128]{0:T(128)} %constant.42) | copy-start | bytes 1540
  31.7 46.8 %copy-start.8 = (s32[80]{0:T(128)S(1)}, s32[80]{0:T(128)}, u32[]{:S(2)}) copy-start(s32[80]{0:T(128)} %param.20) | copy-start | bytes 964
  31.7 86.0 %all-gather.10.cloned.1.call-start = ((), (), s32[]{:S(2)}) async-start(), calls=%async_computation.4 | async-start | bytes 11141120 | tf_op jit(solution)/shard_map/all_gather | solution.py:67
  34.1 166.6 %all-gather.6.cloned.1.call-start = ((), (), s32[]{:S(2)}) async-start(), calls=%async_computation.2 | async-start | bytes 11141120 | tf_op jit(solution)/shard_map/all_gather | solution.py:66
  77.1 181.5 %all-gather.12.cloned.1.call-start = ((), (), s32[]{:S(2)}) async-start(), calls=%async_computation.5 | async-start | bytes 5898240 | tf_op jit(solution)/shard_map/all_gather | solution.py:81
  215.4 7.8 %copy-start.4 = (bf16[448]{0:T(512)(128)(2,1)S(1)}, bf16[448]{0:T(512)(128)(2,1)}, u32[]{:S(2)}) copy-start(bf16[448]{0:T(512)(128)(2,1)} %param.25) | copy-start | bytes 2692
  222.4 74.5 %all-gather.8.cloned.1.call-start = ((), (), s32[]{:S(2)}) async-start(), calls=%async_computation.3 | async-start | bytes 5898240 | tf_op jit(solution)/shard_map/all_gather | solution.py:80
  296.9 21.8 %copy-start.1 = (bf16[80,1,128,128]{3,2,1,0:T(8,128)(2,1)S(1)}, bf16[80,1,128,128]{3,2,1,0:T(8,128)(2,1)}, u32[]{:S(2)}) copy-start(bf16[80,1,128,128]{3,2,1,0:T(8,128)(2,1)} %param.17) | copy-start | bytes 7864324
Sparse Core Ops, SparseCore 0:
  31.8 43.1 reduce-scatter.1
  222.6 36.0 all-gather.11
  260.4 36.5 all-gather.7
Sparse Core Ops, SparseCore 1:
  34.4 83.3 all-gather.9
  120.3 80.4 all-gather.5
where the time goes:
time: 326 us
  waiting for transfers between devices  201 us (62%)
  matrix products  35.7 us (11%)
  local copies, waits for them, and re-layouts  35 us (11%)
  blocking collectives  30.2 us (9%)
  between operations  16.1 us (5%)
  other arithmetic  7.45 us (2%)
    all_gather x1, waiting for transfers between devices, local(): lax.all_gather(hidden, 'dp', axis=1, tiled=True)  78 us
    reduce_scatter x1, waiting for transfers between devices, local(): lax.psum_scatter(head_partial.astype(jnp.bfloat16), 'mp', scatter_dimensi...  40.8 us
    all_gather x1, waiting for transfers between devices, local(): piece_embed = lax.all_gather(mine_embed, 'mp', axis=2, tiled=True)  35.5 us
    all_gather x1, waiting for transfers between devices, local(): piece_hidden = lax.all_gather(mine_hidden, 'mp', axis=2, tiled=True)  29.9 us
    unnamed x1, blocking collectives  17.1 us
    all_gather x1, waiting for transfers between devices, local(): lax.all_gather(embedding, 'dp', axis=1, tiled=True)  16.3 us
    all_gather x1, local copies, waits for them, and re-layouts, local(): lax.all_gather(hidden, 'dp', axis=1, tiled=True)  14.6 us
    dot_general x1, matrix products, local(): jnp.dot(context, out_weight, preferred_element_type=jnp.float32)  13.2 us
  transfers between devices with their start and end apart: 5, of which 5 were waited for; matrix products, arithmetic and copies ran while one was open for 7% of the time, Pallas kernels for 0%

commit v1 on v0

--- a/solution.py
+++ b/solution.py
@@ -4,22 +4,10 @@
 from jax.sharding import PartitionSpec as P
 
 epsilon = 1e-06
+CAP = 10
 
 
-def local(
-    query,
-    token_keys,
-    token_values,
-    cache_keys,
-    stored_values,
-    lengths,
-    talker_row,
-    residual,
-    embedding,
-    out_weight,
-    talker_proj,
-    talker_gain,
-):
+def attend(query, token_keys, token_values, cache_keys, stored_values, lengths):
     step_count, row_count, query_cols = query.shape
     head_dim = cache_keys.shape[3]
     kv_local = cache_keys.shape[1]
@@ -53,7 +41,35 @@
     context = context + jnp.einsum(
         "tskgu,uskd->tskgd", fresh_weights, recent_values, preferred_element_type=jnp.float32
     )
-    context = context.astype(jnp.bfloat16).reshape(step_count * row_count, query_cols)
+    return context.astype(jnp.bfloat16).reshape(step_count * row_count, query_cols)
+
+
+def local(
+    query,
+    token_keys,
+    token_values,
+    cache_keys,
+    stored_values,
+    lengths,
+    talker_row,
+    residual,
+    embedding,
+    out_weight,
+    talker_proj,
+    talker_gain,
+):
+    step_count, row_count, query_cols = query.shape
+    n_dp = lax.axis_size("dp")
+    shard = talker_row // row_count
+    place = talker_row % row_count
+    same = shard[None, :] == shard[:, None]
+    earlier = jnp.arange(row_count)[None, :] < jnp.arange(row_count)[:, None]
+    slot = shard * CAP + jnp.sum((same & earlier).astype(jnp.int32), 1)
+    pick = slot[None, :] == jnp.arange(n_dp * CAP, dtype=jnp.int32)[:, None]
+    sent_place = jnp.sum(jnp.where(pick, place[None, :] + 1, 0), 1).reshape(n_dp, CAP) - 1
+    got_place = lax.all_to_all(sent_place, "dp", 0, 0, tiled=True).reshape(n_dp * CAP)
+
+    context = attend(query, token_keys, token_values, cache_keys, stored_values, lengths)
     head_partial = jnp.dot(context, out_weight, preferred_element_type=jnp.float32).reshape(
         step_count, row_count, -1
     )
@@ -61,38 +77,22 @@
         head_partial.astype(jnp.bfloat16), "mp", scatter_dimension=2, tiled=True
     ).astype(jnp.float32)
     hidden = (residual.astype(jnp.float32) + summed).astype(jnp.bfloat16)
-    own_index = lax.axis_index("dp")
-    all_hidden, all_embed, all_rows = (
-        lax.all_gather(hidden, "dp", axis=1, tiled=True),
-        lax.all_gather(embedding, "dp", axis=1, tiled=True),
-        lax.all_gather(talker_row[None, :], "dp", axis=1, tiled=True),
-    )
-    total_rows = all_rows.shape[1]
-    inverse = (
-        jnp.zeros((total_rows,), jnp.int32)
-        .at[all_rows[0]]
-        .set(jnp.arange(total_rows, dtype=jnp.int32))
-    )
-    wanted = lax.dynamic_slice_in_dim(inverse, own_index * row_count, row_count)
-    mine_hidden = jnp.take(all_hidden, wanted, axis=1)
-    mine_embed = jnp.take(all_embed, wanted, axis=1)
+    both = hidden + embedding
+    piece = lax.all_gather(both, "mp", axis=2, tiled=True)
+    mixed = jnp.einsum("tsd,dc->tsc", piece, talker_proj, preferred_element_type=jnp.float32)
     talk_cols = talker_proj.shape[1]
-    piece_hidden = lax.all_gather(mine_hidden, "mp", axis=2, tiled=True)
-    piece_embed = lax.all_gather(mine_embed, "mp", axis=2, tiled=True)
-    running = jnp.einsum(
-        "tsd,dc->tsc", piece_hidden, talker_proj, preferred_element_type=jnp.float32
-    )
-    mixed = running + jnp.einsum(
-        "tsd,dc->tsc", piece_embed, talker_proj, preferred_element_type=jnp.float32
-    )
     squares = lax.psum(jnp.sum(mixed * mixed, -1), "mp")
     talk_width = talk_cols * lax.axis_size("mp")
     normed = (
         mixed
         * lax.rsqrt(squares / talk_width + epsilon)[..., None]
         * talker_gain.astype(jnp.float32)
-    )
-    return (hidden, normed.astype(jnp.bfloat16))
+    ).astype(jnp.bfloat16)
+    sent = jnp.einsum("ks,tsc->ktc", pick.astype(jnp.bfloat16), normed)
+    got = lax.all_to_all(sent, "dp", 0, 0, tiled=True)
+    put = got_place[None, :] == jnp.arange(row_count, dtype=jnp.int32)[:, None]
+    talker_input = jnp.einsum("sk,ktc->tsc", put.astype(jnp.bfloat16), got)
+    return (hidden, talker_input.astype(jnp.bfloat16))
 
 
 def solution(mesh):

time: 326 us -> 164 us (0.50)
  waiting for transfers between devices: 201 us -> 81.6 us
  local copies, waits for them, and re-layouts: 35 us -> 5.02 us
  blocking collectives: 30.2 us -> 13.1 us
  starting transfers between devices: 0.21 us -> 14 us
  matrix products: 35.7 us -> 29.7 us
    all_gather x4 -> x1, waiting for transfers between devices: 160 us -> 28.2 us  [local(): piece = lax.all_gather(both, 'mp', axis=2, tiled=True)]
    unnamed x1 -> x0, blocking collectives: 17.1 us -> none
    all_gather x1 -> x0, local copies, waits for them, and re-layouts: 14.6 us -> none  [local(): lax.all_gather(hidden, 'dp', axis=1, tiled=True)]
    all_to_all x0 -> x2, starting transfers between devices: none -> 13.9 us  [the longest x1 6.94 us: local(): got = lax.all_to_all(sent, 'dp', 0, 0, tiled=True)]
    all_to_all x0 -> x2, waiting for transfers between devices: none -> 11 us  [the longest x1 11 us: local(): got = lax.all_to_all(sent, 'dp', 0, 0, tiled=True)]
    gather x2 -> x0, local copies, waits for them, and re-layouts: 10.2 us -> none  [the longest x1 5.1 us: local(): mine_hidden = jnp.take(all_hidden, wanted, axis=1)]
    dot_general x6 -> x7, matrix products: 22.5 us -> 16.3 us  [the longest x1 8.59 us: local(): jnp.einsum('tsd,dc->tsc', piece, talker_proj, preferred_element_type=jnp....]
    scatter x1 -> x0, local copies, waits for them, and re-layouts: 5.43 us -> none  [local(): inverse = jnp.zeros((total_rows,), jnp.int32).at[all_rows[0]].set(jnp.ara...]
  transfers between devices with their start and end apart: 5 -> 4, of which waited for: 5 -> 3; matrix products, arithmetic and copies ran while one was open for 7% -> 8% of each run, Pallas kernels for 0% -> 0%
where the time goes in v1:
time: 164 us
  waiting for transfers between devices  81.6 us (50%)
  matrix products  29.7 us (18%)
  between operations  14.2 us (9%)
  starting transfers between devices  14 us (9%)
  blocking collectives  13.1 us (8%)
  other arithmetic  6.27 us (4%)
  local copies, waits for them, and re-layouts  5.02 us (3%)
    reduce_scatter x1, waiting for transfers between devices, local(): lax.psum_scatter(head_partial.astype(jnp.bfloat16), 'mp', scatter_dimensi...  42.5 us
    all_gather x1, waiting for transfers between devices, local(): piece = lax.all_gather(both, 'mp', axis=2, tiled=True)  28.2 us
    dot_general x1, matrix products, local(): jnp.dot(context, out_weight, preferred_element_type=jnp.float32)  13.5 us
    psum x1, blocking collectives, local(): squares = lax.psum(jnp.sum(mixed * mixed, -1), 'mp')  13.1 us
    all_to_all x1, waiting for transfers between devices, local(): got = lax.all_to_all(sent, 'dp', 0, 0, tiled=True)  11 us
    dot_general x1, matrix products, local(): jnp.einsum('tsd,dc->tsc', piece, talker_proj, preferred_element_type=jnp....  8.59 us
    all_to_all x1, starting transfers between devices, local(): got = lax.all_to_all(sent, 'dp', 0, 0, tiled=True)  6.94 us
    all_to_all x1, starting transfers between devices, local(): lax.all_to_all(sent_place, 'dp', 0, 0, tiled=True).reshape(n_dp * CAP)  6.93 us
  transfers between devices with their start and end apart: 4, of which 3 were waited for; matrix products, arithmetic and copies ran while one was open for 8% of the time, Pallas kernels for 0%

profile of v1, /device:TPU:0, one launch (start us, length us, event | category | flops | bytes accessed | tf_op | source)
XLA Modules:
  0.0 163.9 jit_solution(8666752455453600768)
XLA Ops:
  7.2 0.0 copy-start
  7.2 0.0 reduce-scatter.2.cloned.1.call-start
  7.2 0.9 iota_compare_fusion.3
  8.1 1.2 copy.48
  9.3 0.0 copy-done
  9.3 0.0 copy-start.4
  9.4 1.6 bitcast_reduce_fusion
  11.0 0.0 copy-done.4
  11.0 3.0 %fusion.49 = (f32[4,80,8]{2,0,1:T(4,128)S(1)}, f32[4,80,1,8,4]{3,4,0,1,2:T(4,128)S(1)}) fusion(bf16[4,80,128,1]{2,1,0,3:T(8,128)(2,1)S(1)} %bitcast.99, pred[4,4]{1,0:T(4,128)(4,1)S(1)} %iota_compare_fusion.4, bf16[4,80,8,128]{3,2,1,0:T(8,128)(2,1)S(1)} %bitcast.97), kind=kOutput, calls=%fused_computation.62 | convolution fusion | flops 2649600 | bytes 788496 | tf_op jit(solution)/shard_map/tskgd,uskd->tskgu/dot_general | solution.py:26
  14.1 0.0 copy-start.3
  14.1 0.9 fusion.24
  15.0 0.6 fusion.32
  15.7 0.2 copy-done.3
  15.8 0.0 copy-start.5
  15.8 1.1 fusion.7
  16.9 0.0 copy-done.5
  16.9 0.6 fusion.23
  17.5 1.0 dot_general.30
  18.5 13.5 %fusion.2 = bf16[4,80,8192]{2,1,0:T(8,128)(2,1)} fusion(bf16[1024,8192]{1,0:T(8,128)(2,1)} %param.21, bf16[4,80,1024]{2,0,1:T(4,128)(2,1)} %dot_general.30), kind=kOutput, calls=%fused_computation.2 | convolution fusion | flops 5371330560 | bytes 22675456 | tf_op jit(solution)/shard_map/dot_general | solution.py:73
  32.0 0.0 copy-start.1
  32.0 0.0 reduce-scatter.2.cloned.1.call-update
  32.0 0.0 copy-start.6
  32.0 0.0 copy-start.2
  32.0 0.0 all-gather.2.cloned.1.call-start
  32.1 42.5 %reduce-scatter.2.cloned.1.call-done = bf16[4,80,1024]{2,1,0:T(8,128)(2,1)} async-done(((bf16[4,80,8192]{2,1,0:T(8,128)(2,1)}), bf16[4,80,1024]{2,1,0:T(8,128)(2,1)}) %reduce-scatter.2.cloned.1.call-update) | async-done | bytes 655376 | tf_op jit(solution)/shard_map/reduce_scatter | solution.py:76
  74.5 0.0 copy-done.1
  74.5 2.8 %fusion.48 = (bf16[4,80,1024]{2,1,0:T(8,128)(2,1)}, bf16[4,80,1024]{2,1,0:T(8,128)(2,1)}) fusion(bf16[4,80,1024]{2,1,0:T(8,128)(2,1)S(1)} %copy-done.1, bf16[4,80,1024]{2,1,0:T(8,128)(2,1)} %reduce-scatter.2.cloned.1.call-done, bf16[4,80,1024]{2,1,0:T(8,128)(2,1)} %param.19), kind=kLoop, calls=%fused_computation.61 | loop fusion | flops 1638400 | bytes 3276800 | tf_op jit(solution)/shard_map/add | solution.py:80
  77.3 0.0 all-gather.2.cloned.1.call-update
  77.3 0.0 copy-done.6
  77.3 0.2 convert_reduce_fusion
  77.5 0.1 select_reduce_fusion
  77.7 0.7 sub.34
  78.4 6.9 %all-to-all-start.1 = ((s32[16,1,10]{2,1,0:T(1,128)}), s32[16,1,10]{2,1,0:T(1,128)S(1)}, u32[]{:S(2)}, u32[]{:S(2)}) async-start(s32[16,1,10]{2,1,0:T(1,128)} %bitcast.20), calls=%async_computation.2 | async-start | bytes 16384 | tf_op jit(solution)/shard_map/all_to_all | solution.py:70
  85.3 0.0 copy-done.2
  85.3 28.2 %all-gather.2.cloned.1.call-done = bf16[4,80,8192]{2,1,0:T(8,128)(2,1)} async-done(((bf16[4,80,1024]{2,1,0:T(8,128)(2,1)}), bf16[4,80,8192]{2,1,0:T(8,128)(2,1)}) %all-gather.2.cloned.1.call-update) | async-done | bytes 5242896 | tf_op jit(solution)/shard_map/all_gather | solution.py:81
  113.5 8.6 %multiply_reduce_fusion = (f32[4,80]{1,0:T(4,128)S(1)}, f32[4,80,448]{2,1,0:T(8,128)S(1)}) fusion(bf16[4,80,8192]{2,1,0:T(8,128)(2,1)} %all-gather.2.cloned.1.call-done, bf16[8192,448]{0,1:T(8,128)(2,1)} %param.22), kind=kOutput, calls=%fused_computation.29 | convolution fusion | flops 2349096704 | bytes 13157632 | tf_op jit(solution)/shard_map/tsd,dc->tsc/dot_general | solution.py:82
  122.1 13.1 %psum.7 = f32[4,80]{1,0:T(4,128)S(1)} all-reduce(f32[4,80]{1,0:T(4,128)S(1)} %get-tuple-element.10), channel_id=1, replica_groups=mesh['dp'=16,'mp'=8] {'mp'}, use_global_device_ids=true, to_apply=%region_7.8 | all-reduce | flops 320 | bytes 2560 | tf_op jit(solution)/shard_map/psum | solution.py:84
  135.2 0.4 fusion.33
  135.6 1.3 copy.37
  136.9 0.0 all-to-all-done.1
  136.9 6.9 %all-to-all-start = ((bf16[160,4,448]{2,1,0:T(4,128)(2,1)}), bf16[160,4,448]{2,1,0:T(4,128)(2,1)S(1)}, u32[]{:S(2)}, u32[]{:S(2)}) async-start(bf16[160,4,448]{2,1,0:T(4,128)(2,1)} %copy.37), calls=%async_computation.1 | async-start | bytes 1310720 | tf_op jit(solution)/shard_map/all_to_all | solution.py:92
  143.9 0.5 broadcast.63
  144.4 0.7 reduce.7
  145.1 0.1 eq.49
  145.2 11.0 %all-to-all-done = bf16[160,4,448]{2,1,0:T(4,128)(2,1)S(1)} async-done(((bf16[160,4,448]{2,1,0:T(4,128)(2,1)}), bf16[160,4,448]{2,1,0:T(4,128)(2,1)S(1)}, u32[]{:S(2)}, u32[]{:S(2)}) %all-to-all-start) | async-done | bytes 573472 | tf_op jit(solution)/shard_map/all_to_all | solution.py:92
  156.1 1.0 convolution_bitcast_fusion
  (8 shorter events, 0.1 us)
Async XLA Ops:
  7.2 2.2 %copy-start = (bf16[80,1,128,128]{3,2,1,0:T(8,128)(2,1)S(1)}, bf16[80,1,128,128]{3,2,1,0:T(8,128)(2,1)}, u32[]{:S(2)}) copy-start(bf16[80,1,128,128]{3,2,1,0:T(8,128)(2,1)} %param.15) | copy-start | bytes 7864324
  7.2 67.3 %reduce-scatter.2.cloned.1.call-start = ((), (), s32[]{:S(2)}) async-start(), calls=%async_computation.3 | async-start | bytes 5898240 | tf_op jit(solution)/shard_map/reduce_scatter | solution.py:76
  9.3 1.6 %copy-start.4 = (bf16[4,80,128]{2,1,0:T(8,128)(2,1)S(1)}, bf16[4,80,128]{2,1,0:T(8,128)(2,1)}, u32[]{:S(2)}) copy-start(bf16[4,80,128]{2,1,0:T(8,128)(2,1)} %param.13) | copy-start | bytes 245764
  14.1 1.7 %copy-start.3 = (bf16[80,1,128,128]{3,2,1,0:T(8,128)(2,1)S(1)}, bf16[80,1,128,128]{3,2,1,0:T(8,128)(2,1)}, u32[]{:S(2)}) copy-start(bf16[80,1,128,128]{3,2,1,0:T(8,128)(2,1)} %param.16) | copy-start | bytes 7864324
  15.8 1.1 copy-start.5
  32.0 42.6 %copy-start.1 = (bf16[4,80,1024]{2,1,0:T(8,128)(2,1)S(1)}, bf16[4,80,1024]{2,1,0:T(8,128)(2,1)}, u32[]{:S(2)}) copy-start(bf16[4,80,1024]{2,1,0:T(8,128)(2,1)} %param.20) | copy-start | bytes 1966084
  32.0 45.3 %copy-start.6 = (s32[80]{0:T(128)S(1)}, s32[80]{0:T(128)}, u32[]{:S(2)}) copy-start(s32[80]{0:T(128)} %param.18) | copy-start | bytes 964
  32.0 53.3 %copy-start.2 = (bf16[448]{0:T(512)(128)(2,1)S(1)}, bf16[448]{0:T(512)(128)(2,1)}, u32[]{:S(2)}) copy-start(bf16[448]{0:T(512)(128)(2,1)} %param.23) | copy-start | bytes 2692
  32.0 81.5 %all-gather.2.cloned.1.call-start = ((), (), s32[]{:S(2)}) async-start(), calls=%async_computation.4 | async-start | bytes 5898240 | tf_op jit(solution)/shard_map/all_gather | solution.py:81
  78.4 58.6 %all-to-all-start.1 = ((s32[16,1,10]{2,1,0:T(1,128)}), s32[16,1,10]{2,1,0:T(1,128)S(1)}, u32[]{:S(2)}, u32[]{:S(2)}) async-start(s32[16,1,10]{2,1,0:T(1,128)} %bitcast.20), calls=%async_computation.2 | async-start | bytes 16384 | tf_op jit(solution)/shard_map/all_to_all | solution.py:70
  136.9 19.2 %all-to-all-start = ((bf16[160,4,448]{2,1,0:T(4,128)(2,1)}), bf16[160,4,448]{2,1,0:T(4,128)(2,1)S(1)}, u32[]{:S(2)}, u32[]{:S(2)}) async-start(bf16[160,4,448]{2,1,0:T(4,128)(2,1)} %copy.37), calls=%async_computation.1 | async-start | bytes 1310720 | tf_op jit(solution)/shard_map/all_to_all | solution.py:92
Sparse Core Ops, SparseCore 0:
  32.1 42.3 reduce-scatter.1
  77.4 35.9 all-gather.1

commit v2 on v1

v2 whole, which is shorter than its diff:
```python
import jax
import jax.numpy as jnp
from jax import lax
from jax.experimental import pallas as pl
from jax.experimental.pallas import tpu as pltpu
from jax.sharding import PartitionSpec as P

epsilon = 1e-06
CAP = 10


def attend_and_project(query, token_keys, token_values, cache_keys, stored_values, lengths, out_weight, blocks):
    step_count, row_count, query_cols = query.shape
    head_dim = cache_keys.shape[-1]
    slot_count = cache_keys.shape[-2]
    groups = query_cols // head_dim
    streams = 16
    each = step_count * groups
    fresh = step_count * streams
    padded = max(fresh, slot_count)
    chunks = row_count // streams
    rows = step_count * row_count
    count = blocks.shape[0]
    cols = query_cols
    scale = 1.0 / head_dim**0.5

    def body(blocks_ref, len_ref, q_ref, tk_ref, tv_ref, k_ref, v_ref, w_ref, ctx_ref, *rest):
        out_refs, (w_buf, sems) = rest[:count], rest[count:]
        chunk = pl.program_id(0)

        def load(k):
            at = pl.ds(pl.multiple_of(blocks_ref[k] * cols, cols), cols)
            return pltpu.make_async_copy(w_ref.at[:, at], w_buf.at[k], sems.at[k])

        @pl.when(chunk == 0)
        def _():
            for k in range(count):
                load(k).start()

        q = q_ref[...].reshape(step_count, streams, groups, head_dim)
        q = jnp.swapaxes(q, 0, 1).reshape(streams, each, head_dim)
        scores = (
            lax.dot_general(
                q, k_ref[...], (((2,), (2,)), ((0,), (0,))), preferred_element_type=jnp.float32
            )
            * scale
        )
        slot = lax.broadcasted_iota(jnp.int32, (1, 1, slot_count), 2)
        filled = jnp.concatenate(
            [slot < len_ref[chunk * streams + b] for b in range(streams)]
        )
        scores = jnp.where(filled, scores, -1e30)
        q = q.reshape(streams * each, head_dim)
        copies = padded // fresh
        keys = jnp.concatenate([tk_ref[...].reshape(fresh, head_dim)] * copies)
        values = jnp.concatenate([tv_ref[...].reshape(fresh, head_dim)] * copies)
        recent = (
            lax.dot_general(
                q,
                keys,
                (((1,), (1,)), ((), ())),
                preferred_element_type=jnp.float32,
            )
            * scale
        )
        row = lax.broadcasted_iota(jnp.int32, (streams * each, padded), 0)
        col = lax.broadcasted_iota(jnp.int32, (streams * each, padded), 1)
        mine = (row // each == col % streams) & (col // streams <= row // groups % step_count)
        recent = jnp.where(mine, recent, -1e30).reshape(streams, each, padded)
        highest = jnp.max(jnp.maximum(scores, recent), -1, keepdims=True)
        scores, recent = jnp.exp(scores - highest), jnp.exp(recent - highest)
        total = jnp.sum(scores + recent, -1, keepdims=True)
        share = 1.0 / total
        weights = (scores * share).astype(jnp.bfloat16)
        recent = (recent * share).astype(jnp.bfloat16).reshape(streams * each, padded)
        context = lax.dot_general(
            weights, v_ref[...], (((2,), (1,)), ((0,), (0,))), preferred_element_type=jnp.float32
        ).reshape(streams * each, head_dim)
        context += jnp.dot(
            recent, values, preferred_element_type=jnp.float32
        )
        context = jnp.swapaxes(context.reshape(streams, step_count, groups, head_dim), 0, 1)
        context = context.reshape(step_count, streams, cols).astype(jnp.bfloat16)
        for t in range(step_count):
            at = pl.ds(pl.multiple_of(t * row_count + chunk * streams, streams), streams)
            ctx_ref[at, :] = context[t]

        @pl.when(chunk == chunks - 1)
        def _():
            for k in range(count):
                load(k).wait()
                out_refs[k][...] = jnp.dot(
                    ctx_ref[...], w_buf[k], preferred_element_type=jnp.float32
                ).astype(jnp.bfloat16)

    def by_stream(*shape):
        return pl.BlockSpec(shape, lambda i, *_: (i,) + (0,) * (len(shape) - 1))

    def by_step(width):
        return pl.BlockSpec((step_count, streams, width), lambda i, *_: (0, i, 0))

    whole = pl.BlockSpec((rows, cols), lambda i, *_: (0, 0))
    return pl.pallas_call(
        body,
        grid_spec=pltpu.PrefetchScalarGridSpec(
            num_scalar_prefetch=2,
            grid=(chunks,),
            in_specs=[
                by_step(query_cols),
                by_step(head_dim),
                by_step(head_dim),
                by_stream(streams, slot_count, head_dim),
                by_stream(streams, slot_count, head_dim),
                pl.BlockSpec(memory_space=pltpu.HBM),
            ],
            out_specs=[whole] * (1 + count),
            scratch_shapes=[
                pltpu.VMEM((count, out_weight.shape[0], cols), jnp.bfloat16),
                pltpu.SemaphoreType.DMA((count,)),
            ],
        ),
        out_shape=[jax.ShapeDtypeStruct((rows, cols), jnp.bfloat16)] * (1 + count),
        compiler_params=pltpu.CompilerParams(vmem_limit_bytes=60 << 20),
        cost_estimate=pl.CostEstimate(
            flops=2 * count * rows * cols * cols,
            bytes_accessed=32 << 20,
            transcendentals=0,
        ),
    )(
        blocks,
        lengths,
        query,
        token_keys,
        token_values,
        cache_keys.reshape(row_count, slot_count, head_dim),
        stored_values.reshape(row_count, slot_count, head_dim),
        out_weight,
    )


def head_product(context, out_weight, blocks):
    rows, depth = context.shape
    count = blocks.shape[0]
    cols = out_weight.shape[1] // lax.axis_size("mp")

    def body(blocks_ref, context_ref, w_ref, *rest):
        out_refs, (w_buf, sems) = rest[:count], rest[count:]
        loads = []
        for k in range(count):
            at = pl.ds(pl.multiple_of(blocks_ref[k] * cols, cols), cols)
            loads.append(pltpu.make_async_copy(w_ref.at[:, at], w_buf.at[k], sems.at[k]))
            loads[k].start()
        for k in range(count):
            loads[k].wait()
            out_refs[k][...] = jnp.dot(
                context_ref[...], w_buf[k], preferred_element_type=jnp.float32
            ).astype(jnp.bfloat16)

    return pl.pallas_call(
        body,
        in_specs=[
            pl.BlockSpec(memory_space=pltpu.SMEM),
            pl.BlockSpec(memory_space=pltpu.VMEM),
            pl.BlockSpec(memory_space=pltpu.HBM),
        ],
        out_specs=[pl.BlockSpec(memory_space=pltpu.VMEM)] * count,
        out_shape=[jax.ShapeDtypeStruct((rows, cols), jnp.bfloat16)] * count,
        scratch_shapes=[
            pltpu.VMEM((count, depth, cols), jnp.bfloat16),
            pltpu.SemaphoreType.DMA((count,)),
        ],
        compiler_params=pltpu.CompilerParams(vmem_limit_bytes=50 << 20),
        cost_estimate=pl.CostEstimate(
            flops=2 * count * rows * depth * cols,
            bytes_accessed=2 * count * (depth + rows) * cols,
            transcendentals=0,
        ),
    )(blocks, context, out_weight)


def talker_product(total, pieces, proj_columns, blocks):
    depth = pieces[0][0].shape[1]
    rows = sum(part.shape[0] for part in pieces[0])
    sizes = [len(piece) for piece in pieces]
    count = len(pieces)
    cols = proj_columns.shape[0]
    first = [] if total is None else [total]
    parts = [part for piece in pieces for part in piece]

    def body(blocks_ref, w_ref, *refs):
        part_refs, refs = list(refs[: len(parts)]), refs[len(parts) :]
        out_ref, w_buf, sems = refs[len(first) :]
        loads = []
        for k in range(count):
            at = pl.ds(pl.multiple_of(blocks_ref[k] * depth, depth), depth)
            loads.append(pltpu.make_async_copy(w_ref.at[:, at], w_buf.at[k], sems.at[k]))
            loads[k].start()
        for k in range(count):
            piece = jnp.concatenate([part_refs.pop(0)[...] for _ in range(sizes[k])])
            loads[k].wait()
            product = lax.dot_general(
                piece,
                w_buf[k],
                (((1,), (1,)), ((), ())),
                preferred_element_type=jnp.float32,
            )
            if k > 0:
                out_ref[...] += product
            elif total is None:
                out_ref[...] = product
            else:
                out_ref[...] = refs[0][...] + product

    vmem = pl.BlockSpec(memory_space=pltpu.VMEM)
    return pl.pallas_call(
        body,
        in_specs=[
            pl.BlockSpec(memory_space=pltpu.SMEM),
            pl.BlockSpec(memory_space=pltpu.HBM),
        ]
        + [vmem] * len(parts + first),
        out_specs=vmem,
        out_shape=jax.ShapeDtypeStruct((rows, cols), jnp.float32),
        scratch_shapes=[
            pltpu.VMEM((count, cols, depth), jnp.bfloat16),
            pltpu.SemaphoreType.DMA((count,)),
        ],
        compiler_params=pltpu.CompilerParams(vmem_limit_bytes=20 << 20),
        cost_estimate=pl.CostEstimate(
            flops=2 * count * rows * depth * cols,
            bytes_accessed=2 * count * (depth * cols + rows * depth),
            transcendentals=0,
        ),
    )(blocks, proj_columns, *parts, *first)


def shift_y(x, by):
    count = lax.axis_size("mp")
    return lax.ppermute(x, "mp", [(i, (i + 2 * by) % count) for i in range(count)])


def swap(x):
    return lax.ppermute(x, "mp", [(i, i ^ 1) for i in range(lax.axis_size("mp"))])


def after(x, y):
    return lax.optimization_barrier((x, y))[0]


def wide(x):
    return x.astype(jnp.float32)


def narrow(x):
    return x.astype(jnp.bfloat16)


def local(
    query,
    token_keys,
    token_values,
    cache_keys,
    stored_values,
    lengths,
    talker_row,
    residual,
    embedding,
    out_weight,
    talker_proj,
    talker_gain,
):
    step_count, row_count, query_cols = query.shape
    rows = step_count * row_count
    half = rows // 2
    top, low = slice(0, half), slice(half, rows)
    n_dp = lax.axis_size("dp")
    n_mp = lax.axis_size("mp")
    mp = lax.axis_index("mp")
    y, core = mp // 2, mp % 2
    talk_cols = talker_proj.shape[1]

    def blocks(shifts):
        ids = []
        for by in shifts:
            at = (2 * y + 2 * by) % n_mp
            ids += [at + 1 - core, at + core]
        return jnp.stack(ids).astype(jnp.int32)

    context, far_away, far_here, up_away, up_here = attend_and_project(
        query, token_keys, token_values, cache_keys, stored_values, lengths, out_weight, blocks([2, 1])
    )
    far_got, up_got = swap(far_away), swap(up_away)
    down_away, down_here = head_product(context, out_weight, blocks([-1]))
    far_got, context = lax.optimization_barrier((far_got, after(context, down_here)))
    down_got = swap(down_away)
    up_far = shift_y(narrow(wide(far_here[top]) + wide(far_got[top])), 1)
    down_far = shift_y(narrow(wide(far_here[low]) + wide(far_got[low])), -1)
    below_low = shift_y(narrow(wide(up_here[low]) + wide(up_got[low])), 1)
    down_got, context = lax.optimization_barrier((down_got, context))
    above_top = shift_y(narrow(wide(down_here[top]) + wide(down_got[top])), -1)
    own_away, own_here = head_product(context, out_weight, blocks([0]))
    own_got = swap(own_away)
    below_top = shift_y(narrow(wide(up_here[top]) + wide(up_got[top]) + wide(up_far)), 1)
    above_low = shift_y(narrow(wide(down_here[low]) + wide(down_got[low]) + wide(down_far)), -1)
    residual = residual.reshape(rows, -1)
    embedding = embedding.reshape(rows, -1)

    def finish(part, below, above):
        base = wide(residual[part]) + wide(own_here[part]) + wide(own_got[part])
        return narrow(base + wide(below) + wide(above))

    hidden_top = finish(top, below_top, above_top)
    hidden_low = finish(low, below_low, above_low)
    both_top = hidden_top + embedding[top]
    both_low = hidden_low + embedding[low]

    proj_columns = talker_proj.T
    own = [both_top, both_low]
    own_got = [swap(both_top), swap(both_low)]
    below_top, above_low = shift_y(both_top, 1), shift_y(both_low, -1)
    mixed = talker_product(None, [own_got, own], proj_columns, blocks([0]))
    both_top, both_low, mixed = lax.optimization_barrier((both_top, both_low, mixed))
    below_low, above_top = shift_y(both_low, 1), shift_y(both_top, -1)
    beyond_top, beyond_low = shift_y(below_top, 1), shift_y(above_low, -1)
    below, above = [below_top, below_low], [above_top, above_low]
    below_got = [swap(below_top), swap(below_low)]
    above_got = [swap(above_top), swap(above_low)]
    mixed = talker_product(
        mixed, [below_got, below, above_got, above], proj_columns, blocks([-1, 1])
    )
    beyond_top, beyond_low, mixed = lax.optimization_barrier((beyond_top, beyond_low, mixed))
    beyond = [beyond_top, beyond_low]
    beyond_got = [swap(beyond_top), swap(beyond_low)]
    mixed = talker_product(mixed, [beyond_got, beyond], proj_columns, blocks([2]))

    squares = jnp.sum(mixed * mixed, -1)
    squares = squares + swap(squares)
    squares = squares + shift_y(squares, 1) + shift_y(squares, -1) + shift_y(squares, 2)
    normed = (
        mixed
        * lax.rsqrt(squares / (talk_cols * n_mp) + epsilon)[:, None]
        * wide(talker_gain)
    ).astype(jnp.bfloat16)

    shard = talker_row // row_count
    place = talker_row % row_count
    same = shard[None, :] == shard[:, None]
    earlier = jnp.arange(row_count)[None, :] < jnp.arange(row_count)[:, None]
    order = jnp.sum((same & earlier).astype(jnp.int32), 1)
    step = jnp.arange(step_count, dtype=jnp.int32)[:, None]
    slot = ((shard * step_count + step) * CAP + order).reshape(rows)
    slots = n_dp * step_count * CAP
    pick = slot[None, :] == jnp.arange(slots, dtype=jnp.int32)[:, None]
    spare = -talk_cols % 128
    place_cols = jnp.broadcast_to(
        jnp.tile(narrow(place + 1), step_count)[:, None], (rows, spare)
    )
    sent = jnp.dot(narrow(pick), jnp.concatenate([normed, place_cols], 1))
    got = lax.all_to_all(
        sent.reshape(n_dp, slots // n_dp, -1), "dp", 0, 0, tiled=True
    ).reshape(slots, -1)
    got_place = got[:, talk_cols].astype(jnp.int32) - 1
    got_step = jnp.arange(slots, dtype=jnp.int32) // CAP % step_count
    got_row = jnp.where(got_place < 0, rows, got_step * row_count + got_place)
    put = got_row[None, :] == jnp.arange(rows, dtype=jnp.int32)[:, None]
    talker_input = jnp.dot(narrow(put), got[:, :talk_cols])
    hidden = jnp.concatenate([hidden_top, hidden_low])
    return (
        hidden.reshape(step_count, row_count, -1),
        talker_input.reshape(step_count, row_count, -1),
    )


def solution(mesh):
    placed = (
        P(None, "dp", "mp"),
        P(None, "dp", "mp"),
        P(None, "dp", "mp"),
        P("dp", "mp", None, None),
        P("dp", "mp", None, None),
        P("dp"),
        P("dp"),
        P(None, "dp", "mp"),
        P(None, "dp", "mp"),
        P("mp", None),
        P(None, "mp"),
        P("mp"),
    )
    return jax.shard_map(
        local,
        mesh=mesh,
        in_specs=placed,
        out_specs=(P(None, "dp", "mp"), P(None, "dp", "mp")),
        check_vma=False,
    )
```

time: 164 us -> 129 us (0.79)
  waiting for transfers between devices: 81.6 us -> 45.1 us
  Pallas kernels: 0 us -> 30.4 us
  matrix products: 29.7 us -> 2.56 us
  starting transfers between devices: 14 us -> 34 us
  between operations: 14.2 us -> 0.96 us
  blocking collectives: 13.1 us -> 0 us
  other arithmetic: 6.27 us -> 10.3 us
    reduce_scatter x1 -> x0, waiting for transfers between devices: 42.5 us -> none  [local(): lax.psum_scatter(head_partial.astype(jnp.bfloat16), 'mp', scatter_dimensi...]
    ppermute x0 -> x28, waiting for transfers between devices: none -> 34.4 us  [the longest x15 32.1 us: shift_y(): lax.ppermute(x, 'mp', [(i, (i + 2 * by) % count) for i in range(count)])]
    pallas_call x0 -> x6, Pallas kernels: none -> 30.4 us  [the longest x1 15.4 us: attend_and_project(): pl.pallas_call(body, grid_spec=pltpu.PrefetchScalarGridSpec(num_scalar_pr...]
    all_gather x1 -> x0, waiting for transfers between devices: 28.2 us -> none  [local(): piece = lax.all_gather(both, 'mp', axis=2, tiled=True)]
    dot_general x8 -> x2, matrix products: 29.7 us -> 2.56 us  [the longest x1 1.41 us: local(): sent = jnp.dot(narrow(pick), jnp.concatenate([normed, place_cols], 1))]
    ppermute x0 -> x28, starting transfers between devices: none -> 26.3 us  [the longest x15 23.4 us: shift_y(): lax.ppermute(x, 'mp', [(i, (i + 2 * by) % count) for i in range(count)])]
    psum x1 -> x0, blocking collectives: 13.1 us -> none  [local(): squares = lax.psum(jnp.sum(mixed * mixed, -1), 'mp')]
    convert_element_type x1 -> x5, other arithmetic: 0.01 us -> 6.23 us  [the longest x3 5.02 us: narrow(): return x.astype(jnp.bfloat16)]
  transfers between devices with their start and end apart: 4 -> 29, of which waited for: 3 -> 13; matrix products, arithmetic and copies ran while one was open for 8% -> 5% of each run, Pallas kernels for 0% -> 10%
where the time goes in v2:
time: 129 us; the launch traced here: 128 us
  waiting for transfers between devices  45.1 us (35%)
  starting transfers between devices  34 us (26%)
  Pallas kernels  30.4 us (24%)
  other arithmetic  10.3 us (8%)
  local copies, waits for them, and re-layouts  5.14 us (4%)
  matrix products  2.56 us (2%)
    ppermute x15, waiting for transfers between devices, shift_y(): lax.ppermute(x, 'mp', [(i, (i + 2 * by) % count) for i in range(count)])  32.1 us
    ppermute x15, starting transfers between devices, shift_y(): lax.ppermute(x, 'mp', [(i, (i + 2 * by) % count) for i in range(count)])  23.4 us
    pallas_call x1, Pallas kernels, attend_and_project(): pl.pallas_call(body, grid_spec=pltpu.PrefetchScalarGridSpec(num_scalar_pr...  15.4 us
    all_to_all x1, waiting for transfers between devices, local(): lax.all_to_all(sent.reshape(n_dp, slots // n_dp, -1), 'dp', 0, 0, tiled=T...  10.6 us
    pallas_call x2, Pallas kernels, head_product(): pl.pallas_call(body, in_specs=[pl.BlockSpec(memory_space=pltpu.SMEM), pl....  8.06 us
    all_to_all x1, starting transfers between devices, local(): lax.all_to_all(sent.reshape(n_dp, slots // n_dp, -1), 'dp', 0, 0, tiled=T...  7.78 us
    pallas_call x3, Pallas kernels, talker_product(): pl.pallas_call(body, in_specs=[pl.BlockSpec(memory_space=pltpu.SMEM), pl....  6.97 us
    convert_element_type x3, other arithmetic, narrow(): return x.astype(jnp.bfloat16)  5.02 us
  transfers between devices with their start and end apart: 29, of which 13 were waited for; matrix products, arithmetic and copies ran while one was open for 5% of the time, Pallas kernels for 10%

profile of v2, /device:TPU:0, one launch (start us, length us, event | category | flops | bytes accessed | tf_op | source)
XLA Modules:
  0.0 128.4 jit_solution(10167266856377072091)
XLA Ops:
  0.7 0.6 add_add_fusion.blocks_ref
  1.3 15.4 %shard_map.131 = (bf16[320,1024]{1,0:T(8,128)(2,1)}, bf16[320,1024]{1,0:T(8,128)(2,1)}, bf16[320,1024]{1,0:T(8,128)(2,1)}, bf16[320,1024]{1,0:T(8,128)(2,1)}, bf16[320,1024]{1,0:T(8,128)(2,1)}) custom-call(s32[4]{0:T(128)} %add_add_fusion.blocks_ref, s32[80]{0:T(128)} %len_ref.1, bf16[4,80,1024]{2,1,0:T(8,128)(2,1)} %q_ref.1, bf16[4,80,128]{2,1,0:T(8,128)(2,1)} %tk_ref.1, ...), custom_call_target="tpu_custom_call" | custom-call | flops 2684354560 | bytes 33554432 | tf_op jit(solution)/shard_map/pallas_call | solution.py:103
  16.6 0.1 collective-permute-start.1
  16.8 1.1 copy-done.1
  17.9 4.2 %shard_map.132 = (bf16[320,1024]{1,0:T(8,128)(2,1)}, bf16[320,1024]{1,0:T(8,128)(2,1)S(1)}) custom-call(s32[2]{0:T(128)S(1)} %pad_add_fusion.1.blocks_ref, bf16[320,1024]{1,0:T(8,128)(2,1)S(1)} %copy-done.1, bf16[1024,8192]{1,0:T(8,128)(2,1)} %w_ref.5), custom_call_target="tpu_custom_call" | custom-call | flops 1342177280 | bytes 5505024 | tf_op jit(solution)/shard_map/pallas_call | solution.py:159
  22.2 0.8 copy-done.3
  23.0 0.5 collective-permute-start
  23.5 0.9 copy-done.10
  24.4 2.3 %add_convert_fusion.5 = (bf16[160,1024]{1,0:T(8,128)(2,1)}, bf16[160,1024]{1,0:T(8,128)(2,1)}) fusion(bf16[320,1024]{1,0:T(8,128)(2,1)} %copy-done.10, bf16[320,1024]{1,0:T(8,128)(2,1)S(1)} %copy-done.9), kind=kLoop, calls=%fused_computation.23 | loop fusion | flops 1310720 | bytes 1966080 | tf_op jit(solution)/shard_map/convert_element_type | solution.py:255
  26.7 1.7 %collective-permute-start.4 = (bf16[160,1024]{1,0:T(8,128)(2,1)}, bf16[160,1024]{1,0:T(8,128)(2,1)S(1)}, u32[]{:S(2)}, u32[]{:S(2)}) collective-permute-start(bf16[160,1024]{1,0:T(8,128)(2,1)} %get-tuple-element.52), channel_id=1, source_target_pairs={{0,2},{1,3},{2,4},{3,5},{4,6},{5,7},{6,0},{7,1},{8,10},{9,11},{10,... | collective-permute-start | bytes 983048 | tf_op jit(solution)/shard_map/ppermute | solution.py:239
  28.4 1.6 %collective-permute-start.8 = (bf16[160,1024]{1,0:T(8,128)(2,1)}, bf16[160,1024]{1,0:T(8,128)(2,1)S(1)}, u32[]{:S(2)}, u32[]{:S(2)}) collective-permute-start(bf16[160,1024]{1,0:T(8,128)(2,1)} %get-tuple-element.53), channel_id=1, source_target_pairs={{0,6},{1,7},{2,0},{3,1},{4,2},{5,3},{6,4},{7,5},{8,14},{9,15},{10,... | collective-permute-start | bytes 983048 | tf_op jit(solution)/shard_map/ppermute | solution.py:239
  30.0 1.1 copy-done.2
  31.1 3.8 %shard_map.133 = (bf16[320,1024]{1,0:T(8,128)(2,1)S(1)}, bf16[320,1024]{1,0:T(8,128)(2,1)S(1)}) custom-call(s32[2]{0:T(128)S(1)} %pad_add_fusion.blocks_ref, bf16[320,1024]{1,0:T(8,128)(2,1)S(1)} %copy-done.2, bf16[1024,8192]{1,0:T(8,128)(2,1)} %w_ref.5), custom_call_target="tpu_custom_call" | custom-call | flops 1342177280 | bytes 5505024 | tf_op jit(solution)/shard_map/pallas_call | solution.py:159
  35.0 0.1 collective-permute-start.2
  35.2 3.2 %collective-permute-done.4 = bf16[160,1024]{1,0:T(8,128)(2,1)S(1)} collective-permute-done((bf16[160,1024]{1,0:T(8,128)(2,1)}, bf16[160,1024]{1,0:T(8,128)(2,1)S(1)}, u32[]{:S(2)}, u32[]{:S(2)}) %collective-permute-start.4) | collective-permute-done | bytes 327712 | tf_op jit(solution)/shard_map/ppermute | solution.py:239
  38.4 1.4 %add_convert_fusion.4 = (bf16[160,1024]{1,0:T(8,128)(2,1)S(1)}, bf16[160,1024]{1,0:T(8,128)(2,1)S(1)}) fusion(bf16[160,1024]{1,0:T(8,128)(2,1)S(1)} %collective-permute-done.4, bf16[320,1024]{1,0:T(8,128)(2,1)} %collective-permute-done.3, bf16[320,1024]{1,0:T(8,128)(2,1)S(1)} %copy-done.8), kind=kLoop, calls=%fused_computation.22 | loop fusion | flops 1638400 | bytes 2293760 | tf_op jit(solution)/shard_map/convert_element_type | solution.py:255
  39.7 0.4 collective-permute-start.5
  40.1 1.6 %collective-permute-start.7 = (bf16[160,1024]{1,0:T(8,128)(2,1)S(1)}, bf16[160,1024]{1,0:T(8,128)(2,1)S(1)}, u32[]{:S(2)}, u32[]{:S(2)}) collective-permute-start(bf16[160,1024]{1,0:T(8,128)(2,1)S(1)} %get-tuple-element.51), channel_id=1, source_target_pairs={{0,2},{1,3},{2,4},{3,5},{4,6},{5,7},{6,0},{7,1},{8,10},{9,11},{10,... | collective-permute-start | bytes 983048 | tf_op jit(solution)/shard_map/ppermute | solution.py:239
  41.7 1.4 %add_convert_fusion.3 = (bf16[160,1024]{1,0:T(8,128)(2,1)S(1)}, bf16[160,1024]{1,0:T(8,128)(2,1)S(1)}) fusion(bf16[320,1024]{1,0:T(8,128)(2,1)} %collective-permute-done, bf16[320,1024]{1,0:T(8,128)(2,1)S(1)} %copy-done.4, bf16[160,1024]{1,0:T(8,128)(2,1)S(1)} %collective-permute-done.8), kind=kLoop, calls=%fused_computation.21 | loop fusion | flops 1638400 | bytes 2293760 | tf_op jit(solution)/shard_map/convert_element_type | solution.py:255
  43.0 1.7 %collective-permute-start.6 = (bf16[160,1024]{1,0:T(8,128)(2,1)S(1)}, bf16[160,1024]{1,0:T(8,128)(2,1)S(1)}, u32[]{:S(2)}, u32[]{:S(2)}) collective-permute-start(bf16[160,1024]{1,0:T(8,128)(2,1)S(1)} %get-tuple-element.54), channel_id=1, source_target_pairs={{0,6},{1,7},{2,0},{3,1},{4,2},{5,3},{6,4},{7,5},{8,14},{9,15},{10,... | collective-permute-start | bytes 983048 | tf_op jit(solution)/shard_map/ppermute | solution.py:239
  44.8 1.7 %collective-permute-start.9 = (bf16[160,1024]{1,0:T(8,128)(2,1)S(1)}, bf16[160,1024]{1,0:T(8,128)(2,1)S(1)}, u32[]{:S(2)}, u32[]{:S(2)}) collective-permute-start(bf16[160,1024]{1,0:T(8,128)(2,1)S(1)} %get-tuple-element.55), channel_id=1, source_target_pairs={{0,6},{1,7},{2,0},{3,1},{4,2},{5,3},{6,4},{7,5},{8,14},{9,15},{10,... | collective-permute-start | bytes 983048 | tf_op jit(solution)/shard_map/ppermute | solution.py:239
  46.5 0.1 fusion.29
  46.6 5.0 %collective-permute-done.5 = bf16[160,1024]{1,0:T(8,128)(2,1)S(1)} collective-permute-done((bf16[160,1024]{1,0:T(8,128)(2,1)S(1)}, bf16[160,1024]{1,0:T(8,128)(2,1)S(1)}, u32[]{:S(2)}, u32[]{:S(2)}) %collective-permute-start.5) | collective-permute-done | bytes 327712 | tf_op jit(solution)/shard_map/ppermute | solution.py:239
  51.6 5.9 %collective-permute-done.7 = bf16[160,1024]{1,0:T(8,128)(2,1)S(1)} collective-permute-done((bf16[160,1024]{1,0:T(8,128)(2,1)S(1)}, bf16[160,1024]{1,0:T(8,128)(2,1)S(1)}, u32[]{:S(2)}, u32[]{:S(2)}) %collective-permute-start.7) | collective-permute-done | bytes 327712 | tf_op jit(solution)/shard_map/ppermute | solution.py:239
  57.5 1.4 %collective-permute-done.9 = bf16[160,1024]{1,0:T(8,128)(2,1)S(1)} collective-permute-done((bf16[160,1024]{1,0:T(8,128)(2,1)S(1)}, bf16[160,1024]{1,0:T(8,128)(2,1)S(1)}, u32[]{:S(2)}, u32[]{:S(2)}) %collective-permute-start.9) | collective-permute-done | bytes 327712 | tf_op jit(solution)/shard_map/ppermute | solution.py:239
  58.9 1.7 %bitcast_add_fusion.1 = (bf16[160,1024]{1,0:T(8,128)(2,1)S(1)}, bf16[160,1024]{1,0:T(8,128)(2,1)S(1)}, bf16[160,1024]{1,0:T(8,128)(2,1)S(1)}, bf16[160,1024]{1,0:T(8,128)(2,1)}) fusion(bf16[2,80,1024]{2,1,0:T(8,128)(2,1)S(1)} %get-tuple-element.62, bf16[160,1024]{1,0:T(8,128)(2,1)S(1)} %collective-permute-done.6, ...), kind=kLoop, calls=%fused_computation.30 | loop fusion | flops 3604480 | bytes 5242880 | tf_op jit(solution)/shard_map/add | solution.py:314
  60.5 0.5 collective-permute-start.16
  61.1 1.3 collective-permute-start.10
  62.3 2.0 %collective-permute-start.12 = (bf16[160,1024]{1,0:T(8,128)(2,1)S(1)}, bf16[160,1024]{1,0:T(8,128)(2,1)S(1)}, u32[]{:S(2)}, u32[]{:S(2)}) collective-permute-start(bf16[160,1024]{1,0:T(8,128)(2,1)S(1)} %get-tuple-element.36.refs_3_), channel_id=1, source_target_pairs={{0,6},{1,7},{2,0},{3,1},{4,2},{5,3},{6,4},{7,5},{8,14},{9,15},{10,... | collective-permute-start | bytes 983048 | tf_op jit(solution)/shard_map/ppermute | solution.py:239
  64.3 1.9 %shard_map.134.refs_8_ = f32[320,448]{1,0:T(8,128)S(1)} custom-call(s32[2]{0:T(128)S(1)} %pad_add_fusion.blocks_ref, bf16[448,8192]{1,0:T(8,128)(2,1)S(1)} %bitcast.29, bf16[160,1024]{1,0:T(8,128)(2,1)S(1)} %collective-permute-done.15.refs_0_, bf16[160,1024]{1,0:T(8,128)(2,1)S(1)} %collective-permute-done.16.refs_1_, ...), custom_call_target="tpu_custom_call" | custom-call | flops 587202560 | bytes 3145728 | tf_op jit(solution)/shard_map/pallas_call | solution.py:215
  66.2 0.1 collective-permute-start.17
  66.4 3.2 %collective-permute-start.19 = (bf16[160,1024]{1,0:T(8,128)(2,1)S(1)}, bf16[160,1024]{1,0:T(8,128)(2,1)S(1)}, u32[]{:S(2)}, u32[]{:S(2)}) collective-permute-start(bf16[160,1024]{1,0:T(8,128)(2,1)S(1)} %get-tuple-element.37.refs_2_), channel_id=1, source_target_pairs={{0,6},{1,7},{2,0},{3,1},{4,2},{5,3},{6,4},{7,5},{8,14},{9,15},{10,... | collective-permute-start | bytes 983048 | tf_op jit(solution)/shard_map/ppermute | solution.py:239
  69.5 3.3 %collective-permute-done.10.refs_2_ = bf16[160,1024]{1,0:T(8,128)(2,1)S(1)} collective-permute-done((bf16[160,1024]{1,0:T(8,128)(2,1)S(1)}, bf16[160,1024]{1,0:T(8,128)(2,1)S(1)}, u32[]{:S(2)}, u32[]{:S(2)}) %collective-permute-start.10) | collective-permute-done | bytes 327712 | tf_op jit(solution)/shard_map/ppermute | solution.py:239
  72.8 0.1 collective-permute-done.12.refs_7_
  73.0 0.4 collective-permute-start.21
  73.3 5.7 %collective-permute-done.17.refs_3_ = bf16[160,1024]{1,0:T(8,128)(2,1)S(1)} collective-permute-done((bf16[160,1024]{1,0:T(8,128)(2,1)S(1)}, bf16[160,1024]{1,0:T(8,128)(2,1)S(1)}, u32[]{:S(2)}, u32[]{:S(2)}) %collective-permute-start.17) | collective-permute-done | bytes 327712 | tf_op jit(solution)/shard_map/ppermute | solution.py:239
  79.1 0.5 collective-permute-start.20
  79.6 0.8 collective-permute-start.11
  80.4 2.4 %collective-permute-start.13 = (bf16[160,1024]{1,0:T(8,128)(2,1)S(1)}, bf16[160,1024]{1,0:T(8,128)(2,1)S(1)}, u32[]{:S(2)}, u32[]{:S(2)}) collective-permute-start(bf16[160,1024]{1,0:T(8,128)(2,1)S(1)} %collective-permute-done.12.refs_7_), channel_id=1, source_target_pairs={{0,6},{1,7},{2,0},{3,1},{4,2},{5,3},{6,4},{7,5},{8,14},{9,15},{10,... | collective-permute-start | bytes 983048 | tf_op jit(solution)/shard_map/ppermute | solution.py:239
  82.9 3.2 %shard_map.135.refs_4_ = f32[320,448]{1,0:T(8,128)S(1)} custom-call(s32[4]{0:T(128)S(1)} %add_add_fusion.1.blocks_ref, bf16[448,8192]{1,0:T(8,128)(2,1)S(1)} %bitcast.30, bf16[160,1024]{1,0:T(8,128)(2,1)S(1)} %collective-permute-done.14.refs_0_, bf16[160,1024]{1,0:T(8,128)(2,1)S(1)} %collective-permute-done.18.refs_1_, ...), custom_call_target="tpu_custom_call" | custom-call | flops 1174405120 | bytes 6291456 | tf_op jit(solution)/shard_map/pallas_call | solution.py:215
  86.1 4.3 %collective-permute-done.11.refs_2_ = bf16[160,1024]{1,0:T(8,128)(2,1)S(1)} collective-permute-done((bf16[160,1024]{1,0:T(8,128)(2,1)S(1)}, bf16[160,1024]{1,0:T(8,128)(2,1)S(1)}, u32[]{:S(2)}, u32[]{:S(2)}) %collective-permute-start.11) | collective-permute-done | bytes 327712 | tf_op jit(solution)/shard_map/ppermute | solution.py:239
  90.4 0.5 collective-permute-start.23
  91.0 1.0 collective-permute-done.22.refs_0_
  92.0 0.5 collective-permute-done.23.refs_1_
  92.5 1.9 %shard_map.136 = f32[320,448]{1,0:T(8,128)S(1)} custom-call(s32[2]{0:T(128)S(1)} %pad_add_fusion.2.blocks_ref, bf16[448,8192]{1,0:T(8,128)(2,1)S(1)} %bitcast.31, bf16[160,1024]{1,0:T(8,128)(2,1)S(1)} %collective-permute-done.22.refs_0_, bf16[160,1024]{1,0:T(8,128)(2,1)S(1)} %collective-permute-done.23.refs_1_, ...), custom_call_target="tpu_custom_call" | custom-call | flops 587202560 | bytes 3145728 | tf_op jit(solution)/shard_map/pallas_call | solution.py:215
  94.4 0.8 copy-done
  95.2 0.1 multiply_reduce_fusion
  95.4 0.2 collective-permute-start.24
  95.6 0.2 convert_reduce_fusion
  95.8 0.8 collective-permute-done.24
  96.6 1.4 %collective-permute-start.25 = (f32[320]{0:T(512)S(1)}, f32[320]{0:T(512)S(1)}, u32[]{:S(2)}, u32[]{:S(2)}) collective-permute-start(f32[320]{0:T(512)S(1)} %add.249), channel_id=1, source_target_pairs={{0,2},{1,3},{2,4},{3,5},{4,6},{5,7},{6,0},{7,1},{8,10},{9,11},{10,... | collective-permute-start | bytes 3848 | tf_op jit(solution)/shard_map/ppermute | solution.py:239
  98.0 1.8 %collective-permute-start.26 = (f32[320]{0:T(512)S(1)}, f32[320]{0:T(512)S(1)}, u32[]{:S(2)}, u32[]{:S(2)}) collective-permute-start(f32[320]{0:T(512)S(1)} %add.249), channel_id=1, source_target_pairs={{0,6},{1,7},{2,0},{3,1},{4,2},{5,3},{6,4},{7,5},{8,14},{9,15},{10,... | collective-permute-start | bytes 3848 | tf_op jit(solution)/shard_map/ppermute | solution.py:239
  99.8 1.7 %collective-permute-start.27 = (f32[320]{0:T(512)S(1)}, f32[320]{0:T(512)S(1)}, u32[]{:S(2)}, u32[]{:S(2)}) collective-permute-start(f32[320]{0:T(512)S(1)} %add.249), channel_id=1, source_target_pairs={{0,4},{1,5},{2,6},{3,7},{4,0},{5,1},{6,2},{7,3},{8,12},{9,13},{10,... | collective-permute-start | bytes 3848 | tf_op jit(solution)/shard_map/ppermute | solution.py:239
  101.6 0.1 add.246
  101.7 0.1 broadcast_in_dim.7
  101.8 3.2 %collective-permute-done.27 = f32[320]{0:T(512)S(1)} collective-permute-done((f32[320]{0:T(512)S(1)}, f32[320]{0:T(512)S(1)}, u32[]{:S(2)}, u32[]{:S(2)}) %collective-permute-start.27) | collective-permute-done | bytes 1312 | tf_op jit(solution)/shard_map/ppermute | solution.py:239
  104.9 1.2 multiply_convert_fusion
  106.2 0.1 broadcast_in_dim.8
  106.3 1.4 %fusion = bf16[640,512]{1,0:T(8,128)(2,1)} fusion(s32[320]{0:T(512)S(1)} %add.246, bf16[320,64]{1,0:T(8,128)(2,1)S(1)} %broadcast_in_dim.8, bf16[320,448]{1,0:T(8,128)(2,1)S(1)} %multiply_convert_fusion), kind=kOutput, calls=%fused_computation.1 | convolution fusion | flops 210575360 | bytes 984320 | tf_op jit(solution)/shard_map/dot_general | solution.py:358
  107.7 7.8 %all-to-all-start = ((bf16[16,40,512]{2,1,0:T(8,128)(2,1)}), bf16[16,40,512]{2,1,0:T(8,128)(2,1)S(1)}, u32[]{:S(2)}, u32[]{:S(2)}) async-start(bf16[16,40,512]{2,1,0:T(8,128)(2,1)} %bitcast.16), calls=%async_computation | async-start | bytes 1310720 | tf_op jit(solution)/shard_map/all_to_all | solution.py:359
  115.5 0.9 pad_maximum_fusion
  116.4 10.6 %all-to-all-done = bf16[16,40,512]{2,1,0:T(8,128)(2,1)S(1)} async-done(((bf16[16,40,512]{2,1,0:T(8,128)(2,1)}), bf16[16,40,512]{2,1,0:T(8,128)(2,1)S(1)}, u32[]{:S(2)}, u32[]{:S(2)}) %all-to-all-start) | async-done | bytes 655392 | tf_op jit(solution)/shard_map/all_to_all | solution.py:359
  127.0 0.2 add_reduce_fusion
  127.3 1.2 fusion.1
  (58 shorter events, 0.5 us)
Async XLA Ops:
  16.6 6.9 %collective-permute-start.1 = (bf16[320,1024]{1,0:T(8,128)(2,1)}, bf16[320,1024]{1,0:T(8,128)(2,1)S(1)}, u32[]{:S(2)}, u32[]{:S(2)}) collective-permute-start(bf16[320,1024]{1,0:T(8,128)(2,1)} %get-tuple-element.24), channel_id=1, source_target_pairs={{0,1},{1,0},{2,3},{3,2},{4,5},{5,4},{6,7},{7,6},{8,9},{9,8},{10,11... | collective-permute-start | bytes 1966088 | tf_op jit(solution)/shard_map/ppermute | solution.py:243
  16.8 1.1 copy-start.1
  17.9 6.5 %copy-start.9 = (bf16[320,1024]{1,0:T(8,128)(2,1)S(1)}, bf16[320,1024]{1,0:T(8,128)(2,1)}, u32[]{:S(2)}) copy-start(bf16[320,1024]{1,0:T(8,128)(2,1)} %get-tuple-element.33) | copy-start | bytes 1966084
  22.1 0.9 copy-start.3
  23.0 5.4 %collective-permute-start = (bf16[320,1024]{1,0:T(8,128)(2,1)}, bf16[320,1024]{1,0:T(8,128)(2,1)}, u32[]{:S(2)}, u32[]{:S(2)}) collective-permute-start(bf16[320,1024]{1,0:T(8,128)(2,1)} %get-tuple-element.23), channel_id=1, source_target_pairs={{0,1},{1,0},{2,3},{3,2},{4,5},{5,4},{6,7},{7,6},{8,9},{9,8},{10,11... | collective-permute-start | bytes 1966088 | tf_op jit(solution)/shard_map/ppermute | solution.py:243
  23.5 11.7 %collective-permute-start.3 = (bf16[320,1024]{1,0:T(8,128)(2,1)}, bf16[320,1024]{1,0:T(8,128)(2,1)}, u32[]{:S(2)}, u32[]{:S(2)}) collective-permute-start(bf16[320,1024]{1,0:T(8,128)(2,1)} %get-tuple-element.32), channel_id=1, source_target_pairs={{0,1},{1,0},{2,3},{3,2},{4,5},{5,4},{6,7},{7,6},{8,9},{9,8},{10,11... | collective-permute-start | bytes 1966088 | tf_op jit(solution)/shard_map/ppermute | solution.py:243
  23.5 0.9 copy-start.10
  24.4 39.9 %slice-start = ((s8[7340032]{0:T(1024)(128)(4,1)}), s8[3145728]{0:T(1024)(128)(4,1)S(1)}, s32[]{:S(2)}) async-start(s8[7340032]{0:T(1024)(128)(4,1)} %bitcast.27), calls=%async_computation.1 | async-start | bytes 6291456
  26.7 11.7 %collective-permute-start.4 = (bf16[160,1024]{1,0:T(8,128)(2,1)}, bf16[160,1024]{1,0:T(8,128)(2,1)S(1)}, u32[]{:S(2)}, u32[]{:S(2)}) collective-permute-start(bf16[160,1024]{1,0:T(8,128)(2,1)} %get-tuple-element.52), channel_id=1, source_target_pairs={{0,2},{1,3},{2,4},{3,5},{4,6},{5,7},{6,0},{7,1},{8,10},{9,11},{10,... | collective-permute-start | bytes 983048 | tf_op jit(solution)/shard_map/ppermute | solution.py:239
  28.4 35.9 %slice-start.1 = ((s8[7340032]{0:T(1024)(128)(4,1)}), s8[4194304]{0:T(1024)(128)(4,1)S(1)}, s32[]{:S(2)}) async-start(s8[7340032]{0:T(1024)(128)(4,1)} %bitcast.27), calls=%async_computation.2 | async-start | bytes 8388608
  28.4 13.2 %collective-permute-start.8 = (bf16[160,1024]{1,0:T(8,128)(2,1)}, bf16[160,1024]{1,0:T(8,128)(2,1)S(1)}, u32[]{:S(2)}, u32[]{:S(2)}) collective-permute-start(bf16[160,1024]{1,0:T(8,128)(2,1)} %get-tuple-element.53), channel_id=1, source_target_pairs={{0,6},{1,7},{2,0},{3,1},{4,2},{5,3},{6,4},{7,5},{8,14},{9,15},{10,... | collective-permute-start | bytes 983048 | tf_op jit(solution)/shard_map/ppermute | solution.py:239
  30.0 1.1 copy-start.2
  31.1 7.2 %copy-start.8 = (bf16[320,1024]{1,0:T(8,128)(2,1)S(1)}, bf16[320,1024]{1,0:T(8,128)(2,1)}, u32[]{:S(2)}) copy-start(bf16[320,1024]{1,0:T(8,128)(2,1)} %get-tuple-element.31) | copy-start | bytes 1966084
  35.0 6.7 %copy-start.4 = (bf16[320,1024]{1,0:T(8,128)(2,1)S(1)}, bf16[320,1024]{1,0:T(8,128)(2,1)}, u32[]{:S(2)}) copy-start(bf16[320,1024]{1,0:T(8,128)(2,1)} %copy-done.3) | copy-start | bytes 1966084
  35.0 11.5 %copy-start.6 = (bf16[4,80,1024]{2,1,0:T(8,128)(2,1)S(1)}, bf16[4,80,1024]{2,1,0:T(8,128)(2,1)}, u32[]{:S(2)}) copy-start(bf16[4,80,1024]{2,1,0:T(8,128)(2,1)} %param.19) | copy-start | bytes 1966084
  35.0 11.5 %copy-start.7 = (bf16[4,80,1024]{2,1,0:T(8,128)(2,1)S(1)}, bf16[4,80,1024]{2,1,0:T(8,128)(2,1)}, u32[]{:S(2)}) copy-start(bf16[4,80,1024]{2,1,0:T(8,128)(2,1)} %param.20) | copy-start | bytes 1966084
  35.0 11.6 %collective-permute-start.2 = (bf16[320,1024]{1,0:T(8,128)(2,1)S(1)}, bf16[320,1024]{1,0:T(8,128)(2,1)S(1)}, u32[]{:S(2)}, u32[]{:S(2)}) collective-permute-start(bf16[320,1024]{1,0:T(8,128)(2,1)S(1)} %get-tuple-element.30), channel_id=1, source_target_pairs={{0,1},{1,0},{2,3},{3,2},{4,5},{5,4},{6,7},{7,6},{8,9},{9,8},{10,11... | collective-permute-start | bytes 1966088 | tf_op jit(solution)/shard_map/ppermute | solution.py:243
  39.7 11.9 %collective-permute-start.5 = (bf16[160,1024]{1,0:T(8,128)(2,1)S(1)}, bf16[160,1024]{1,0:T(8,128)(2,1)S(1)}, u32[]{:S(2)}, u32[]{:S(2)}) collective-permute-start(bf16[160,1024]{1,0:T(8,128)(2,1)S(1)} %get-tuple-element.50), channel_id=1, source_target_pairs={{0,2},{1,3},{2,4},{3,5},{4,6},{5,7},{6,0},{7,1},{8,10},{9,11},{10,... | collective-permute-start | bytes 983048 | tf_op jit(solution)/shard_map/ppermute | solution.py:239
  40.1 17.4 %collective-permute-start.7 = (bf16[160,1024]{1,0:T(8,128)(2,1)S(1)}, bf16[160,1024]{1,0:T(8,128)(2,1)S(1)}, u32[]{:S(2)}, u32[]{:S(2)}) collective-permute-start(bf16[160,1024]{1,0:T(8,128)(2,1)S(1)} %get-tuple-element.51), channel_id=1, source_target_pairs={{0,2},{1,3},{2,4},{3,5},{4,6},{5,7},{6,0},{7,1},{8,10},{9,11},{10,... | collective-permute-start | bytes 983048 | tf_op jit(solution)/shard_map/ppermute | solution.py:239
  43.0 14.4 %collective-permute-start.6 = (bf16[160,1024]{1,0:T(8,128)(2,1)S(1)}, bf16[160,1024]{1,0:T(8,128)(2,1)S(1)}, u32[]{:S(2)}, u32[]{:S(2)}) collective-permute-start(bf16[160,1024]{1,0:T(8,128)(2,1)S(1)} %get-tuple-element.54), channel_id=1, source_target_pairs={{0,6},{1,7},{2,0},{3,1},{4,2},{5,3},{6,4},{7,5},{8,14},{9,15},{10,... | collective-permute-start | bytes 983048 | tf_op jit(solution)/shard_map/ppermute | solution.py:239
  44.8 14.1 %collective-permute-start.9 = (bf16[160,1024]{1,0:T(8,128)(2,1)S(1)}, bf16[160,1024]{1,0:T(8,128)(2,1)S(1)}, u32[]{:S(2)}, u32[]{:S(2)}) collective-permute-start(bf16[160,1024]{1,0:T(8,128)(2,1)S(1)} %get-tuple-element.55), channel_id=1, source_target_pairs={{0,6},{1,7},{2,0},{3,1},{4,2},{5,3},{6,4},{7,5},{8,14},{9,15},{10,... | collective-permute-start | bytes 983048 | tf_op jit(solution)/shard_map/ppermute | solution.py:239
  60.5 3.8 %collective-permute-start.15 = (bf16[160,1024]{1,0:T(8,128)(2,1)S(1)}, bf16[160,1024]{1,0:T(8,128)(2,1)S(1)}, u32[]{:S(2)}, u32[]{:S(2)}) collective-permute-start(bf16[160,1024]{1,0:T(8,128)(2,1)S(1)} %get-tuple-element.37.refs_2_), channel_id=1, source_target_pairs={{0,1},{1,0},{2,3},{3,2},{4,5},{5,4},{6,7},{7,6},{8,9},{9,8},{10,11... | collective-permute-start | bytes 983048 | tf_op jit(solution)/shard_map/ppermute | solution.py:243
  60.5 3.8 %collective-permute-start.16 = (bf16[160,1024]{1,0:T(8,128)(2,1)S(1)}, bf16[160,1024]{1,0:T(8,128)(2,1)S(1)}, u32[]{:S(2)}, u32[]{:S(2)}) collective-permute-start(bf16[160,1024]{1,0:T(8,128)(2,1)S(1)} %get-tuple-element.36.refs_3_), channel_id=1, source_target_pairs={{0,1},{1,0},{2,3},{3,2},{4,5},{5,4},{6,7},{7,6},{8,9},{9,8},{10,11... | collective-permute-start | bytes 983048 | tf_op jit(solution)/shard_map/ppermute | solution.py:243
  61.1 11.8 %collective-permute-start.10 = (bf16[160,1024]{1,0:T(8,128)(2,1)S(1)}, bf16[160,1024]{1,0:T(8,128)(2,1)S(1)}, u32[]{:S(2)}, u32[]{:S(2)}) collective-permute-start(bf16[160,1024]{1,0:T(8,128)(2,1)S(1)} %get-tuple-element.37.refs_2_), channel_id=1, source_target_pairs={{0,2},{1,3},{2,4},{3,5},{4,6},{5,7},{6,0},{7,1},{8,10},{9,11},{10,... | collective-permute-start | bytes 983048 | tf_op jit(solution)/shard_map/ppermute | solution.py:239
  62.3 10.6 %collective-permute-start.12 = (bf16[160,1024]{1,0:T(8,128)(2,1)S(1)}, bf16[160,1024]{1,0:T(8,128)(2,1)S(1)}, u32[]{:S(2)}, u32[]{:S(2)}) collective-permute-start(bf16[160,1024]{1,0:T(8,128)(2,1)S(1)} %get-tuple-element.36.refs_3_), channel_id=1, source_target_pairs={{0,6},{1,7},{2,0},{3,1},{4,2},{5,3},{6,4},{7,5},{8,14},{9,15},{10,... | collective-permute-start | bytes 983048 | tf_op jit(solution)/shard_map/ppermute | solution.py:239
  66.2 12.8 %collective-permute-start.17 = (bf16[160,1024]{1,0:T(8,128)(2,1)S(1)}, bf16[160,1024]{1,0:T(8,128)(2,1)S(1)}, u32[]{:S(2)}, u32[]{:S(2)}) collective-permute-start(bf16[160,1024]{1,0:T(8,128)(2,1)S(1)} %get-tuple-element.36.refs_3_), channel_id=1, source_target_pairs={{0,2},{1,3},{2,4},{3,5},{4,6},{5,7},{6,0},{7,1},{8,10},{9,11},{10,... | collective-permute-start | bytes 983048 | tf_op jit(solution)/shard_map/ppermute | solution.py:239
  66.4 12.7 %collective-permute-start.19 = (bf16[160,1024]{1,0:T(8,128)(2,1)S(1)}, bf16[160,1024]{1,0:T(8,128)(2,1)S(1)}, u32[]{:S(2)}, u32[]{:S(2)}) collective-permute-start(bf16[160,1024]{1,0:T(8,128)(2,1)S(1)} %get-tuple-element.37.refs_2_), channel_id=1, source_target_pairs={{0,6},{1,7},{2,0},{3,1},{4,2},{5,3},{6,4},{7,5},{8,14},{9,15},{10,... | collective-permute-start | bytes 983048 | tf_op jit(solution)/shard_map/ppermute | solution.py:239
  72.8 7.5 %collective-permute-start.14 = (bf16[160,1024]{1,0:T(8,128)(2,1)S(1)}, bf16[160,1024]{1,0:T(8,128)(2,1)S(1)}, u32[]{:S(2)}, u32[]{:S(2)}) collective-permute-start(bf16[160,1024]{1,0:T(8,128)(2,1)S(1)} %collective-permute-done.10.refs_2_), channel_id=1, source_target_pairs={{0,1},{1,0},{2,3},{3,2},{4,5},{5,4},{6,7},{7,6},{8,9},{9,8},{10,11... | collective-permute-start | bytes 983048 | tf_op jit(solution)/shard_map/ppermute | solution.py:243
  73.0 9.9 %collective-permute-start.21 = (bf16[160,1024]{1,0:T(8,128)(2,1)S(1)}, bf16[160,1024]{1,0:T(8,128)(2,1)S(1)}, u32[]{:S(2)}, u32[]{:S(2)}) collective-permute-start(bf16[160,1024]{1,0:T(8,128)(2,1)S(1)} %collective-permute-done.12.refs_7_), channel_id=1, source_target_pairs={{0,1},{1,0},{2,3},{3,2},{4,5},{5,4},{6,7},{7,6},{8,9},{9,8},{10,11... | collective-permute-start | bytes 983048 | tf_op jit(solution)/shard_map/ppermute | solution.py:243
  79.0 3.8 %collective-permute-start.18 = (bf16[160,1024]{1,0:T(8,128)(2,1)S(1)}, bf16[160,1024]{1,0:T(8,128)(2,1)S(1)}, u32[]{:S(2)}, u32[]{:S(2)}) collective-permute-start(bf16[160,1024]{1,0:T(8,128)(2,1)S(1)} %collective-permute-done.17.refs_3_), channel_id=1, source_target_pairs={{0,1},{1,0},{2,3},{3,2},{4,5},{5,4},{6,7},{7,6},{8,9},{9,8},{10,11... | collective-permute-start | bytes 983048 | tf_op jit(solution)/shard_map/ppermute | solution.py:243
  79.1 3.8 %collective-permute-start.20 = (bf16[160,1024]{1,0:T(8,128)(2,1)S(1)}, bf16[160,1024]{1,0:T(8,128)(2,1)S(1)}, u32[]{:S(2)}, u32[]{:S(2)}) collective-permute-start(bf16[160,1024]{1,0:T(8,128)(2,1)S(1)} %collective-permute-done.19.refs_6_), channel_id=1, source_target_pairs={{0,1},{1,0},{2,3},{3,2},{4,5},{5,4},{6,7},{7,6},{8,9},{9,8},{10,11... | collective-permute-start | bytes 983048 | tf_op jit(solution)/shard_map/ppermute | solution.py:243
  79.6 10.8 %collective-permute-start.11 = (bf16[160,1024]{1,0:T(8,128)(2,1)S(1)}, bf16[160,1024]{1,0:T(8,128)(2,1)S(1)}, u32[]{:S(2)}, u32[]{:S(2)}) collective-permute-start(bf16[160,1024]{1,0:T(8,128)(2,1)S(1)} %collective-permute-done.10.refs_2_), channel_id=1, source_target_pairs={{0,2},{1,3},{2,4},{3,5},{4,6},{5,7},{6,0},{7,1},{8,10},{9,11},{10,... | collective-permute-start | bytes 983048 | tf_op jit(solution)/shard_map/ppermute | solution.py:239
  80.4 10.0 %collective-permute-start.13 = (bf16[160,1024]{1,0:T(8,128)(2,1)S(1)}, bf16[160,1024]{1,0:T(8,128)(2,1)S(1)}, u32[]{:S(2)}, u32[]{:S(2)}) collective-permute-start(bf16[160,1024]{1,0:T(8,128)(2,1)S(1)} %collective-permute-done.12.refs_7_), channel_id=1, source_target_pairs={{0,6},{1,7},{2,0},{3,1},{4,2},{5,3},{6,4},{7,5},{8,14},{9,15},{10,... | collective-permute-start | bytes 983048 | tf_op jit(solution)/shard_map/ppermute | solution.py:239
  82.9 8.1 %copy-start.12 = (s32[80]{0:T(128)S(1)}, s32[80]{0:T(128)}, u32[]{:S(2)}) copy-start(s32[80]{0:T(128)} %param.18) | copy-start | bytes 964
  90.4 1.6 %collective-permute-start.22 = (bf16[160,1024]{1,0:T(8,128)(2,1)S(1)}, bf16[160,1024]{1,0:T(8,128)(2,1)S(1)}, u32[]{:S(2)}, u32[]{:S(2)}) collective-permute-start(bf16[160,1024]{1,0:T(8,128)(2,1)S(1)} %collective-permute-done.11.refs_2_), channel_id=1, source_target_pairs={{0,1},{1,0},{2,3},{3,2},{4,5},{5,4},{6,7},{7,6},{8,9},{9,8},{10,11... | collective-permute-start | bytes 983048 | tf_op jit(solution)/shard_map/ppermute | solution.py:243
  90.4 2.1 %collective-permute-start.23 = (bf16[160,1024]{1,0:T(8,128)(2,1)S(1)}, bf16[160,1024]{1,0:T(8,128)(2,1)S(1)}, u32[]{:S(2)}, u32[]{:S(2)}) collective-permute-start(bf16[160,1024]{1,0:T(8,128)(2,1)S(1)} %collective-permute-done.13.refs_3_), channel_id=1, source_target_pairs={{0,1},{1,0},{2,3},{3,2},{4,5},{5,4},{6,7},{7,6},{8,9},{9,8},{10,11... | collective-permute-start | bytes 983048 | tf_op jit(solution)/shard_map/ppermute | solution.py:243
  91.0 10.6 %copy-start.11 = (bf16[448]{0:T(512)(128)(2,1)S(1)}, bf16[448]{0:T(512)(128)(2,1)}, u32[]{:S(2)}) copy-start(bf16[448]{0:T(512)(128)(2,1)} %param.23) | copy-start | bytes 2692
  94.4 0.8 copy-start
  95.2 20.3 %copy-start.5 = (bf16[160,1024]{1,0:T(8,128)(2,1)S(1)}, bf16[160,1024]{1,0:T(8,128)(2,1)}, u32[]{:S(2)}) copy-start(bf16[160,1024]{1,0:T(8,128)(2,1)} %get-tuple-element.49) | copy-start | bytes 983044
  95.4 1.2 collective-permute-start.24
  96.6 5.1 %collective-permute-start.25 = (f32[320]{0:T(512)S(1)}, f32[320]{0:T(512)S(1)}, u32[]{:S(2)}, u32[]{:S(2)}) collective-permute-start(f32[320]{0:T(512)S(1)} %add.249), channel_id=1, source_target_pairs={{0,2},{1,3},{2,4},{3,5},{4,6},{5,7},{6,0},{7,1},{8,10},{9,11},{10,... | collective-permute-start | bytes 3848 | tf_op jit(solution)/shard_map/ppermute | solution.py:239
  98.0 3.8 %collective-permute-start.26 = (f32[320]{0:T(512)S(1)}, f32[320]{0:T(512)S(1)}, u32[]{:S(2)}, u32[]{:S(2)}) collective-permute-start(f32[320]{0:T(512)S(1)} %add.249), channel_id=1, source_target_pairs={{0,6},{1,7},{2,0},{3,1},{4,2},{5,3},{6,4},{7,5},{8,14},{9,15},{10,... | collective-permute-start | bytes 3848 | tf_op jit(solution)/shard_map/ppermute | solution.py:239
  99.8 5.1 %collective-permute-start.27 = (f32[320]{0:T(512)S(1)}, f32[320]{0:T(512)S(1)}, u32[]{:S(2)}, u32[]{:S(2)}) collective-permute-start(f32[320]{0:T(512)S(1)} %add.249), channel_id=1, source_target_pairs={{0,4},{1,5},{2,6},{3,7},{4,0},{5,1},{6,2},{7,3},{8,12},{9,13},{10,... | collective-permute-start | bytes 3848 | tf_op jit(solution)/shard_map/ppermute | solution.py:239
  107.7 19.3 %all-to-all-start = ((bf16[16,40,512]{2,1,0:T(8,128)(2,1)}), bf16[16,40,512]{2,1,0:T(8,128)(2,1)S(1)}, u32[]{:S(2)}, u32[]{:S(2)}) async-start(bf16[16,40,512]{2,1,0:T(8,128)(2,1)} %bitcast.16), calls=%async_computation | async-start | bytes 1310720 | tf_op jit(solution)/shard_map/all_to_all | solution.py:359

commit v3 on v2

--- a/solution.py
+++ b/solution.py
@@ -120,7 +120,7 @@
             ],
         ),
         out_shape=[jax.ShapeDtypeStruct((rows, cols), jnp.bfloat16)] * (1 + count),
-        compiler_params=pltpu.CompilerParams(vmem_limit_bytes=60 << 20),
+        compiler_params=pltpu.CompilerParams(vmem_limit_bytes=40 << 20),
         cost_estimate=pl.CostEstimate(
             flops=2 * count * rows * cols * cols,
             bytes_accessed=32 << 20,
@@ -129,12 +129,12 @@
     )(
         blocks,
         lengths,
-        query,
-        token_keys,
-        token_values,
-        cache_keys.reshape(row_count, slot_count, head_dim),
-        stored_values.reshape(row_count, slot_count, head_dim),
-        out_weight,
+        in_hbm(query),
+        in_hbm(token_keys),
+        in_hbm(token_values),
+        in_hbm(cache_keys.reshape(row_count, slot_count, head_dim)),
+        in_hbm(stored_values.reshape(row_count, slot_count, head_dim)),
+        in_hbm(out_weight),
     )
 
 
@@ -169,13 +169,13 @@
             pltpu.VMEM((count, depth, cols), jnp.bfloat16),
             pltpu.SemaphoreType.DMA((count,)),
         ],
-        compiler_params=pltpu.CompilerParams(vmem_limit_bytes=50 << 20),
+        compiler_params=pltpu.CompilerParams(vmem_limit_bytes=24 << 20),
         cost_estimate=pl.CostEstimate(
             flops=2 * count * rows * depth * cols,
             bytes_accessed=2 * count * (depth + rows) * cols,
             transcendentals=0,
         ),
-    )(blocks, context, out_weight)
+    )(blocks, context, in_hbm(out_weight))
 
 
 def talker_product(total, pieces, proj_columns, blocks):
@@ -189,18 +189,13 @@
 
     def body(blocks_ref, w_ref, *refs):
         part_refs, refs = list(refs[: len(parts)]), refs[len(parts) :]
-        out_ref, w_buf, sems = refs[len(first) :]
-        loads = []
-        for k in range(count):
-            at = pl.ds(pl.multiple_of(blocks_ref[k] * depth, depth), depth)
-            loads.append(pltpu.make_async_copy(w_ref.at[:, at], w_buf.at[k], sems.at[k]))
-            loads[k].start()
+        out_ref = refs[-1]
         for k in range(count):
             piece = jnp.concatenate([part_refs.pop(0)[...] for _ in range(sizes[k])])
-            loads[k].wait()
+            at = pl.ds(pl.multiple_of(blocks_ref[k] * depth, depth), depth)
             product = lax.dot_general(
                 piece,
-                w_buf[k],
+                w_ref[:, at],
                 (((1,), (1,)), ((), ())),
                 preferred_element_type=jnp.float32,
             )
@@ -216,15 +211,11 @@
         body,
         in_specs=[
             pl.BlockSpec(memory_space=pltpu.SMEM),
-            pl.BlockSpec(memory_space=pltpu.HBM),
+            vmem,
         ]
         + [vmem] * len(parts + first),
         out_specs=vmem,
         out_shape=jax.ShapeDtypeStruct((rows, cols), jnp.float32),
-        scratch_shapes=[
-            pltpu.VMEM((count, cols, depth), jnp.bfloat16),
-            pltpu.SemaphoreType.DMA((count,)),
-        ],
         compiler_params=pltpu.CompilerParams(vmem_limit_bytes=20 << 20),
         cost_estimate=pl.CostEstimate(
             flops=2 * count * rows * depth * cols,
@@ -239,12 +230,23 @@
     return lax.ppermute(x, "mp", [(i, (i + 2 * by) % count) for i in range(count)])
 
 
+def onward(x):
+    count = lax.axis_size("mp")
+    return lax.ppermute(x, "mp", [(i, (i + 2 - 4 * (i % 2)) % count) for i in range(count)])
+
+
+def across(x, by):
+    count = lax.axis_size("mp")
+    moves = [(i, (i + 1 + 2 * by if i % 2 == 0 else i - 1 - 2 * by) % count) for i in range(count)]
+    return lax.ppermute(x, "mp", moves)
+
+
 def swap(x):
     return lax.ppermute(x, "mp", [(i, i ^ 1) for i in range(lax.axis_size("mp"))])
 
 
-def after(x, y):
-    return lax.optimization_barrier((x, y))[0]
+def in_hbm(x):
+    return pltpu.with_memory_space_constraint(x, pltpu.HBM)
 
 
 def wide(x):
@@ -271,67 +273,65 @@
 ):
     step_count, row_count, query_cols = query.shape
     rows = step_count * row_count
-    half = rows // 2
-    top, low = slice(0, half), slice(half, rows)
     n_dp = lax.axis_size("dp")
     n_mp = lax.axis_size("mp")
     mp = lax.axis_index("mp")
     y, core = mp // 2, mp % 2
     talk_cols = talker_proj.shape[1]
 
-    def blocks(shifts):
-        ids = []
-        for by in shifts:
-            at = (2 * y + 2 * by) % n_mp
-            ids += [at + 1 - core, at + core]
+    ahead = 1 - 2 * core
+
+    def blocks(*wanted):
+        ids = [(2 * (y + shift)) % n_mp + core + other * ahead for shift, other in wanted]
         return jnp.stack(ids).astype(jnp.int32)
 
-    context, far_away, far_here, up_away, up_here = attend_and_project(
-        query, token_keys, token_values, cache_keys, stored_values, lengths, out_weight, blocks([2, 1])
-    )
-    far_got, up_got = swap(far_away), swap(up_away)
-    down_away, down_here = head_product(context, out_weight, blocks([-1]))
-    far_got, context = lax.optimization_barrier((far_got, after(context, down_here)))
-    down_got = swap(down_away)
-    up_far = shift_y(narrow(wide(far_here[top]) + wide(far_got[top])), 1)
-    down_far = shift_y(narrow(wide(far_here[low]) + wide(far_got[low])), -1)
-    below_low = shift_y(narrow(wide(up_here[low]) + wide(up_got[low])), 1)
-    down_got, context = lax.optimization_barrier((down_got, context))
-    above_top = shift_y(narrow(wide(down_here[top]) + wide(down_got[top])), -1)
-    own_away, own_here = head_product(context, out_weight, blocks([0]))
-    own_got = swap(own_away)
-    below_top = shift_y(narrow(wide(up_here[top]) + wide(up_got[top]) + wide(up_far)), 1)
-    above_low = shift_y(narrow(wide(down_here[low]) + wide(down_got[low]) + wide(down_far)), -1)
+    context, far_away, far_here = attend_and_project(
+        query,
+        token_keys,
+        token_values,
+        cache_keys,
+        stored_values,
+        lengths,
+        out_weight,
+        blocks((2, 1), (2, 0)),
+    )
+    far_got = swap(far_away)
+    other_away, other_here = head_product(context, out_weight, blocks((-ahead, 0), (ahead, 1)))
+    far_got, other_away, context = lax.optimization_barrier((far_got, other_away, context))
+    far = narrow(wide(far_here) + wide(far_got))
+    far_on = onward(far)
+    other_got = swap(other_away)
+    other = narrow(wide(other_here) + wide(other_got))
+    other, context = lax.optimization_barrier((other, context))
+    other_in = across(other, 1)
+    same_away, same_here, own_away, own_here = head_product(
+        context, out_weight, blocks((-ahead, 1), (ahead, 0), (0, 1), (0, 0))
+    )
+    same_got, own_got = swap(same_away), swap(own_away)
+    same_in = onward(narrow(wide(same_here) + wide(same_got) + wide(far_on)))
     residual = residual.reshape(rows, -1)
     embedding = embedding.reshape(rows, -1)
 
-    def finish(part, below, above):
-        base = wide(residual[part]) + wide(own_here[part]) + wide(own_got[part])
-        return narrow(base + wide(below) + wide(above))
-
-    hidden_top = finish(top, below_top, above_top)
-    hidden_low = finish(low, below_low, above_low)
-    both_top = hidden_top + embedding[top]
-    both_low = hidden_low + embedding[low]
+    base = wide(residual) + wide(own_here) + wide(own_got)
+    hidden = narrow(base + wide(same_in) + wide(other_in))
+    both = hidden + embedding
 
     proj_columns = talker_proj.T
-    own = [both_top, both_low]
-    own_got = [swap(both_top), swap(both_low)]
-    below_top, above_low = shift_y(both_top, 1), shift_y(both_low, -1)
-    mixed = talker_product(None, [own_got, own], proj_columns, blocks([0]))
-    both_top, both_low, mixed = lax.optimization_barrier((both_top, both_low, mixed))
-    below_low, above_top = shift_y(both_low, 1), shift_y(both_top, -1)
-    beyond_top, beyond_low = shift_y(below_top, 1), shift_y(above_low, -1)
-    below, above = [below_top, below_low], [above_top, above_low]
-    below_got = [swap(below_top), swap(below_low)]
-    above_got = [swap(above_top), swap(above_low)]
+    near = onward(both)
+    cross = across(both, -1)
+    both_got = swap(both)
+    beyond = onward(near)
+    mixed = talker_product(None, [[both_got], [both]], proj_columns, blocks((0, 1), (0, 0)))
+    near_got = swap(near)
     mixed = talker_product(
-        mixed, [below_got, below, above_got, above], proj_columns, blocks([-1, 1])
-    )
-    beyond_top, beyond_low, mixed = lax.optimization_barrier((beyond_top, beyond_low, mixed))
-    beyond = [beyond_top, beyond_low]
-    beyond_got = [swap(beyond_top), swap(beyond_low)]
-    mixed = talker_product(mixed, [beyond_got, beyond], proj_columns, blocks([2]))
+        mixed, [[near_got], [near]], proj_columns, blocks((ahead, 1), (-ahead, 0))
+    )
+    cross_got = swap(cross)
+    mixed = talker_product(
+        mixed, [[cross_got], [cross]], proj_columns, blocks((ahead, 0), (-ahead, 1))
+    )
+    beyond, mixed = lax.optimization_barrier((beyond, mixed))
+    mixed = talker_product(mixed, [[swap(beyond)], [beyond]], proj_columns, blocks((2, 1), (2, 0)))
 
     squares = jnp.sum(mixed * mixed, -1)
     squares = squares + swap(squares)
@@ -364,7 +364,6 @@
     got_row = jnp.where(got_place < 0, rows, got_step * row_count + got_place)
     put = got_row[None, :] == jnp.arange(rows, dtype=jnp.int32)[:, None]
     talker_input = jnp.dot(narrow(put), got[:, :talk_cols])
-    hidden = jnp.concatenate([hidden_top, hidden_low])
     return (
         hidden.reshape(step_count, row_count, -1),
         talker_input.reshape(step_count, row_count, -1),

time: 129 us -> 112 us (0.87)
  starting transfers between devices: 34 us -> 9.26 us
  blocking collectives: 0 us -> 19.4 us
  Pallas kernels: 30.4 us -> 25.8 us
  other arithmetic: 10.3 us -> 6.12 us
  local copies, waits for them, and re-layouts: 5.14 us -> 0.97 us
  waiting for transfers between devices: 45.1 us -> 47.8 us
    ppermute x0 -> x6, waiting for transfers between devices: none -> 40.7 us  [the longest x4 33.5 us: onward(): lax.ppermute(x, 'mp', [(i, (i + 2 - 4 * (i % 2)) % count) for i in range(...]
    ppermute x15 -> x3, waiting for transfers between devices: 32.1 us -> 4.04 us  [shift_y(): lax.ppermute(x, 'mp', [(i, (i + 2 * by) % count) for i in range(count)])]
    ppermute x15 -> x3, starting transfers between devices: 23.4 us -> 2.03 us  [shift_y(): lax.ppermute(x, 'mp', [(i, (i + 2 * by) % count) for i in range(count)])]
    all_to_all x0 -> x1, blocking collectives: none -> 19.4 us  [local(): lax.all_to_all(sent.reshape(n_dp, slots // n_dp, -1), 'dp', 0, 0, tiled=T...]
    all_to_all x1 -> x0, waiting for transfers between devices: 10.6 us -> none  [local(): lax.all_to_all(sent.reshape(n_dp, slots // n_dp, -1), 'dp', 0, 0, tiled=T...]
    all_to_all x1 -> x0, starting transfers between devices: 7.78 us -> none  [local(): lax.all_to_all(sent.reshape(n_dp, slots // n_dp, -1), 'dp', 0, 0, tiled=T...]
    pallas_call x1, Pallas kernels: 15.4 us -> 10.6 us  [attend_and_project(): pl.pallas_call(body, grid_spec=pltpu.PrefetchScalarGridSpec(num_scalar_pr...]
    unnamed x30 -> x14, local copies, waits for them, and re-layouts: 4.77 us -> 0.69 us
  transfers between devices with their start and end apart: 29 -> 18, of which waited for: 13 -> 10; matrix products, arithmetic and copies ran while one was open for 5% -> 3% of each run, Pallas kernels for 10% -> 12%
where the time goes in v3:
time: 112 us
  waiting for transfers between devices  47.8 us (43%)
  Pallas kernels  25.8 us (23%)
  blocking collectives  19.4 us (17%)
  starting transfers between devices  9.26 us (8%)
  other arithmetic  6.12 us (5%)
  matrix products  1.72 us (2%)
    ppermute x4, waiting for transfers between devices, onward(): lax.ppermute(x, 'mp', [(i, (i + 2 - 4 * (i % 2)) % count) for i in range(...  33.5 us
    all_to_all x1, blocking collectives, local(): lax.all_to_all(sent.reshape(n_dp, slots // n_dp, -1), 'dp', 0, 0, tiled=T...  19.4 us
    pallas_call x1, Pallas kernels, attend_and_project(): pl.pallas_call(body, grid_spec=pltpu.PrefetchScalarGridSpec(num_scalar_pr...  10.6 us
    pallas_call x2, Pallas kernels, head_product(): pl.pallas_call(body, in_specs=[pl.BlockSpec(memory_space=pltpu.SMEM), pl....  9.64 us
    ppermute x2, waiting for transfers between devices, across(): return lax.ppermute(x, 'mp', moves)  7.13 us
    pallas_call x4, Pallas kernels, talker_product(): pl.pallas_call(body, in_specs=[pl.BlockSpec(memory_space=pltpu.SMEM), vme...  5.63 us
    ppermute x3, waiting for transfers between devices, shift_y(): lax.ppermute(x, 'mp', [(i, (i + 2 * by) % count) for i in range(count)])  4.04 us
    ppermute x9, starting transfers between devices, swap(): lax.ppermute(x, 'mp', [(i, i ^ 1) for i in range(lax.axis_size('mp'))])  3.91 us
  transfers between devices with their start and end apart: 18, of which 10 were waited for; matrix products, arithmetic and copies ran while one was open for 3% of the time, Pallas kernels for 12%

profile of v3, /device:TPU:0, one launch (start us, length us, event | category | flops | bytes accessed | tf_op | source)
XLA Modules:
  0.0 112.0 jit_solution(9258791951799054999)
XLA Ops:
  0.7 0.1 pad_add_fusion.2.blocks_ref
  0.7 0.7 copy-done
  1.4 10.6 %shard_map.131 = (bf16[320,1024]{1,0:T(8,128)(2,1)S(1)}, bf16[320,1024]{1,0:T(8,128)(2,1)S(1)}, bf16[320,1024]{1,0:T(8,128)(2,1)S(1)}) custom-call(s32[2]{0:T(128)S(1)} %pad_add_fusion.2.blocks_ref, s32[80]{0:T(128)S(1)} %copy-done, bf16[4,80,1024]{2,1,0:T(8,128)(2,1)} %q_ref.1, bf16[4,80,128]{2,1,0:T(8,128)(2,1)} %tk_ref.1, bf16[4,80,128]{2,1,0:T(8,128)(2,1)} %tv_ref.1, ...), custom_call_target="tpu_custom_call" | custom-call | flops 1342177280 | bytes 33554432 | tf_op jit(solution)/shard_map/pallas_call | solution.py:103
  12.0 0.1 collective-permute-start
  12.1 0.1 pad_add_fusion.1.blocks_ref
  12.2 3.8 %shard_map.132 = (bf16[320,1024]{1,0:T(8,128)(2,1)S(1)}, bf16[320,1024]{1,0:T(8,128)(2,1)S(1)}) custom-call(s32[2]{0:T(128)S(1)} %pad_add_fusion.1.blocks_ref, bf16[320,1024]{1,0:T(8,128)(2,1)S(1)} %get-tuple-element.24.context_ref, bf16[1024,8192]{1,0:T(8,128)(2,1)} %w_ref.5), custom_call_target="tpu_custom_call" | custom-call | flops 1342177280 | bytes 5505024 | tf_op jit(solution)/shard_map/pallas_call | solution.py:159
  16.1 0.0 collective-permute-done
  16.1 0.5 collective-permute-start.1
  16.6 0.1 pad_add_fusion.blocks_ref
  16.7 1.3 %add_convert_fusion.1 = bf16[320,1024]{1,0:T(8,128)(2,1)S(1)} fusion(bf16[320,1024]{1,0:T(8,128)(2,1)} %collective-permute-done, bf16[320,1024]{1,0:T(8,128)(2,1)S(1)} %get-tuple-element.29), kind=kLoop, calls=%fused_computation.6 | loop fusion | flops 1310720 | bytes 1966080 | tf_op jit(solution)/shard_map/convert_element_type | solution.py:257
  18.0 1.7 %collective-permute-start.4 = (bf16[320,1024]{1,0:T(8,128)(2,1)S(1)}, bf16[320,1024]{1,0:T(8,128)(2,1)S(1)}, u32[]{:S(2)}, u32[]{:S(2)}) collective-permute-start(bf16[320,1024]{1,0:T(8,128)(2,1)S(1)} %add_convert_fusion.1), channel_id=1, source_target_pairs={{0,2},{1,7},{2,4},{3,1},{4,6},{5,3},{6,0},{7,5},{8,10},{9,15},{10,... | collective-permute-start | bytes 1966088 | tf_op jit(solution)/shard_map/ppermute | solution.py:235
  19.7 0.0 collective-permute-done.1
  19.7 1.5 %add_convert_fusion.2 = bf16[320,1024]{1,0:T(8,128)(2,1)S(1)} fusion(bf16[320,1024]{1,0:T(8,128)(2,1)} %collective-permute-done.1, bf16[320,1024]{1,0:T(8,128)(2,1)S(1)} %get-tuple-element.19), kind=kLoop, calls=%fused_computation.7 | loop fusion | flops 1310720 | bytes 1966080 | tf_op jit(solution)/shard_map/convert_element_type | solution.py:257
  21.2 0.0 slice-start.1
  21.2 5.8 %shard_map.133 = (bf16[320,1024]{1,0:T(8,128)(2,1)S(1)}, bf16[320,1024]{1,0:T(8,128)(2,1)S(1)}, bf16[320,1024]{1,0:T(8,128)(2,1)S(1)}, bf16[320,1024]{1,0:T(8,128)(2,1)S(1)}) custom-call(s32[4]{0:T(128)S(1)} %pad_add_fusion.blocks_ref, bf16[320,1024]{1,0:T(8,128)(2,1)S(1)} %get-tuple-element.24.context_ref, bf16[1024,8192]{1,0:T(8,128)(2,1)} %w_ref.5), custom_call_target="tpu_custom_call" | custom-call | flops 2684354560 | bytes 11010048 | tf_op jit(solution)/shard_map/pallas_call | solution.py:159
  27.0 1.3 %collective-permute-start.3 = (bf16[320,1024]{1,0:T(8,128)(2,1)S(1)}, bf16[320,1024]{1,0:T(8,128)(2,1)S(1)}, u32[]{:S(2)}, u32[]{:S(2)}) collective-permute-start(bf16[320,1024]{1,0:T(8,128)(2,1)S(1)} %get-tuple-element.28), channel_id=1, source_target_pairs={{0,1},{1,0},{2,3},{3,2},{4,5},{5,4},{6,7},{7,6},{8,9},{9,8},{10,11... | collective-permute-start | bytes 1966088 | tf_op jit(solution)/shard_map/ppermute | solution.py:245
  28.3 0.5 collective-permute-start.6
  28.8 0.6 collective-permute-start.2
  29.4 0.4 collective-permute-done.4
  29.9 0.2 collective-permute-done.3
  30.1 0.3 add_convert_fusion
  30.4 0.8 collective-permute-start.5
  31.2 7.1 %collective-permute-done.6 = bf16[320,1024]{1,0:T(8,128)(2,1)S(1)} collective-permute-done((bf16[320,1024]{1,0:T(8,128)(2,1)S(1)}, bf16[320,1024]{1,0:T(8,128)(2,1)S(1)}, u32[]{:S(2)}, u32[]{:S(2)}) %collective-permute-start.6) | collective-permute-done | bytes 655392 | tf_op jit(solution)/shard_map/ppermute | solution.py:241
  38.3 0.0 collective-permute-done.2
  38.3 8.5 %collective-permute-done.5 = bf16[320,1024]{1,0:T(8,128)(2,1)S(1)} collective-permute-done((bf16[320,1024]{1,0:T(8,128)(2,1)S(1)}, bf16[320,1024]{1,0:T(8,128)(2,1)S(1)}, u32[]{:S(2)}, u32[]{:S(2)}) %collective-permute-start.5) | collective-permute-done | bytes 655392 | tf_op jit(solution)/shard_map/ppermute | solution.py:235
  46.8 1.8 %bitcast_add_fusion = (bf16[320,1024]{1,0:T(8,128)(2,1)S(1)}, bf16[320,1024]{1,0:T(8,128)(2,1)}) fusion(bf16[4,80,1024]{2,1,0:T(8,128)(2,1)S(1)} %copy-done.1, bf16[320,1024]{1,0:T(8,128)(2,1)S(1)} %collective-permute-done.6, bf16[320,1024]{1,0:T(8,128)(2,1)S(1)} %collective-permute-done.5, bf16[320,1024]{1,0:T(8,128)(2,1)S(1)} %collective-permute-done.2, ...), kind=kLoop, calls=%fused_computation.13 | loop fusion | flops 3604480 | bytes 5242880 | tf_op jit(solution)/shard_map/add | solution.py:317
  48.6 0.0 collective-permute-start.7
  48.6 0.3 collective-permute-start.9
  48.9 0.7 collective-permute-start.12
  49.6 17.3 %collective-permute-done.7.refs_1_ = bf16[320,1024]{1,0:T(8,128)(2,1)S(1)} collective-permute-done((bf16[320,1024]{1,0:T(8,128)(2,1)S(1)}, bf16[320,1024]{1,0:T(8,128)(2,1)S(1)}, u32[]{:S(2)}, u32[]{:S(2)}) %collective-permute-start.7) | collective-permute-done | bytes 655392 | tf_op jit(solution)/shard_map/ppermute | solution.py:235
  66.9 0.0 collective-permute-start.11
  66.9 0.0 collective-permute-done.9.refs_1_
  66.9 0.5 collective-permute-start.10
  67.4 0.0 collective-permute-start.8
  67.4 0.1 pad_add_fusion.3.blocks_ref
  67.5 0.1 pad_add_fusion.5.blocks_ref
  67.6 0.1 pad_add_fusion.4.blocks_ref
  67.7 0.0 collective-permute-done.12.refs_0_
  67.7 1.4 %shard_map.134.refs_2_ = f32[320,448]{1,0:T(8,128)S(1)} custom-call(s32[2]{0:T(128)S(1)} %pad_add_fusion.5.blocks_ref, bf16[448,8192]{1,0:T(8,128)(2,1)S(1)} %bitcast.23, bf16[320,1024]{1,0:T(8,128)(2,1)S(1)} %collective-permute-done.12.refs_0_, bf16[320,1024]{1,0:T(8,128)(2,1)S(1)} %get-tuple-element.34.refs_1_), custom_call_target="tpu_custom_call" | custom-call | flops 587202560 | bytes 3145728 | tf_op jit(solution)/shard_map/pallas_call | solution.py:210
  69.1 1.4 %shard_map.135.refs_2_ = f32[320,448]{1,0:T(8,128)S(1)} custom-call(s32[2]{0:T(128)S(1)} %pad_add_fusion.4.blocks_ref, bf16[448,8192]{1,0:T(8,128)(2,1)S(1)} %bitcast.24, bf16[320,1024]{1,0:T(8,128)(2,1)S(1)} %collective-permute-done.11.refs_0_, bf16[320,1024]{1,0:T(8,128)(2,1)S(1)} %collective-permute-done.7.refs_1_, f32[320,448]{1,0:T(8,128)S(1)} %shard_map.134.refs_2_), custom_call_target="tpu_custom_call" | custom-call | flops 587202560 | bytes 3145728 | tf_op jit(solution)/shard_map/pallas_call | solution.py:210
  70.5 0.0 copy-start.4
  70.5 0.0 collective-permute-done.10.refs_0_
  70.5 1.4 %shard_map.136.refs_2_ = f32[320,448]{1,0:T(8,128)S(1)} custom-call(s32[2]{0:T(128)S(1)} %pad_add_fusion.3.blocks_ref, bf16[448,8192]{1,0:T(8,128)(2,1)S(1)} %bitcast.25, bf16[320,1024]{1,0:T(8,128)(2,1)S(1)} %collective-permute-done.10.refs_0_, bf16[320,1024]{1,0:T(8,128)(2,1)S(1)} %collective-permute-done.9.refs_1_, f32[320,448]{1,0:T(8,128)S(1)} %shard_map.135.refs_2_), custom_call_target="tpu_custom_call" | custom-call | flops 587202560 | bytes 3145728 | tf_op jit(solution)/shard_map/pallas_call | solution.py:210
  72.0 7.3 %collective-permute-done.8.refs_1_ = bf16[320,1024]{1,0:T(8,128)(2,1)S(1)} collective-permute-done((bf16[320,1024]{1,0:T(8,128)(2,1)S(1)}, bf16[320,1024]{1,0:T(8,128)(2,1)S(1)}, u32[]{:S(2)}, u32[]{:S(2)}) %collective-permute-start.8) | collective-permute-done | bytes 655392 | tf_op jit(solution)/shard_map/ppermute | solution.py:235
  79.2 0.0 collective-permute-start.13
  79.2 0.0 copy-start.3
  79.3 2.1 %collective-permute-done.13.refs_0_ = bf16[320,1024]{1,0:T(8,128)(2,1)S(1)} collective-permute-done((bf16[320,1024]{1,0:T(8,128)(2,1)S(1)}, bf16[320,1024]{1,0:T(8,128)(2,1)S(1)}, u32[]{:S(2)}, u32[]{:S(2)}) %collective-permute-start.13) | collective-permute-done | bytes 655392 | tf_op jit(solution)/shard_map/ppermute | solution.py:245
  81.3 1.4 %shard_map.137 = f32[320,448]{1,0:T(8,128)S(1)} custom-call(s32[2]{0:T(128)S(1)} %pad_add_fusion.2.blocks_ref, bf16[448,8192]{1,0:T(8,128)(2,1)S(1)} %bitcast.26, bf16[320,1024]{1,0:T(8,128)(2,1)S(1)} %collective-permute-done.13.refs_0_, bf16[320,1024]{1,0:T(8,128)(2,1)S(1)} %collective-permute-done.8.refs_1_, f32[320,448]{1,0:T(8,128)S(1)} %shard_map.136.refs_2_), custom_call_target="tpu_custom_call" | custom-call | flops 587202560 | bytes 3145728 | tf_op jit(solution)/shard_map/pallas_call | solution.py:210
  82.7 0.1 multiply_reduce_fusion
  82.9 0.2 collective-permute-start.14
  83.1 0.2 convert_reduce_fusion
  83.3 0.8 collective-permute-done.14
  84.1 1.5 %collective-permute-start.16 = (f32[320]{0:T(512)S(1)}, f32[320]{0:T(512)S(1)}, u32[]{:S(2)}, u32[]{:S(2)}) collective-permute-start(f32[320]{0:T(512)S(1)} %add.235), channel_id=1, source_target_pairs={{0,6},{1,7},{2,0},{3,1},{4,2},{5,3},{6,4},{7,5},{8,14},{9,15},{10,... | collective-permute-start | bytes 3848 | tf_op jit(solution)/shard_map/ppermute | solution.py:230
  85.6 0.6 collective-permute-start.15
  86.2 0.1 add.233
  86.2 0.1 broadcast_in_dim.7
  86.3 2.9 %collective-permute-done.17 = f32[320]{0:T(512)S(1)} collective-permute-done((f32[320]{0:T(512)S(1)}, f32[320]{0:T(512)S(1)}, u32[]{:S(2)}, u32[]{:S(2)}) %collective-permute-start.17) | collective-permute-done | bytes 1312 | tf_op jit(solution)/shard_map/ppermute | solution.py:230
  89.2 1.2 %collective-permute-done.15 = f32[320]{0:T(512)S(1)} collective-permute-done((f32[320]{0:T(512)S(1)}, f32[320]{0:T(512)S(1)}, u32[]{:S(2)}, u32[]{:S(2)}) %collective-permute-start.15) | collective-permute-done | bytes 1312 | tf_op jit(solution)/shard_map/ppermute | solution.py:230
  90.4 0.1 multiply_convert_fusion
  90.5 0.1 broadcast_in_dim.8
  90.6 0.6 fusion.4
  91.2 19.4 %all_to_all.5 = bf16[16,40,512]{2,1,0:T(8,128)(2,1)S(1)} all-to-all(bf16[16,40,512]{2,1,0:T(8,128)(2,1)S(1)} %bitcast.32), channel_id=1, replica_groups=mesh['dp'=16,'mp'=8] {'dp'}, dimensions={0} | all-to-all | bytes 1310720 | tf_op jit(solution)/shard_map/all_to_all | solution.py:359
  110.6 0.2 add_reduce_fusion
  110.8 1.2 %fusion.5 = bf16[320,448]{1,0:T(8,128)(2,1)} fusion(bf16[640,512]{1,0:T(8,128)(2,1)S(1)} %bitcast.30, s32[640]{0:T(1024)S(1)} %fusion.16), kind=kOutput, calls=%fused_computation.11 | convolution fusion | flops 183705600 | bytes 944640 | tf_op jit(solution)/shard_map/dot_general | solution.py:366
  (21 shorter events, 0.1 us)
Async XLA Ops:
  0.7 0.7 copy-start
  12.0 4.1 %collective-permute-start = (bf16[320,1024]{1,0:T(8,128)(2,1)S(1)}, bf16[320,1024]{1,0:T(8,128)(2,1)}, u32[]{:S(2)}, u32[]{:S(2)}) collective-permute-start(bf16[320,1024]{1,0:T(8,128)(2,1)S(1)} %get-tuple-element.20), channel_id=1, source_target_pairs={{0,1},{1,0},{2,3},{3,2},{4,5},{5,4},{6,7},{7,6},{8,9},{9,8},{10,11... | collective-permute-start | bytes 1966088 | tf_op jit(solution)/shard_map/ppermute | solution.py:245
  16.1 3.7 %collective-permute-start.1 = (bf16[320,1024]{1,0:T(8,128)(2,1)S(1)}, bf16[320,1024]{1,0:T(8,128)(2,1)}, u32[]{:S(2)}, u32[]{:S(2)}) collective-permute-start(bf16[320,1024]{1,0:T(8,128)(2,1)S(1)} %get-tuple-element.22), channel_id=1, source_target_pairs={{0,1},{1,0},{2,3},{3,2},{4,5},{5,4},{6,7},{7,6},{8,9},{9,8},{10,11... | collective-permute-start | bytes 1966088 | tf_op jit(solution)/shard_map/ppermute | solution.py:245
  18.0 11.9 %collective-permute-start.4 = (bf16[320,1024]{1,0:T(8,128)(2,1)S(1)}, bf16[320,1024]{1,0:T(8,128)(2,1)S(1)}, u32[]{:S(2)}, u32[]{:S(2)}) collective-permute-start(bf16[320,1024]{1,0:T(8,128)(2,1)S(1)} %add_convert_fusion.1), channel_id=1, source_target_pairs={{0,2},{1,7},{2,4},{3,1},{4,6},{5,3},{6,0},{7,5},{8,10},{9,15},{10,... | collective-permute-start | bytes 1966088 | tf_op jit(solution)/shard_map/ppermute | solution.py:235
  19.7 47.9 %slice-start = ((s8[7340032]{0:T(1024)(128)(4,1)}), s8[4194304]{0:T(1024)(128)(4,1)S(1)}, s32[]{:S(2)}) async-start(s8[7340032]{0:T(1024)(128)(4,1)} %bitcast.21), calls=%async_computation.1 | async-start | bytes 8388608
  21.2 46.4 %slice-start.1 = ((s8[7340032]{0:T(1024)(128)(4,1)}), s8[3145728]{0:T(1024)(128)(4,1)S(1)}, s32[]{:S(2)}) async-start(s8[7340032]{0:T(1024)(128)(4,1)} %bitcast.21), calls=%async_computation.2 | async-start | bytes 6291456
  27.0 3.0 %collective-permute-start.3 = (bf16[320,1024]{1,0:T(8,128)(2,1)S(1)}, bf16[320,1024]{1,0:T(8,128)(2,1)S(1)}, u32[]{:S(2)}, u32[]{:S(2)}) collective-permute-start(bf16[320,1024]{1,0:T(8,128)(2,1)S(1)} %get-tuple-element.28), channel_id=1, source_target_pairs={{0,1},{1,0},{2,3},{3,2},{4,5},{5,4},{6,7},{7,6},{8,9},{9,8},{10,11... | collective-permute-start | bytes 1966088 | tf_op jit(solution)/shard_map/ppermute | solution.py:245
  28.3 10.0 %collective-permute-start.6 = (bf16[320,1024]{1,0:T(8,128)(2,1)S(1)}, bf16[320,1024]{1,0:T(8,128)(2,1)S(1)}, u32[]{:S(2)}, u32[]{:S(2)}) collective-permute-start(bf16[320,1024]{1,0:T(8,128)(2,1)S(1)} %add_convert_fusion.2), channel_id=1, source_target_pairs={{0,3},{1,6},{2,5},{3,0},{4,7},{5,2},{6,1},{7,4},{8,11},{9,14},{10,... | collective-permute-start | bytes 1966088 | tf_op jit(solution)/shard_map/ppermute | solution.py:241
  28.8 9.5 %collective-permute-start.2 = (bf16[320,1024]{1,0:T(8,128)(2,1)S(1)}, bf16[320,1024]{1,0:T(8,128)(2,1)S(1)}, u32[]{:S(2)}, u32[]{:S(2)}) collective-permute-start(bf16[320,1024]{1,0:T(8,128)(2,1)S(1)} %get-tuple-element.26), channel_id=1, source_target_pairs={{0,1},{1,0},{2,3},{3,2},{4,5},{5,4},{6,7},{7,6},{8,9},{9,8},{10,11... | collective-permute-start | bytes 1966088 | tf_op jit(solution)/shard_map/ppermute | solution.py:245
  30.0 16.8 %copy-start.1 = (bf16[4,80,1024]{2,1,0:T(8,128)(2,1)S(1)}, bf16[4,80,1024]{2,1,0:T(8,128)(2,1)}, u32[]{:S(2)}) copy-start(bf16[4,80,1024]{2,1,0:T(8,128)(2,1)} %param.20) | copy-start | bytes 1966084
  30.1 16.8 %copy-start.2 = (bf16[4,80,1024]{2,1,0:T(8,128)(2,1)S(1)}, bf16[4,80,1024]{2,1,0:T(8,128)(2,1)}, u32[]{:S(2)}) copy-start(bf16[4,80,1024]{2,1,0:T(8,128)(2,1)} %param.19) | copy-start | bytes 1966084
  30.4 16.4 %collective-permute-start.5 = (bf16[320,1024]{1,0:T(8,128)(2,1)S(1)}, bf16[320,1024]{1,0:T(8,128)(2,1)S(1)}, u32[]{:S(2)}, u32[]{:S(2)}) collective-permute-start(bf16[320,1024]{1,0:T(8,128)(2,1)S(1)} %add_convert_fusion), channel_id=1, source_target_pairs={{0,2},{1,7},{2,4},{3,1},{4,6},{5,3},{6,0},{7,5},{8,10},{9,15},{10,... | collective-permute-start | bytes 1966088 | tf_op jit(solution)/shard_map/ppermute | solution.py:235
  48.6 18.3 %collective-permute-start.7 = (bf16[320,1024]{1,0:T(8,128)(2,1)S(1)}, bf16[320,1024]{1,0:T(8,128)(2,1)S(1)}, u32[]{:S(2)}, u32[]{:S(2)}) collective-permute-start(bf16[320,1024]{1,0:T(8,128)(2,1)S(1)} %get-tuple-element.34.refs_1_), channel_id=1, source_target_pairs={{0,2},{1,7},{2,4},{3,1},{4,6},{5,3},{6,0},{7,5},{8,10},{9,15},{10,... | collective-permute-start | bytes 1966088 | tf_op jit(solution)/shard_map/ppermute | solution.py:235
  48.6 18.3 %collective-permute-start.9 = (bf16[320,1024]{1,0:T(8,128)(2,1)S(1)}, bf16[320,1024]{1,0:T(8,128)(2,1)S(1)}, u32[]{:S(2)}, u32[]{:S(2)}) collective-permute-start(bf16[320,1024]{1,0:T(8,128)(2,1)S(1)} %get-tuple-element.34.refs_1_), channel_id=1, source_target_pairs={{0,7},{1,2},{2,1},{3,4},{4,3},{5,6},{6,5},{7,0},{8,15},{9,10},{10,... | collective-permute-start | bytes 1966088 | tf_op jit(solution)/shard_map/ppermute | solution.py:241
  48.9 18.7 %collective-permute-start.12 = (bf16[320,1024]{1,0:T(8,128)(2,1)S(1)}, bf16[320,1024]{1,0:T(8,128)(2,1)S(1)}, u32[]{:S(2)}, u32[]{:S(2)}) collective-permute-start(bf16[320,1024]{1,0:T(8,128)(2,1)S(1)} %get-tuple-element.34.refs_1_), channel_id=1, source_target_pairs={{0,1},{1,0},{2,3},{3,2},{4,5},{5,4},{6,7},{7,6},{8,9},{9,8},{10,11... | collective-permute-start | bytes 1966088 | tf_op jit(solution)/shard_map/ppermute | solution.py:245
  66.9 2.2 %collective-permute-start.11 = (bf16[320,1024]{1,0:T(8,128)(2,1)S(1)}, bf16[320,1024]{1,0:T(8,128)(2,1)S(1)}, u32[]{:S(2)}, u32[]{:S(2)}) collective-permute-start(bf16[320,1024]{1,0:T(8,128)(2,1)S(1)} %collective-permute-done.7.refs_1_), channel_id=1, source_target_pairs={{0,1},{1,0},{2,3},{3,2},{4,5},{5,4},{6,7},{7,6},{8,9},{9,8},{10,11... | collective-permute-start | bytes 1966088 | tf_op jit(solution)/shard_map/ppermute | solution.py:245
  66.9 3.6 %collective-permute-start.10 = (bf16[320,1024]{1,0:T(8,128)(2,1)S(1)}, bf16[320,1024]{1,0:T(8,128)(2,1)S(1)}, u32[]{:S(2)}, u32[]{:S(2)}) collective-permute-start(bf16[320,1024]{1,0:T(8,128)(2,1)S(1)} %collective-permute-done.9.refs_1_), channel_id=1, source_target_pairs={{0,1},{1,0},{2,3},{3,2},{4,5},{5,4},{6,7},{7,6},{8,9},{9,8},{10,11... | collective-permute-start | bytes 1966088 | tf_op jit(solution)/shard_map/ppermute | solution.py:245
  67.4 11.8 %collective-permute-start.8 = (bf16[320,1024]{1,0:T(8,128)(2,1)S(1)}, bf16[320,1024]{1,0:T(8,128)(2,1)S(1)}, u32[]{:S(2)}, u32[]{:S(2)}) collective-permute-start(bf16[320,1024]{1,0:T(8,128)(2,1)S(1)} %collective-permute-done.7.refs_1_), channel_id=1, source_target_pairs={{0,2},{1,7},{2,4},{3,1},{4,6},{5,3},{6,0},{7,5},{8,10},{9,15},{10,... | collective-permute-start | bytes 1966088 | tf_op jit(solution)/shard_map/ppermute | solution.py:235
  70.5 8.7 %copy-start.4 = (s32[80]{0:T(128)S(1)}, s32[80]{0:T(128)}, u32[]{:S(2)}) copy-start(s32[80]{0:T(128)} %param.18) | copy-start | bytes 964
  79.2 2.1 %collective-permute-start.13 = (bf16[320,1024]{1,0:T(8,128)(2,1)S(1)}, bf16[320,1024]{1,0:T(8,128)(2,1)S(1)}, u32[]{:S(2)}, u32[]{:S(2)}) collective-permute-start(bf16[320,1024]{1,0:T(8,128)(2,1)S(1)} %collective-permute-done.8.refs_1_), channel_id=1, source_target_pairs={{0,1},{1,0},{2,3},{3,2},{4,5},{5,4},{6,7},{7,6},{8,9},{9,8},{10,11... | collective-permute-start | bytes 1966088 | tf_op jit(solution)/shard_map/ppermute | solution.py:245
  79.2 7.1 %copy-start.3 = (bf16[448]{0:T(512)(128)(2,1)S(1)}, bf16[448]{0:T(512)(128)(2,1)}, u32[]{:S(2)}) copy-start(bf16[448]{0:T(512)(128)(2,1)} %param.23) | copy-start | bytes 2692
  82.9 1.2 %collective-permute-start.14 = (f32[320]{0:T(512)S(1)}, f32[320]{0:T(512)S(1)}, u32[]{:S(2)}, u32[]{:S(2)}) collective-permute-start(f32[320]{0:T(512)S(1)} %multiply_reduce_fusion), channel_id=1, source_target_pairs={{0,1},{1,0},{2,3},{3,2},{4,5},{5,4},{6,7},{7,6},{8,9},{9,8},{10,11... | collective-permute-start | bytes 3848 | tf_op jit(solution)/shard_map/ppermute | solution.py:245
  84.1 5.1 %collective-permute-start.17 = (f32[320]{0:T(512)S(1)}, f32[320]{0:T(512)S(1)}, u32[]{:S(2)}, u32[]{:S(2)}) collective-permute-start(f32[320]{0:T(512)S(1)} %add.235), channel_id=1, source_target_pairs={{0,4},{1,5},{2,6},{3,7},{4,0},{5,1},{6,2},{7,3},{8,12},{9,13},{10,... | collective-permute-start | bytes 3848 | tf_op jit(solution)/shard_map/ppermute | solution.py:230
  84.1 5.1 %collective-permute-start.16 = (f32[320]{0:T(512)S(1)}, f32[320]{0:T(512)S(1)}, u32[]{:S(2)}, u32[]{:S(2)}) collective-permute-start(f32[320]{0:T(512)S(1)} %add.235), channel_id=1, source_target_pairs={{0,6},{1,7},{2,0},{3,1},{4,2},{5,3},{6,4},{7,5},{8,14},{9,15},{10,... | collective-permute-start | bytes 3848 | tf_op jit(solution)/shard_map/ppermute | solution.py:230
  85.6 4.8 %collective-permute-start.15 = (f32[320]{0:T(512)S(1)}, f32[320]{0:T(512)S(1)}, u32[]{:S(2)}, u32[]{:S(2)}) collective-permute-start(f32[320]{0:T(512)S(1)} %add.235), channel_id=1, source_target_pairs={{0,2},{1,3},{2,4},{3,5},{4,6},{5,7},{6,0},{7,1},{8,10},{9,11},{10,... | collective-permute-start | bytes 3848 | tf_op jit(solution)/shard_map/ppermute | solution.py:230

commit v4 on v3

--- a/solution.py
+++ b/solution.py
@@ -169,7 +169,7 @@
             pltpu.VMEM((count, depth, cols), jnp.bfloat16),
             pltpu.SemaphoreType.DMA((count,)),
         ],
-        compiler_params=pltpu.CompilerParams(vmem_limit_bytes=24 << 20),
+        compiler_params=pltpu.CompilerParams(vmem_limit_bytes=28 << 20),
         cost_estimate=pl.CostEstimate(
             flops=2 * count * rows * depth * cols,
             bytes_accessed=2 * count * (depth + rows) * cols,
@@ -295,25 +295,26 @@
         out_weight,
         blocks((2, 1), (2, 0)),
     )
-    far_got = swap(far_away)
-    other_away, other_here = head_product(context, out_weight, blocks((-ahead, 0), (ahead, 1)))
-    far_got, other_away, context = lax.optimization_barrier((far_got, other_away, context))
-    far = narrow(wide(far_here) + wide(far_got))
+    far = narrow(wide(far_here) + wide(swap(far_away)))
+    far, context = lax.optimization_barrier((far, context))
     far_on = onward(far)
-    other_got = swap(other_away)
+    other_away, other_here, same_away, same_here, own_away, own_here = head_product(
+        context,
+        out_weight,
+        blocks((-ahead, 0), (ahead, 1), (-ahead, 1), (ahead, 0), (0, 1), (0, 0)),
+    )
+    other_got, same_got = swap(other_away), swap(same_away)
     other = narrow(wide(other_here) + wide(other_got))
-    other, context = lax.optimization_barrier((other, context))
+    far_on, own_away = lax.optimization_barrier((far_on, own_away))
+    own_got = swap(own_away)
     other_in = across(other, 1)
-    same_away, same_here, own_away, own_here = head_product(
-        context, out_weight, blocks((-ahead, 1), (ahead, 0), (0, 1), (0, 0))
-    )
-    same_got, own_got = swap(same_away), swap(own_away)
     same_in = onward(narrow(wide(same_here) + wide(same_got) + wide(far_on)))
     residual = residual.reshape(rows, -1)
     embedding = embedding.reshape(rows, -1)
 
-    base = wide(residual) + wide(own_here) + wide(own_got)
-    hidden = narrow(base + wide(same_in) + wide(other_in))
+    base = wide(residual) + wide(own_here) + wide(own_got) + wide(other_in)
+    base = lax.optimization_barrier(base)
+    hidden = narrow(base + wide(same_in))
     both = hidden + embedding
 
     proj_columns = talker_proj.T
@@ -335,7 +336,8 @@
 
     squares = jnp.sum(mixed * mixed, -1)
     squares = squares + swap(squares)
-    squares = squares + shift_y(squares, 1) + shift_y(squares, -1) + shift_y(squares, 2)
+    beside = onward(squares)
+    squares = squares + shift_y(squares, 2) + (beside + swap(beside))
     normed = (
         mixed
         * lax.rsqrt(squares / (talk_cols * n_mp) + epsilon)[:, None]

time: 112 us -> 112 us (level)
  waiting for transfers between devices: 47.8 us -> 52.1 us
  other arithmetic: 6.12 us -> 3.58 us
  Pallas kernels: 25.8 us -> 23.5 us
  starting transfers between devices: 9.26 us -> 7.78 us
  blocking collectives: 19.4 us -> 20.8 us
    ppermute x4 -> x5, waiting for transfers between devices: 33.5 us -> 37.9 us  [onward(): lax.ppermute(x, 'mp', [(i, (i + 2 - 4 * (i % 2)) % count) for i in range(...]
    ppermute x3 -> x1, waiting for transfers between devices: 4.04 us -> 0.34 us  [shift_y(): lax.ppermute(x, 'mp', [(i, (i + 2 * by) % count) for i in range(count)])]
    ppermute x9 -> x10, waiting for transfers between devices: 3.11 us -> 6.1 us  [swap(): lax.ppermute(x, 'mp', [(i, i ^ 1) for i in range(lax.axis_size('mp'))])]
    pallas_call x2 -> x1, Pallas kernels: 9.64 us -> 7.27 us  [head_product(): pl.pallas_call(body, in_specs=[pl.BlockSpec(memory_space=pltpu.SMEM), pl....]
    convert_element_type x3, other arithmetic: 3.13 us -> 0.8 us  [narrow(): return x.astype(jnp.bfloat16)]
    ppermute x9 -> x10, starting transfers between devices: 3.91 us -> 2.36 us  [swap(): lax.ppermute(x, 'mp', [(i, i ^ 1) for i in range(lax.axis_size('mp'))])]
    all_to_all x1, blocking collectives: 19.4 us -> 20.8 us  [local(): lax.all_to_all(sent.reshape(n_dp, slots // n_dp, -1), 'dp', 0, 0, tiled=T...]
    ppermute x4 -> x5, starting transfers between devices: 2.54 us -> 3.1 us  [onward(): lax.ppermute(x, 'mp', [(i, (i + 2 - 4 * (i % 2)) % count) for i in range(...]
  transfers between devices with their start and end apart: 18 -> 18, of which waited for: 10 -> 13; matrix products, arithmetic and copies ran while one was open for 3% -> 2% of each run, Pallas kernels for 12% -> 10%
where the time goes in v4:
time: 112 us; the launch traced here: 111 us
  waiting for transfers between devices  52.1 us (47%)
  Pallas kernels  23.5 us (21%)
  blocking collectives  20.8 us (19%)
  starting transfers between devices  7.78 us (7%)
  other arithmetic  3.58 us (3%)
  matrix products  1.72 us (2%)
    ppermute x5, waiting for transfers between devices, onward(): lax.ppermute(x, 'mp', [(i, (i + 2 - 4 * (i % 2)) % count) for i in range(...  37.9 us
    all_to_all x1, blocking collectives, local(): lax.all_to_all(sent.reshape(n_dp, slots // n_dp, -1), 'dp', 0, 0, tiled=T...  20.8 us
    pallas_call x1, Pallas kernels, attend_and_project(): pl.pallas_call(body, grid_spec=pltpu.PrefetchScalarGridSpec(num_scalar_pr...  10.6 us
    ppermute x2, waiting for transfers between devices, across(): return lax.ppermute(x, 'mp', moves)  7.69 us
    pallas_call x1, Pallas kernels, head_product(): pl.pallas_call(body, in_specs=[pl.BlockSpec(memory_space=pltpu.SMEM), pl....  7.27 us
    ppermute x10, waiting for transfers between devices, swap(): lax.ppermute(x, 'mp', [(i, i ^ 1) for i in range(lax.axis_size('mp'))])  6.1 us
    pallas_call x4, Pallas kernels, talker_product(): pl.pallas_call(body, in_specs=[pl.BlockSpec(memory_space=pltpu.SMEM), vme...  5.61 us
    ppermute x5, starting transfers between devices, onward(): lax.ppermute(x, 'mp', [(i, (i + 2 - 4 * (i % 2)) % count) for i in range(...  3.1 us
  transfers between devices with their start and end apart: 18, of which 13 were waited for; matrix products, arithmetic and copies ran while one was open for 2% of the time, Pallas kernels for 10%

profile of v4, /device:TPU:0, one launch (start us, length us, event | category | flops | bytes accessed | tf_op | source)
XLA Modules:
  0.0 111.3 jit_solution(1109882061593803568)
XLA Ops:
  0.7 0.1 pad_add_fusion.blocks_ref
  0.7 0.7 copy-done
  1.4 10.6 %shard_map.131 = (bf16[320,1024]{1,0:T(8,128)(2,1)S(1)}, bf16[320,1024]{1,0:T(8,128)(2,1)S(1)}, bf16[320,1024]{1,0:T(8,128)(2,1)S(1)}) custom-call(s32[2]{0:T(128)S(1)} %pad_add_fusion.blocks_ref, s32[80]{0:T(128)S(1)} %copy-done, bf16[4,80,1024]{2,1,0:T(8,128)(2,1)} %q_ref.1, bf16[4,80,128]{2,1,0:T(8,128)(2,1)} %tk_ref.1, bf16[4,80,128]{2,1,0:T(8,128)(2,1)} %tv_ref.1, ...), custom_call_target="tpu_custom_call" | custom-call | flops 1342177280 | bytes 33554432 | tf_op jit(solution)/shard_map/pallas_call | solution.py:103
  12.0 0.1 collective-permute-start
  12.1 0.1 stack.54.blocks_ref
  12.2 1.9 %collective-permute-done = bf16[320,1024]{1,0:T(8,128)(2,1)S(1)} collective-permute-done((bf16[320,1024]{1,0:T(8,128)(2,1)S(1)}, bf16[320,1024]{1,0:T(8,128)(2,1)S(1)}, u32[]{:S(2)}, u32[]{:S(2)}) %collective-permute-start) | collective-permute-done | bytes 655392 | tf_op jit(solution)/shard_map/ppermute | solution.py:245
  14.2 0.2 add_convert_fusion.3
  14.4 0.0 slice-start.1
  14.4 1.7 %collective-permute-start.1 = (bf16[320,1024]{1,0:T(8,128)(2,1)S(1)}, bf16[320,1024]{1,0:T(8,128)(2,1)S(1)}, u32[]{:S(2)}, u32[]{:S(2)}) collective-permute-start(bf16[320,1024]{1,0:T(8,128)(2,1)S(1)} %add_convert_fusion.3), channel_id=1, source_target_pairs={{0,2},{1,7},{2,4},{3,1},{4,6},{5,3},{6,0},{7,5},{8,10},{9,15},{10,... | collective-permute-start | bytes 1966088 | tf_op jit(solution)/shard_map/ppermute | solution.py:235
  16.1 7.3 %shard_map.132 = (bf16[320,1024]{1,0:T(8,128)(2,1)S(1)}, bf16[320,1024]{1,0:T(8,128)(2,1)S(1)}, bf16[320,1024]{1,0:T(8,128)(2,1)S(1)}, bf16[320,1024]{1,0:T(8,12...) custom-call(s32[6]{0:T(128)S(1)} %stack.54.blocks_ref, ...), custom_call_target="tpu_custom_call" | custom-call | flops 4026531840 | bytes 16515072 | tf_op jit(solution)/shard_map/pallas_call | solution.py:159
  23.4 1.4 %collective-permute-start.3 = (bf16[320,1024]{1,0:T(8,128)(2,1)S(1)}, bf16[320,1024]{1,0:T(8,128)(2,1)S(1)}, u32[]{:S(2)}, u32[]{:S(2)}) collective-permute-start(bf16[320,1024]{1,0:T(8,128)(2,1)S(1)} %get-tuple-element.26), channel_id=1, source_target_pairs={{0,1},{1,0},{2,3},{3,2},{4,5},{5,4},{6,7},{7,6},{8,9},{9,8},{10,11... | collective-permute-start | bytes 1966088 | tf_op jit(solution)/shard_map/ppermute | solution.py:245
  24.8 0.1 collective-permute-start.5
  24.9 1.4 %collective-permute-done.1 = bf16[320,1024]{1,0:T(8,128)(2,1)S(1)} collective-permute-done((bf16[320,1024]{1,0:T(8,128)(2,1)S(1)}, bf16[320,1024]{1,0:T(8,128)(2,1)S(1)}, u32[]{:S(2)}, u32[]{:S(2)}) %collective-permute-start.1) | collective-permute-done | bytes 655392 | tf_op jit(solution)/shard_map/ppermute | solution.py:235
  26.3 0.0 collective-permute-start.2
  26.3 0.2 collective-permute-done.3
  26.5 0.2 add_convert_fusion.2
  26.8 0.5 collective-permute-start.4
  27.2 0.2 collective-permute-done.5
  27.5 0.3 add_convert_fusion.1
  27.8 1.4 %collective-permute-start.6 = (bf16[320,1024]{1,0:T(8,128)(2,1)S(1)}, bf16[320,1024]{1,0:T(8,128)(2,1)S(1)}, u32[]{:S(2)}, u32[]{:S(2)}) collective-permute-start(bf16[320,1024]{1,0:T(8,128)(2,1)S(1)} %add_convert_fusion.1), channel_id=1, source_target_pairs={{0,2},{1,7},{2,4},{3,1},{4,6},{5,3},{6,0},{7,5},{8,10},{9,15},{10,... | collective-permute-start | bytes 1966088 | tf_op jit(solution)/shard_map/ppermute | solution.py:235
  29.2 0.0 collective-permute-done.2
  29.2 7.7 %collective-permute-done.4 = bf16[320,1024]{1,0:T(8,128)(2,1)S(1)} collective-permute-done((bf16[320,1024]{1,0:T(8,128)(2,1)S(1)}, bf16[320,1024]{1,0:T(8,128)(2,1)S(1)}, u32[]{:S(2)}, u32[]{:S(2)}) %collective-permute-start.4) | collective-permute-done | bytes 655392 | tf_op jit(solution)/shard_map/ppermute | solution.py:241
  36.9 0.5 fusion.1
  37.3 8.3 %collective-permute-done.6 = bf16[320,1024]{1,0:T(8,128)(2,1)S(1)} collective-permute-done((bf16[320,1024]{1,0:T(8,128)(2,1)S(1)}, bf16[320,1024]{1,0:T(8,128)(2,1)S(1)}, u32[]{:S(2)}, u32[]{:S(2)}) %collective-permute-start.6) | collective-permute-done | bytes 655392 | tf_op jit(solution)/shard_map/ppermute | solution.py:235
  45.6 1.2 %bitcast_add_fusion = (bf16[320,1024]{1,0:T(8,128)(2,1)S(1)}, bf16[320,1024]{1,0:T(8,128)(2,1)}) fusion(bf16[4,80,1024]{2,1,0:T(8,128)(2,1)S(1)} %copy-done.2, f32[320,1024]{1,0:T(8,128)S(1)} %fusion.1, bf16[320,1024]{1,0:T(8,128)(2,1)S(1)} %collective-permute-done.6), kind=kLoop, calls=%fused_computation.12 | loop fusion | flops 1310720 | bytes 3932160 | tf_op jit(solution)/shard_map/add | solution.py:318
  46.9 0.0 collective-permute-start.7
  46.9 0.8 collective-permute-start.9
  47.6 0.1 collective-permute-start.12
  47.7 17.4 %collective-permute-done.7.refs_1_ = bf16[320,1024]{1,0:T(8,128)(2,1)S(1)} collective-permute-done((bf16[320,1024]{1,0:T(8,128)(2,1)S(1)}, bf16[320,1024]{1,0:T(8,128)(2,1)S(1)}, u32[]{:S(2)}, u32[]{:S(2)}) %collective-permute-start.7) | collective-permute-done | bytes 655392 | tf_op jit(solution)/shard_map/ppermute | solution.py:235
  65.2 0.0 collective-permute-start.11
  65.2 0.0 collective-permute-done.9.refs_1_
  65.2 0.5 collective-permute-start.10
  65.7 0.0 collective-permute-start.8
  65.7 0.1 pad_add_fusion.3.blocks_ref
  65.8 0.1 pad_add_fusion.2.blocks_ref
  65.8 0.1 pad_add_fusion.1.blocks_ref
  65.9 0.0 collective-permute-done.12.refs_0_
  65.9 1.4 %shard_map.133.refs_2_ = f32[320,448]{1,0:T(8,128)S(1)} custom-call(s32[2]{0:T(128)S(1)} %pad_add_fusion.3.blocks_ref, bf16[448,8192]{1,0:T(8,128)(2,1)S(1)} %bitcast.22, bf16[320,1024]{1,0:T(8,128)(2,1)S(1)} %collective-permute-done.12.refs_0_, bf16[320,1024]{1,0:T(8,128)(2,1)S(1)} %get-tuple-element.32.refs_1_), custom_call_target="tpu_custom_call" | custom-call | flops 587202560 | bytes 3145728 | tf_op jit(solution)/shard_map/pallas_call | solution.py:210
  67.4 1.4 %shard_map.134.refs_2_ = f32[320,448]{1,0:T(8,128)S(1)} custom-call(s32[2]{0:T(128)S(1)} %pad_add_fusion.2.blocks_ref, bf16[448,8192]{1,0:T(8,128)(2,1)S(1)} %bitcast.23, bf16[320,1024]{1,0:T(8,128)(2,1)S(1)} %collective-permute-done.11.refs_0_, bf16[320,1024]{1,0:T(8,128)(2,1)S(1)} %collective-permute-done.7.refs_1_, f32[320,448]{1,0:T(8,128)S(1)} %shard_map.133.refs_2_), custom_call_target="tpu_custom_call" | custom-call | flops 587202560 | bytes 3145728 | tf_op jit(solution)/shard_map/pallas_call | solution.py:210
  68.8 1.4 %shard_map.135.refs_2_ = f32[320,448]{1,0:T(8,128)S(1)} custom-call(s32[2]{0:T(128)S(1)} %pad_add_fusion.1.blocks_ref, bf16[448,8192]{1,0:T(8,128)(2,1)S(1)} %bitcast.24, bf16[320,1024]{1,0:T(8,128)(2,1)S(1)} %collective-permute-done.10.refs_0_, bf16[320,1024]{1,0:T(8,128)(2,1)S(1)} %collective-permute-done.9.refs_1_, f32[320,448]{1,0:T(8,128)S(1)} %shard_map.134.refs_2_), custom_call_target="tpu_custom_call" | custom-call | flops 587202560 | bytes 3145728 | tf_op jit(solution)/shard_map/pallas_call | solution.py:210
  70.2 0.0 copy-start.4
  70.2 0.0 copy-start.3
  70.2 7.3 %collective-permute-done.8.refs_1_ = bf16[320,1024]{1,0:T(8,128)(2,1)S(1)} collective-permute-done((bf16[320,1024]{1,0:T(8,128)(2,1)S(1)}, bf16[320,1024]{1,0:T(8,128)(2,1)S(1)}, u32[]{:S(2)}, u32[]{:S(2)}) %collective-permute-start.8) | collective-permute-done | bytes 655392 | tf_op jit(solution)/shard_map/ppermute | solution.py:235
  77.5 0.0 collective-permute-start.13
  77.5 2.1 %collective-permute-done.13.refs_0_ = bf16[320,1024]{1,0:T(8,128)(2,1)S(1)} collective-permute-done((bf16[320,1024]{1,0:T(8,128)(2,1)S(1)}, bf16[320,1024]{1,0:T(8,128)(2,1)S(1)}, u32[]{:S(2)}, u32[]{:S(2)}) %collective-permute-start.13) | collective-permute-done | bytes 655392 | tf_op jit(solution)/shard_map/ppermute | solution.py:245
  79.6 1.4 %shard_map.136 = f32[320,448]{1,0:T(8,128)S(1)} custom-call(s32[2]{0:T(128)S(1)} %pad_add_fusion.blocks_ref, bf16[448,8192]{1,0:T(8,128)(2,1)S(1)} %bitcast.25, bf16[320,1024]{1,0:T(8,128)(2,1)S(1)} %collective-permute-done.13.refs_0_, bf16[320,1024]{1,0:T(8,128)(2,1)S(1)} %collective-permute-done.8.refs_1_, f32[320,448]{1,0:T(8,128)S(1)} %shard_map.135.refs_2_), custom_call_target="tpu_custom_call" | custom-call | flops 587202560 | bytes 3145728 | tf_op jit(solution)/shard_map/pallas_call | solution.py:210
  81.0 0.1 multiply_reduce_fusion
  81.1 0.2 collective-permute-start.14
  81.4 1.0 collective-permute-done.14
  82.4 0.0 collective-permute-start.16
  82.4 0.2 convert_reduce_fusion
  82.6 1.1 collective-permute-start.15
  83.6 3.5 %collective-permute-done.16 = f32[320]{0:T(512)S(1)} collective-permute-done((f32[320]{0:T(512)S(1)}, f32[320]{0:T(512)S(1)}, u32[]{:S(2)}, u32[]{:S(2)}) %collective-permute-start.16) | collective-permute-done | bytes 1312 | tf_op jit(solution)/shard_map/ppermute | solution.py:235
  87.2 0.0 collective-permute-start.17
  87.2 0.1 add.233
  87.3 0.1 broadcast_in_dim.7
  87.4 0.3 collective-permute-done.15
  87.7 0.6 collective-permute-done.17
  88.3 0.1 multiply_convert_fusion
  88.5 0.1 broadcast_in_dim.8
  88.6 0.6 fusion.2
  89.1 20.8 %all_to_all.5 = bf16[16,40,512]{2,1,0:T(8,128)(2,1)S(1)} all-to-all(bf16[16,40,512]{2,1,0:T(8,128)(2,1)S(1)} %bitcast.30), channel_id=1, replica_groups=mesh['dp'=16,'mp'=8] {'dp'}, dimensions={0} | all-to-all | bytes 1310720 | tf_op jit(solution)/shard_map/all_to_all | solution.py:361
  109.9 0.2 add_reduce_fusion
  110.2 1.2 %fusion.3 = bf16[320,448]{1,0:T(8,128)(2,1)} fusion(bf16[640,512]{1,0:T(8,128)(2,1)S(1)} %bitcast.29, s32[640]{0:T(1024)S(1)} %fusion.14), kind=kOutput, calls=%fused_computation.10 | convolution fusion | flops 183705600 | bytes 944640 | tf_op jit(solution)/shard_map/dot_general | solution.py:368
  (20 shorter events, 0.1 us)
Async XLA Ops:
  0.7 0.7 copy-start
  12.0 2.2 %collective-permute-start = (bf16[320,1024]{1,0:T(8,128)(2,1)S(1)}, bf16[320,1024]{1,0:T(8,128)(2,1)S(1)}, u32[]{:S(2)}, u32[]{:S(2)}) collective-permute-start(bf16[320,1024]{1,0:T(8,128)(2,1)S(1)} %get-tuple-element.18), channel_id=1, source_target_pairs={{0,1},{1,0},{2,3},{3,2},{4,5},{5,4},{6,7},{7,6},{8,9},{9,8},{10,11... | collective-permute-start | bytes 1966088 | tf_op jit(solution)/shard_map/ppermute | solution.py:245
  14.2 51.8 %slice-start = ((s8[7340032]{0:T(1024)(128)(4,1)}), s8[4194304]{0:T(1024)(128)(4,1)S(1)}, s32[]{:S(2)}) async-start(s8[7340032]{0:T(1024)(128)(4,1)} %bitcast.20), calls=%async_computation.1 | async-start | bytes 8388608
  14.4 51.5 %slice-start.1 = ((s8[7340032]{0:T(1024)(128)(4,1)}), s8[3145728]{0:T(1024)(128)(4,1)S(1)}, s32[]{:S(2)}) async-start(s8[7340032]{0:T(1024)(128)(4,1)} %bitcast.20), calls=%async_computation.2 | async-start | bytes 6291456
  14.4 11.9 %collective-permute-start.1 = (bf16[320,1024]{1,0:T(8,128)(2,1)S(1)}, bf16[320,1024]{1,0:T(8,128)(2,1)S(1)}, u32[]{:S(2)}, u32[]{:S(2)}) collective-permute-start(bf16[320,1024]{1,0:T(8,128)(2,1)S(1)} %add_convert_fusion.3), channel_id=1, source_target_pairs={{0,2},{1,7},{2,4},{3,1},{4,6},{5,3},{6,0},{7,5},{8,10},{9,15},{10,... | collective-permute-start | bytes 1966088 | tf_op jit(solution)/shard_map/ppermute | solution.py:235
  23.4 3.1 %collective-permute-start.3 = (bf16[320,1024]{1,0:T(8,128)(2,1)S(1)}, bf16[320,1024]{1,0:T(8,128)(2,1)S(1)}, u32[]{:S(2)}, u32[]{:S(2)}) collective-permute-start(bf16[320,1024]{1,0:T(8,128)(2,1)S(1)} %get-tuple-element.26), channel_id=1, source_target_pairs={{0,1},{1,0},{2,3},{3,2},{4,5},{5,4},{6,7},{7,6},{8,9},{9,8},{10,11... | collective-permute-start | bytes 1966088 | tf_op jit(solution)/shard_map/ppermute | solution.py:245
  24.8 2.7 %collective-permute-start.5 = (bf16[320,1024]{1,0:T(8,128)(2,1)S(1)}, bf16[320,1024]{1,0:T(8,128)(2,1)S(1)}, u32[]{:S(2)}, u32[]{:S(2)}) collective-permute-start(bf16[320,1024]{1,0:T(8,128)(2,1)S(1)} %get-tuple-element.28), channel_id=1, source_target_pairs={{0,1},{1,0},{2,3},{3,2},{4,5},{5,4},{6,7},{7,6},{8,9},{9,8},{10,11... | collective-permute-start | bytes 1966088 | tf_op jit(solution)/shard_map/ppermute | solution.py:245
  26.3 2.9 %collective-permute-start.2 = (bf16[320,1024]{1,0:T(8,128)(2,1)S(1)}, bf16[320,1024]{1,0:T(8,128)(2,1)S(1)}, u32[]{:S(2)}, u32[]{:S(2)}) collective-permute-start(bf16[320,1024]{1,0:T(8,128)(2,1)S(1)} %get-tuple-element.24), channel_id=1, source_target_pairs={{0,1},{1,0},{2,3},{3,2},{4,5},{5,4},{6,7},{7,6},{8,9},{9,8},{10,11... | collective-permute-start | bytes 1966088 | tf_op jit(solution)/shard_map/ppermute | solution.py:245
  26.8 10.1 %collective-permute-start.4 = (bf16[320,1024]{1,0:T(8,128)(2,1)S(1)}, bf16[320,1024]{1,0:T(8,128)(2,1)S(1)}, u32[]{:S(2)}, u32[]{:S(2)}) collective-permute-start(bf16[320,1024]{1,0:T(8,128)(2,1)S(1)} %add_convert_fusion.2), channel_id=1, source_target_pairs={{0,3},{1,6},{2,5},{3,0},{4,7},{5,2},{6,1},{7,4},{8,11},{9,14},{10,... | collective-permute-start | bytes 1966088 | tf_op jit(solution)/shard_map/ppermute | solution.py:241
  27.5 9.4 %copy-start.1 = (bf16[4,80,1024]{2,1,0:T(8,128)(2,1)S(1)}, bf16[4,80,1024]{2,1,0:T(8,128)(2,1)}, u32[]{:S(2)}) copy-start(bf16[4,80,1024]{2,1,0:T(8,128)(2,1)} %param.19) | copy-start | bytes 1966084
  27.8 17.8 %collective-permute-start.6 = (bf16[320,1024]{1,0:T(8,128)(2,1)S(1)}, bf16[320,1024]{1,0:T(8,128)(2,1)S(1)}, u32[]{:S(2)}, u32[]{:S(2)}) collective-permute-start(bf16[320,1024]{1,0:T(8,128)(2,1)S(1)} %add_convert_fusion.1), channel_id=1, source_target_pairs={{0,2},{1,7},{2,4},{3,1},{4,6},{5,3},{6,0},{7,5},{8,10},{9,15},{10,... | collective-permute-start | bytes 1966088 | tf_op jit(solution)/shard_map/ppermute | solution.py:235
  36.9 8.8 %copy-start.2 = (bf16[4,80,1024]{2,1,0:T(8,128)(2,1)S(1)}, bf16[4,80,1024]{2,1,0:T(8,128)(2,1)}, u32[]{:S(2)}) copy-start(bf16[4,80,1024]{2,1,0:T(8,128)(2,1)} %param.20) | copy-start | bytes 1966084
  46.9 18.3 %collective-permute-start.7 = (bf16[320,1024]{1,0:T(8,128)(2,1)S(1)}, bf16[320,1024]{1,0:T(8,128)(2,1)S(1)}, u32[]{:S(2)}, u32[]{:S(2)}) collective-permute-start(bf16[320,1024]{1,0:T(8,128)(2,1)S(1)} %get-tuple-element.32.refs_1_), channel_id=1, source_target_pairs={{0,2},{1,7},{2,4},{3,1},{4,6},{5,3},{6,0},{7,5},{8,10},{9,15},{10,... | collective-permute-start | bytes 1966088 | tf_op jit(solution)/shard_map/ppermute | solution.py:235
  46.9 18.3 %collective-permute-start.9 = (bf16[320,1024]{1,0:T(8,128)(2,1)S(1)}, bf16[320,1024]{1,0:T(8,128)(2,1)S(1)}, u32[]{:S(2)}, u32[]{:S(2)}) collective-permute-start(bf16[320,1024]{1,0:T(8,128)(2,1)S(1)} %get-tuple-element.32.refs_1_), channel_id=1, source_target_pairs={{0,7},{1,2},{2,1},{3,4},{4,3},{5,6},{6,5},{7,0},{8,15},{9,10},{10,... | collective-permute-start | bytes 1966088 | tf_op jit(solution)/shard_map/ppermute | solution.py:241
  47.6 18.3 %collective-permute-start.12 = (bf16[320,1024]{1,0:T(8,128)(2,1)S(1)}, bf16[320,1024]{1,0:T(8,128)(2,1)S(1)}, u32[]{:S(2)}, u32[]{:S(2)}) collective-permute-start(bf16[320,1024]{1,0:T(8,128)(2,1)S(1)} %get-tuple-element.32.refs_1_), channel_id=1, source_target_pairs={{0,1},{1,0},{2,3},{3,2},{4,5},{5,4},{6,7},{7,6},{8,9},{9,8},{10,11... | collective-permute-start | bytes 1966088 | tf_op jit(solution)/shard_map/ppermute | solution.py:245
  65.2 2.2 %collective-permute-start.11 = (bf16[320,1024]{1,0:T(8,128)(2,1)S(1)}, bf16[320,1024]{1,0:T(8,128)(2,1)S(1)}, u32[]{:S(2)}, u32[]{:S(2)}) collective-permute-start(bf16[320,1024]{1,0:T(8,128)(2,1)S(1)} %collective-permute-done.7.refs_1_), channel_id=1, source_target_pairs={{0,1},{1,0},{2,3},{3,2},{4,5},{5,4},{6,7},{7,6},{8,9},{9,8},{10,11... | collective-permute-start | bytes 1966088 | tf_op jit(solution)/shard_map/ppermute | solution.py:245
  65.2 3.6 %collective-permute-start.10 = (bf16[320,1024]{1,0:T(8,128)(2,1)S(1)}, bf16[320,1024]{1,0:T(8,128)(2,1)S(1)}, u32[]{:S(2)}, u32[]{:S(2)}) collective-permute-start(bf16[320,1024]{1,0:T(8,128)(2,1)S(1)} %collective-permute-done.9.refs_1_), channel_id=1, source_target_pairs={{0,1},{1,0},{2,3},{3,2},{4,5},{5,4},{6,7},{7,6},{8,9},{9,8},{10,11... | collective-permute-start | bytes 1966088 | tf_op jit(solution)/shard_map/ppermute | solution.py:245
  65.7 11.8 %collective-permute-start.8 = (bf16[320,1024]{1,0:T(8,128)(2,1)S(1)}, bf16[320,1024]{1,0:T(8,128)(2,1)S(1)}, u32[]{:S(2)}, u32[]{:S(2)}) collective-permute-start(bf16[320,1024]{1,0:T(8,128)(2,1)S(1)} %collective-permute-done.7.refs_1_), channel_id=1, source_target_pairs={{0,2},{1,7},{2,4},{3,1},{4,6},{5,3},{6,0},{7,5},{8,10},{9,15},{10,... | collective-permute-start | bytes 1966088 | tf_op jit(solution)/shard_map/ppermute | solution.py:235
  70.2 11.2 %copy-start.4 = (s32[80]{0:T(128)S(1)}, s32[80]{0:T(128)}, u32[]{:S(2)}) copy-start(s32[80]{0:T(128)} %param.18) | copy-start | bytes 964
  70.2 17.0 %copy-start.3 = (bf16[448]{0:T(512)(128)(2,1)S(1)}, bf16[448]{0:T(512)(128)(2,1)}, u32[]{:S(2)}) copy-start(bf16[448]{0:T(512)(128)(2,1)} %param.23) | copy-start | bytes 2692
  77.5 2.1 %collective-permute-start.13 = (bf16[320,1024]{1,0:T(8,128)(2,1)S(1)}, bf16[320,1024]{1,0:T(8,128)(2,1)S(1)}, u32[]{:S(2)}, u32[]{:S(2)}) collective-permute-start(bf16[320,1024]{1,0:T(8,128)(2,1)S(1)} %collective-permute-done.8.refs_1_), channel_id=1, source_target_pairs={{0,1},{1,0},{2,3},{3,2},{4,5},{5,4},{6,7},{7,6},{8,9},{9,8},{10,11... | collective-permute-start | bytes 1966088 | tf_op jit(solution)/shard_map/ppermute | solution.py:245
  81.1 1.2 %collective-permute-start.14 = (f32[320]{0:T(512)S(1)}, f32[320]{0:T(512)S(1)}, u32[]{:S(2)}, u32[]{:S(2)}) collective-permute-start(f32[320]{0:T(512)S(1)} %multiply_reduce_fusion), channel_id=1, source_target_pairs={{0,1},{1,0},{2,3},{3,2},{4,5},{5,4},{6,7},{7,6},{8,9},{9,8},{10,11... | collective-permute-start | bytes 3848 | tf_op jit(solution)/shard_map/ppermute | solution.py:245
  82.4 4.8 %collective-permute-start.16 = (f32[320]{0:T(512)S(1)}, f32[320]{0:T(512)S(1)}, u32[]{:S(2)}, u32[]{:S(2)}) collective-permute-start(f32[320]{0:T(512)S(1)} %add.235), channel_id=1, source_target_pairs={{0,2},{1,7},{2,4},{3,1},{4,6},{5,3},{6,0},{7,5},{8,10},{9,15},{10,... | collective-permute-start | bytes 3848 | tf_op jit(solution)/shard_map/ppermute | solution.py:235
  82.6 5.2 %collective-permute-start.15 = (f32[320]{0:T(512)S(1)}, f32[320]{0:T(512)S(1)}, u32[]{:S(2)}, u32[]{:S(2)}) collective-permute-start(f32[320]{0:T(512)S(1)} %add.235), channel_id=1, source_target_pairs={{0,4},{1,5},{2,6},{3,7},{4,0},{5,1},{6,2},{7,3},{8,12},{9,13},{10,... | collective-permute-start | bytes 3848 | tf_op jit(solution)/shard_map/ppermute | solution.py:230
  87.2 1.2 %collective-permute-start.17 = (f32[320]{0:T(512)S(1)}, f32[320]{0:T(512)S(1)}, u32[]{:S(2)}, u32[]{:S(2)}) collective-permute-start(f32[320]{0:T(512)S(1)} %collective-permute-done.16), channel_id=1, source_target_pairs={{0,1},{1,0},{2,3},{3,2},{4,5},{5,4},{6,7},{7,6},{8,9},{9,8},{10,11... | collective-permute-start | bytes 3848 | tf_op jit(solution)/shard_map/ppermute | solution.py:245

commit v5 on v4

--- a/solution.py
+++ b/solution.py
@@ -128,7 +128,7 @@
         ),
     )(
         blocks,
-        lengths,
+        in_hbm(lengths),
         in_hbm(query),
         in_hbm(token_keys),
         in_hbm(token_values),
@@ -332,7 +332,8 @@
         mixed, [[cross_got], [cross]], proj_columns, blocks((ahead, 0), (-ahead, 1))
     )
     beyond, mixed = lax.optimization_barrier((beyond, mixed))
-    mixed = talker_product(mixed, [[swap(beyond)], [beyond]], proj_columns, blocks((2, 1), (2, 0)))
+    mixed = talker_product(mixed, [[beyond]], proj_columns, blocks((2, 0)))
+    mixed = talker_product(mixed, [[swap(beyond)]], proj_columns, blocks((2, 1)))
 
     squares = jnp.sum(mixed * mixed, -1)
     squares = squares + swap(squares)

time: 112 us -> 110 us (0.982)
    pallas_call x4 -> x5, Pallas kernels: 5.61 us -> 5.27 us  [talker_product(): pl.pallas_call(body, in_specs=[pl.BlockSpec(memory_space=pltpu.SMEM), vme...]
  transfers between devices with their start and end apart: 18 -> 18, of which waited for: 13 -> 13; matrix products, arithmetic and copies ran while one was open for 2% -> 2% of each run, Pallas kernels for 10% -> 11%
where the time goes in v5:
time: 110 us
  waiting for transfers between devices  51.5 us (47%)
  Pallas kernels  23.2 us (21%)
  blocking collectives  20.8 us (19%)
  starting transfers between devices  7.77 us (7%)
  other arithmetic  3.57 us (3%)
  matrix products  1.71 us (2%)
    ppermute x5, waiting for transfers between devices, onward(): lax.ppermute(x, 'mp', [(i, (i + 2 - 4 * (i % 2)) % count) for i in range(...  38 us
    all_to_all x1, blocking collectives, local(): lax.all_to_all(sent.reshape(n_dp, slots // n_dp, -1), 'dp', 0, 0, tiled=T...  20.8 us
    pallas_call x1, Pallas kernels, attend_and_project(): pl.pallas_call(body, grid_spec=pltpu.PrefetchScalarGridSpec(num_scalar_pr...  10.7 us
    ppermute x2, waiting for transfers between devices, across(): return lax.ppermute(x, 'mp', moves)  7.69 us
    pallas_call x1, Pallas kernels, head_product(): pl.pallas_call(body, in_specs=[pl.BlockSpec(memory_space=pltpu.SMEM), pl....  7.27 us
    ppermute x10, waiting for transfers between devices, swap(): lax.ppermute(x, 'mp', [(i, i ^ 1) for i in range(lax.axis_size('mp'))])  5.55 us
    pallas_call x5, Pallas kernels, talker_product(): pl.pallas_call(body, in_specs=[pl.BlockSpec(memory_space=pltpu.SMEM), vme...  5.27 us
    ppermute x5, starting transfers between devices, onward(): lax.ppermute(x, 'mp', [(i, (i + 2 - 4 * (i % 2)) % count) for i in range(...  3.09 us
  transfers between devices with their start and end apart: 18, of which 13 were waited for; matrix products, arithmetic and copies ran while one was open for 2% of the time, Pallas kernels for 11%

profile of v5, /device:TPU:0, one launch (start us, length us, event | category | flops | bytes accessed | tf_op | source)
XLA Modules:
  0.0 110.0 jit_solution(5336638700989798285)
XLA Ops:
  0.7 0.1 pad_add_fusion.blocks_ref
  0.7 10.7 %shard_map.131 = (bf16[320,1024]{1,0:T(8,128)(2,1)S(1)}, bf16[320,1024]{1,0:T(8,128)(2,1)S(1)}, bf16[320,1024]{1,0:T(8,128)(2,1)S(1)}) custom-call(s32[2]{0:T(128)S(1)} %pad_add_fusion.blocks_ref, s32[80]{0:T(128)} %len_ref.1, bf16[4,80,1024]{2,1,0:T(8,128)(2,1)} %q_ref.1, bf16[4,80,128]{2,1,0:T(8,128)(2,1)} %tk_ref.1, bf16[4,80,128]{2,1,0:T(8,128)(2,1)} %tv_ref.1, ...), custom_call_target="tpu_custom_call" | custom-call | flops 1342177280 | bytes 33554432 | tf_op jit(solution)/shard_map/pallas_call | solution.py:103
  11.5 0.1 collective-permute-start
  11.6 0.1 stack.53.blocks_ref
  11.7 1.9 %collective-permute-done = bf16[320,1024]{1,0:T(8,128)(2,1)S(1)} collective-permute-done((bf16[320,1024]{1,0:T(8,128)(2,1)S(1)}, bf16[320,1024]{1,0:T(8,128)(2,1)S(1)}, u32[]{:S(2)}, u32[]{:S(2)}) %collective-permute-start) | collective-permute-done | bytes 655392 | tf_op jit(solution)/shard_map/ppermute | solution.py:245
  13.6 0.2 add_convert_fusion.3
  13.9 0.0 slice-start.1
  13.9 1.7 %collective-permute-start.1 = (bf16[320,1024]{1,0:T(8,128)(2,1)S(1)}, bf16[320,1024]{1,0:T(8,128)(2,1)S(1)}, u32[]{:S(2)}, u32[]{:S(2)}) collective-permute-start(bf16[320,1024]{1,0:T(8,128)(2,1)S(1)} %add_convert_fusion.3), channel_id=1, source_target_pairs={{0,2},{1,7},{2,4},{3,1},{4,6},{5,3},{6,0},{7,5},{8,10},{9,15},{10,... | collective-permute-start | bytes 1966088 | tf_op jit(solution)/shard_map/ppermute | solution.py:235
  15.6 7.3 %shard_map.132 = (bf16[320,1024]{1,0:T(8,128)(2,1)S(1)}, bf16[320,1024]{1,0:T(8,128)(2,1)S(1)}, bf16[320,1024]{1,0:T(8,128)(2,1)S(1)}, bf16[320,1024]{1,0:T(8,12...) custom-call(s32[6]{0:T(128)S(1)} %stack.53.blocks_ref, ...), custom_call_target="tpu_custom_call" | custom-call | flops 4026531840 | bytes 16515072 | tf_op jit(solution)/shard_map/pallas_call | solution.py:159
  22.9 1.4 %collective-permute-start.3 = (bf16[320,1024]{1,0:T(8,128)(2,1)S(1)}, bf16[320,1024]{1,0:T(8,128)(2,1)S(1)}, u32[]{:S(2)}, u32[]{:S(2)}) collective-permute-start(bf16[320,1024]{1,0:T(8,128)(2,1)S(1)} %get-tuple-element.26), channel_id=1, source_target_pairs={{0,1},{1,0},{2,3},{3,2},{4,5},{5,4},{6,7},{7,6},{8,9},{9,8},{10,11... | collective-permute-start | bytes 1966088 | tf_op jit(solution)/shard_map/ppermute | solution.py:245
  24.3 0.1 collective-permute-start.5
  24.4 1.4 %collective-permute-done.1 = bf16[320,1024]{1,0:T(8,128)(2,1)S(1)} collective-permute-done((bf16[320,1024]{1,0:T(8,128)(2,1)S(1)}, bf16[320,1024]{1,0:T(8,128)(2,1)S(1)}, u32[]{:S(2)}, u32[]{:S(2)}) %collective-permute-start.1) | collective-permute-done | bytes 655392 | tf_op jit(solution)/shard_map/ppermute | solution.py:235
  25.8 0.0 collective-permute-start.2
  25.8 0.2 collective-permute-done.3
  26.0 0.2 add_convert_fusion.2
  26.2 0.5 collective-permute-start.4
  26.7 0.2 collective-permute-done.5
  26.9 0.3 add_convert_fusion.1
  27.3 1.4 %collective-permute-start.6 = (bf16[320,1024]{1,0:T(8,128)(2,1)S(1)}, bf16[320,1024]{1,0:T(8,128)(2,1)S(1)}, u32[]{:S(2)}, u32[]{:S(2)}) collective-permute-start(bf16[320,1024]{1,0:T(8,128)(2,1)S(1)} %add_convert_fusion.1), channel_id=1, source_target_pairs={{0,2},{1,7},{2,4},{3,1},{4,6},{5,3},{6,0},{7,5},{8,10},{9,15},{10,... | collective-permute-start | bytes 1966088 | tf_op jit(solution)/shard_map/ppermute | solution.py:235
  28.6 0.0 collective-permute-done.2
  28.6 7.7 %collective-permute-done.4 = bf16[320,1024]{1,0:T(8,128)(2,1)S(1)} collective-permute-done((bf16[320,1024]{1,0:T(8,128)(2,1)S(1)}, bf16[320,1024]{1,0:T(8,128)(2,1)S(1)}, u32[]{:S(2)}, u32[]{:S(2)}) %collective-permute-start.4) | collective-permute-done | bytes 655392 | tf_op jit(solution)/shard_map/ppermute | solution.py:241
  36.3 0.5 fusion.1
  36.8 8.3 %collective-permute-done.6 = bf16[320,1024]{1,0:T(8,128)(2,1)S(1)} collective-permute-done((bf16[320,1024]{1,0:T(8,128)(2,1)S(1)}, bf16[320,1024]{1,0:T(8,128)(2,1)S(1)}, u32[]{:S(2)}, u32[]{:S(2)}) %collective-permute-start.6) | collective-permute-done | bytes 655392 | tf_op jit(solution)/shard_map/ppermute | solution.py:235
  45.1 1.2 %bitcast_add_fusion = (bf16[320,1024]{1,0:T(8,128)(2,1)S(1)}, bf16[320,1024]{1,0:T(8,128)(2,1)}) fusion(bf16[4,80,1024]{2,1,0:T(8,128)(2,1)S(1)} %copy-done.1, f32[320,1024]{1,0:T(8,128)S(1)} %fusion.1, bf16[320,1024]{1,0:T(8,128)(2,1)S(1)} %collective-permute-done.6), kind=kLoop, calls=%fused_computation.12 | loop fusion | flops 1310720 | bytes 3932160 | tf_op jit(solution)/shard_map/add | solution.py:318
  46.4 0.0 collective-permute-start.7
  46.4 0.7 collective-permute-start.9
  47.1 0.1 collective-permute-start.12
  47.2 17.4 %collective-permute-done.7.refs_1_ = bf16[320,1024]{1,0:T(8,128)(2,1)S(1)} collective-permute-done((bf16[320,1024]{1,0:T(8,128)(2,1)S(1)}, bf16[320,1024]{1,0:T(8,128)(2,1)S(1)}, u32[]{:S(2)}, u32[]{:S(2)}) %collective-permute-start.7) | collective-permute-done | bytes 655392 | tf_op jit(solution)/shard_map/ppermute | solution.py:235
  64.6 0.0 collective-permute-start.11
  64.6 0.0 collective-permute-done.9.refs_1_
  64.7 0.5 collective-permute-start.10
  65.2 0.0 collective-permute-start.8
  65.2 0.1 pad_add_fusion.3.blocks_ref
  65.2 0.1 pad_add_fusion.2.blocks_ref
  65.3 0.1 pad_add_fusion.1.blocks_ref
  65.4 0.0 collective-permute-done.12.refs_0_
  65.4 1.4 %shard_map.133.refs_2_ = f32[320,448]{1,0:T(8,128)S(1)} custom-call(s32[2]{0:T(128)S(1)} %pad_add_fusion.3.blocks_ref, bf16[448,8192]{1,0:T(8,128)(2,1)S(1)} %bitcast.22, bf16[320,1024]{1,0:T(8,128)(2,1)S(1)} %collective-permute-done.12.refs_0_, bf16[320,1024]{1,0:T(8,128)(2,1)S(1)} %get-tuple-element.32.refs_1_), custom_call_target="tpu_custom_call" | custom-call | flops 587202560 | bytes 3145728 | tf_op jit(solution)/shard_map/pallas_call | solution.py:210
  66.8 0.0 collective-permute-done.11.refs_0_
  66.8 1.4 %shard_map.134.refs_2_ = f32[320,448]{1,0:T(8,128)S(1)} custom-call(s32[2]{0:T(128)S(1)} %pad_add_fusion.2.blocks_ref, bf16[448,8192]{1,0:T(8,128)(2,1)S(1)} %bitcast.23, bf16[320,1024]{1,0:T(8,128)(2,1)S(1)} %collective-permute-done.11.refs_0_, bf16[320,1024]{1,0:T(8,128)(2,1)S(1)} %collective-permute-done.7.refs_1_, f32[320,448]{1,0:T(8,128)S(1)} %shard_map.133.refs_2_), custom_call_target="tpu_custom_call" | custom-call | flops 587202560 | bytes 3145728 | tf_op jit(solution)/shard_map/pallas_call | solution.py:210
  68.2 0.0 collective-permute-done.10.refs_0_
  68.3 1.4 %shard_map.135.refs_1_ = f32[320,448]{1,0:T(8,128)S(1)} custom-call(s32[2]{0:T(128)S(1)} %pad_add_fusion.1.blocks_ref, bf16[448,8192]{1,0:T(8,128)(2,1)S(1)} %bitcast.24, bf16[320,1024]{1,0:T(8,128)(2,1)S(1)} %collective-permute-done.10.refs_0_, bf16[320,1024]{1,0:T(8,128)(2,1)S(1)} %collective-permute-done.9.refs_1_, f32[320,448]{1,0:T(8,128)S(1)} %shard_map.134.refs_2_), custom_call_target="tpu_custom_call" | custom-call | flops 587202560 | bytes 3145728 | tf_op jit(solution)/shard_map/pallas_call | solution.py:210
  69.7 7.3 %collective-permute-done.8.refs_0_ = bf16[320,1024]{1,0:T(8,128)(2,1)S(1)} collective-permute-done((bf16[320,1024]{1,0:T(8,128)(2,1)S(1)}, bf16[320,1024]{1,0:T(8,128)(2,1)S(1)}, u32[]{:S(2)}, u32[]{:S(2)}) %collective-permute-start.8) | collective-permute-done | bytes 655392 | tf_op jit(solution)/shard_map/ppermute | solution.py:235
  77.0 0.5 shard_map.136.refs_1_
  77.5 0.0 copy-start.3
  77.5 0.0 copy-start.2
  77.5 1.5 %collective-permute-done.13.refs_0_ = bf16[320,1024]{1,0:T(8,128)(2,1)S(1)} collective-permute-done((bf16[320,1024]{1,0:T(8,128)(2,1)S(1)}, bf16[320,1024]{1,0:T(8,128)(2,1)S(1)}, u32[]{:S(2)}, u32[]{:S(2)}) %collective-permute-start.13) | collective-permute-done | bytes 655392 | tf_op jit(solution)/shard_map/ppermute | solution.py:245
  79.1 0.5 shard_map.137
  79.6 0.1 multiply_reduce_fusion
  79.7 0.2 collective-permute-start.14
  80.0 1.0 collective-permute-done.14
  81.0 0.2 convert_reduce_fusion
  81.2 1.1 collective-permute-start.15
  82.2 3.5 %collective-permute-done.16 = f32[320]{0:T(512)S(1)} collective-permute-done((f32[320]{0:T(512)S(1)}, f32[320]{0:T(512)S(1)}, u32[]{:S(2)}, u32[]{:S(2)}) %collective-permute-start.16) | collective-permute-done | bytes 1312 | tf_op jit(solution)/shard_map/ppermute | solution.py:235
  85.8 0.0 collective-permute-start.17
  85.8 0.1 add.233
  85.9 0.1 broadcast_in_dim.7
  86.0 0.3 collective-permute-done.15
  86.3 0.6 collective-permute-done.17
  86.9 0.1 multiply_convert_fusion
  87.1 0.1 broadcast_in_dim.8
  87.2 0.6 fusion.2
  87.7 20.8 %all_to_all.5 = bf16[16,40,512]{2,1,0:T(8,128)(2,1)S(1)} all-to-all(bf16[16,40,512]{2,1,0:T(8,128)(2,1)S(1)} %bitcast.31), channel_id=1, replica_groups=mesh['dp'=16,'mp'=8] {'dp'}, dimensions={0} | all-to-all | bytes 1310720 | tf_op jit(solution)/shard_map/all_to_all | solution.py:362
  108.5 0.2 add_reduce_fusion
  108.8 1.2 %fusion.3 = bf16[320,448]{1,0:T(8,128)(2,1)} fusion(bf16[640,512]{1,0:T(8,128)(2,1)S(1)} %bitcast.30, s32[640]{0:T(1024)S(1)} %fusion.14), kind=kOutput, calls=%fused_computation.10 | convolution fusion | flops 183705600 | bytes 944640 | tf_op jit(solution)/shard_map/dot_general | solution.py:369
  (19 shorter events, 0.1 us)
Async XLA Ops:
  11.5 2.2 %collective-permute-start = (bf16[320,1024]{1,0:T(8,128)(2,1)S(1)}, bf16[320,1024]{1,0:T(8,128)(2,1)S(1)}, u32[]{:S(2)}, u32[]{:S(2)}) collective-permute-start(bf16[320,1024]{1,0:T(8,128)(2,1)S(1)} %get-tuple-element.18), channel_id=1, source_target_pairs={{0,1},{1,0},{2,3},{3,2},{4,5},{5,4},{6,7},{7,6},{8,9},{9,8},{10,11... | collective-permute-start | bytes 1966088 | tf_op jit(solution)/shard_map/ppermute | solution.py:245
  13.6 51.8 %slice-start = ((s8[7340032]{0:T(1024)(128)(4,1)}), s8[4194304]{0:T(1024)(128)(4,1)S(1)}, s32[]{:S(2)}) async-start(s8[7340032]{0:T(1024)(128)(4,1)} %bitcast.20), calls=%async_computation.1 | async-start | bytes 8388608
  13.9 51.5 %slice-start.1 = ((s8[7340032]{0:T(1024)(128)(4,1)}), s8[3145728]{0:T(1024)(128)(4,1)S(1)}, s32[]{:S(2)}) async-start(s8[7340032]{0:T(1024)(128)(4,1)} %bitcast.20), calls=%async_computation.2 | async-start | bytes 6291456
  13.9 11.9 %collective-permute-start.1 = (bf16[320,1024]{1,0:T(8,128)(2,1)S(1)}, bf16[320,1024]{1,0:T(8,128)(2,1)S(1)}, u32[]{:S(2)}, u32[]{:S(2)}) collective-permute-start(bf16[320,1024]{1,0:T(8,128)(2,1)S(1)} %add_convert_fusion.3), channel_id=1, source_target_pairs={{0,2},{1,7},{2,4},{3,1},{4,6},{5,3},{6,0},{7,5},{8,10},{9,15},{10,... | collective-permute-start | bytes 1966088 | tf_op jit(solution)/shard_map/ppermute | solution.py:235
  22.9 3.1 %collective-permute-start.3 = (bf16[320,1024]{1,0:T(8,128)(2,1)S(1)}, bf16[320,1024]{1,0:T(8,128)(2,1)S(1)}, u32[]{:S(2)}, u32[]{:S(2)}) collective-permute-start(bf16[320,1024]{1,0:T(8,128)(2,1)S(1)} %get-tuple-element.26), channel_id=1, source_target_pairs={{0,1},{1,0},{2,3},{3,2},{4,5},{5,4},{6,7},{7,6},{8,9},{9,8},{10,11... | collective-permute-start | bytes 1966088 | tf_op jit(solution)/shard_map/ppermute | solution.py:245
  24.3 2.7 %collective-permute-start.5 = (bf16[320,1024]{1,0:T(8,128)(2,1)S(1)}, bf16[320,1024]{1,0:T(8,128)(2,1)S(1)}, u32[]{:S(2)}, u32[]{:S(2)}) collective-permute-start(bf16[320,1024]{1,0:T(8,128)(2,1)S(1)} %get-tuple-element.28), channel_id=1, source_target_pairs={{0,1},{1,0},{2,3},{3,2},{4,5},{5,4},{6,7},{7,6},{8,9},{9,8},{10,11... | collective-permute-start | bytes 1966088 | tf_op jit(solution)/shard_map/ppermute | solution.py:245
  25.8 2.9 %collective-permute-start.2 = (bf16[320,1024]{1,0:T(8,128)(2,1)S(1)}, bf16[320,1024]{1,0:T(8,128)(2,1)S(1)}, u32[]{:S(2)}, u32[]{:S(2)}) collective-permute-start(bf16[320,1024]{1,0:T(8,128)(2,1)S(1)} %get-tuple-element.24), channel_id=1, source_target_pairs={{0,1},{1,0},{2,3},{3,2},{4,5},{5,4},{6,7},{7,6},{8,9},{9,8},{10,11... | collective-permute-start | bytes 1966088 | tf_op jit(solution)/shard_map/ppermute | solution.py:245
  26.2 10.1 %collective-permute-start.4 = (bf16[320,1024]{1,0:T(8,128)(2,1)S(1)}, bf16[320,1024]{1,0:T(8,128)(2,1)S(1)}, u32[]{:S(2)}, u32[]{:S(2)}) collective-permute-start(bf16[320,1024]{1,0:T(8,128)(2,1)S(1)} %add_convert_fusion.2), channel_id=1, source_target_pairs={{0,3},{1,6},{2,5},{3,0},{4,7},{5,2},{6,1},{7,4},{8,11},{9,14},{10,... | collective-permute-start | bytes 1966088 | tf_op jit(solution)/shard_map/ppermute | solution.py:241
  26.9 9.4 %copy-start = (bf16[4,80,1024]{2,1,0:T(8,128)(2,1)S(1)}, bf16[4,80,1024]{2,1,0:T(8,128)(2,1)}, u32[]{:S(2)}) copy-start(bf16[4,80,1024]{2,1,0:T(8,128)(2,1)} %param.19) | copy-start | bytes 1966084
  27.3 17.8 %collective-permute-start.6 = (bf16[320,1024]{1,0:T(8,128)(2,1)S(1)}, bf16[320,1024]{1,0:T(8,128)(2,1)S(1)}, u32[]{:S(2)}, u32[]{:S(2)}) collective-permute-start(bf16[320,1024]{1,0:T(8,128)(2,1)S(1)} %add_convert_fusion.1), channel_id=1, source_target_pairs={{0,2},{1,7},{2,4},{3,1},{4,6},{5,3},{6,0},{7,5},{8,10},{9,15},{10,... | collective-permute-start | bytes 1966088 | tf_op jit(solution)/shard_map/ppermute | solution.py:235
  36.3 8.8 %copy-start.1 = (bf16[4,80,1024]{2,1,0:T(8,128)(2,1)S(1)}, bf16[4,80,1024]{2,1,0:T(8,128)(2,1)}, u32[]{:S(2)}) copy-start(bf16[4,80,1024]{2,1,0:T(8,128)(2,1)} %param.20) | copy-start | bytes 1966084
  46.4 18.3 %collective-permute-start.7 = (bf16[320,1024]{1,0:T(8,128)(2,1)S(1)}, bf16[320,1024]{1,0:T(8,128)(2,1)S(1)}, u32[]{:S(2)}, u32[]{:S(2)}) collective-permute-start(bf16[320,1024]{1,0:T(8,128)(2,1)S(1)} %get-tuple-element.32.refs_1_), channel_id=1, source_target_pairs={{0,2},{1,7},{2,4},{3,1},{4,6},{5,3},{6,0},{7,5},{8,10},{9,15},{10,... | collective-permute-start | bytes 1966088 | tf_op jit(solution)/shard_map/ppermute | solution.py:235
  46.4 18.3 %collective-permute-start.9 = (bf16[320,1024]{1,0:T(8,128)(2,1)S(1)}, bf16[320,1024]{1,0:T(8,128)(2,1)S(1)}, u32[]{:S(2)}, u32[]{:S(2)}) collective-permute-start(bf16[320,1024]{1,0:T(8,128)(2,1)S(1)} %get-tuple-element.32.refs_1_), channel_id=1, source_target_pairs={{0,7},{1,2},{2,1},{3,4},{4,3},{5,6},{6,5},{7,0},{8,15},{9,10},{10,... | collective-permute-start | bytes 1966088 | tf_op jit(solution)/shard_map/ppermute | solution.py:241
  47.1 18.3 %collective-permute-start.12 = (bf16[320,1024]{1,0:T(8,128)(2,1)S(1)}, bf16[320,1024]{1,0:T(8,128)(2,1)S(1)}, u32[]{:S(2)}, u32[]{:S(2)}) collective-permute-start(bf16[320,1024]{1,0:T(8,128)(2,1)S(1)} %get-tuple-element.32.refs_1_), channel_id=1, source_target_pairs={{0,1},{1,0},{2,3},{3,2},{4,5},{5,4},{6,7},{7,6},{8,9},{9,8},{10,11... | collective-permute-start | bytes 1966088 | tf_op jit(solution)/shard_map/ppermute | solution.py:245
  64.6 2.2 %collective-permute-start.11 = (bf16[320,1024]{1,0:T(8,128)(2,1)S(1)}, bf16[320,1024]{1,0:T(8,128)(2,1)S(1)}, u32[]{:S(2)}, u32[]{:S(2)}) collective-permute-start(bf16[320,1024]{1,0:T(8,128)(2,1)S(1)} %collective-permute-done.7.refs_1_), channel_id=1, source_target_pairs={{0,1},{1,0},{2,3},{3,2},{4,5},{5,4},{6,7},{7,6},{8,9},{9,8},{10,11... | collective-permute-start | bytes 1966088 | tf_op jit(solution)/shard_map/ppermute | solution.py:245
  64.7 3.6 %collective-permute-start.10 = (bf16[320,1024]{1,0:T(8,128)(2,1)S(1)}, bf16[320,1024]{1,0:T(8,128)(2,1)S(1)}, u32[]{:S(2)}, u32[]{:S(2)}) collective-permute-start(bf16[320,1024]{1,0:T(8,128)(2,1)S(1)} %collective-permute-done.9.refs_1_), channel_id=1, source_target_pairs={{0,1},{1,0},{2,3},{3,2},{4,5},{5,4},{6,7},{7,6},{8,9},{9,8},{10,11... | collective-permute-start | bytes 1966088 | tf_op jit(solution)/shard_map/ppermute | solution.py:245
  65.2 11.8 %collective-permute-start.8 = (bf16[320,1024]{1,0:T(8,128)(2,1)S(1)}, bf16[320,1024]{1,0:T(8,128)(2,1)S(1)}, u32[]{:S(2)}, u32[]{:S(2)}) collective-permute-start(bf16[320,1024]{1,0:T(8,128)(2,1)S(1)} %collective-permute-done.7.refs_1_), channel_id=1, source_target_pairs={{0,2},{1,7},{2,4},{3,1},{4,6},{5,3},{6,0},{7,5},{8,10},{9,15},{10,... | collective-permute-start | bytes 1966088 | tf_op jit(solution)/shard_map/ppermute | solution.py:235
  77.0 2.1 %collective-permute-start.13 = (bf16[320,1024]{1,0:T(8,128)(2,1)S(1)}, bf16[320,1024]{1,0:T(8,128)(2,1)S(1)}, u32[]{:S(2)}, u32[]{:S(2)}) collective-permute-start(bf16[320,1024]{1,0:T(8,128)(2,1)S(1)} %collective-permute-done.8.refs_0_), channel_id=1, source_target_pairs={{0,1},{1,0},{2,3},{3,2},{4,5},{5,4},{6,7},{7,6},{8,9},{9,8},{10,11... | collective-permute-start | bytes 1966088 | tf_op jit(solution)/shard_map/ppermute | solution.py:245
  77.5 2.5 %copy-start.3 = (s32[80]{0:T(128)S(1)}, s32[80]{0:T(128)}, u32[]{:S(2)}) copy-start(s32[80]{0:T(128)} %param.18) | copy-start | bytes 964
  77.5 8.3 %copy-start.2 = (bf16[448]{0:T(512)(128)(2,1)S(1)}, bf16[448]{0:T(512)(128)(2,1)}, u32[]{:S(2)}) copy-start(bf16[448]{0:T(512)(128)(2,1)} %param.23) | copy-start | bytes 2692
  79.7 1.2 %collective-permute-start.14 = (f32[320]{0:T(512)S(1)}, f32[320]{0:T(512)S(1)}, u32[]{:S(2)}, u32[]{:S(2)}) collective-permute-start(f32[320]{0:T(512)S(1)} %multiply_reduce_fusion), channel_id=1, source_target_pairs={{0,1},{1,0},{2,3},{3,2},{4,5},{5,4},{6,7},{7,6},{8,9},{9,8},{10,11... | collective-permute-start | bytes 3848 | tf_op jit(solution)/shard_map/ppermute | solution.py:245
  81.0 4.8 %collective-permute-start.16 = (f32[320]{0:T(512)S(1)}, f32[320]{0:T(512)S(1)}, u32[]{:S(2)}, u32[]{:S(2)}) collective-permute-start(f32[320]{0:T(512)S(1)} %add.235), channel_id=1, source_target_pairs={{0,2},{1,7},{2,4},{3,1},{4,6},{5,3},{6,0},{7,5},{8,10},{9,15},{10,... | collective-permute-start | bytes 3848 | tf_op jit(solution)/shard_map/ppermute | solution.py:235
  81.2 5.2 %collective-permute-start.15 = (f32[320]{0:T(512)S(1)}, f32[320]{0:T(512)S(1)}, u32[]{:S(2)}, u32[]{:S(2)}) collective-permute-start(f32[320]{0:T(512)S(1)} %add.235), channel_id=1, source_target_pairs={{0,4},{1,5},{2,6},{3,7},{4,0},{5,1},{6,2},{7,3},{8,12},{9,13},{10,... | collective-permute-start | bytes 3848 | tf_op jit(solution)/shard_map/ppermute | solution.py:230
  85.8 1.2 %collective-permute-start.17 = (f32[320]{0:T(512)S(1)}, f32[320]{0:T(512)S(1)}, u32[]{:S(2)}, u32[]{:S(2)}) collective-permute-start(f32[320]{0:T(512)S(1)} %collective-permute-done.16), channel_id=1, source_target_pairs={{0,1},{1,0},{2,3},{3,2},{4,5},{5,4},{6,7},{7,6},{8,9},{9,8},{10,11... | collective-permute-start | bytes 3848 | tf_op jit(solution)/shard_map/ppermute | solution.py:245

commit v6 on v5

--- a/solution.py
+++ b/solution.py
@@ -69,16 +69,18 @@
         recent = jnp.where(mine, recent, -1e30).reshape(streams, each, padded)
         highest = jnp.max(jnp.maximum(scores, recent), -1, keepdims=True)
         scores, recent = jnp.exp(scores - highest), jnp.exp(recent - highest)
-        total = jnp.sum(scores + recent, -1, keepdims=True)
-        share = 1.0 / total
-        weights = (scores * share).astype(jnp.bfloat16)
-        recent = (recent * share).astype(jnp.bfloat16).reshape(streams * each, padded)
+        scores = scores.astype(jnp.bfloat16)
+        recent = recent.astype(jnp.bfloat16).reshape(streams * each, padded)
         context = lax.dot_general(
-            weights, v_ref[...], (((2,), (1,)), ((0,), (0,))), preferred_element_type=jnp.float32
+            scores, v_ref[...], (((2,), (1,)), ((0,), (0,))), preferred_element_type=jnp.float32
         ).reshape(streams * each, head_dim)
-        context += jnp.dot(
-            recent, values, preferred_element_type=jnp.float32
+        context += jnp.dot(recent, values, preferred_element_type=jnp.float32)
+        ones = jnp.ones((padded, head_dim), jnp.bfloat16)
+        total = jnp.dot(recent, ones, preferred_element_type=jnp.float32)
+        total += jnp.dot(
+            scores.reshape(streams * each, slot_count), ones, preferred_element_type=jnp.float32
         )
+        context /= total
         context = jnp.swapaxes(context.reshape(streams, step_count, groups, head_dim), 0, 1)
         context = context.reshape(step_count, streams, cols).astype(jnp.bfloat16)
         for t in range(step_count):

time: 110 us -> 110 us (level)
  no operation moved by 1% of the time
where the time goes in v6:
time: 110 us; the launch traced here: 109 us
  waiting for transfers between devices  51.5 us (47%)
  Pallas kernels  22.7 us (21%)
  blocking collectives  20.8 us (19%)
  starting transfers between devices  7.79 us (7%)
  other arithmetic  3.57 us (3%)
  matrix products  1.71 us (2%)
    ppermute x5, waiting for transfers between devices, onward(): lax.ppermute(x, 'mp', [(i, (i + 2 - 4 * (i % 2)) % count) for i in range(...  38 us
    all_to_all x1, blocking collectives, local(): lax.all_to_all(sent.reshape(n_dp, slots // n_dp, -1), 'dp', 0, 0, tiled=T...  20.8 us
    pallas_call x1, Pallas kernels, attend_and_project(): pl.pallas_call(body, grid_spec=pltpu.PrefetchScalarGridSpec(num_scalar_pr...  10.2 us
    ppermute x2, waiting for transfers between devices, across(): return lax.ppermute(x, 'mp', moves)  7.69 us
    pallas_call x1, Pallas kernels, head_product(): pl.pallas_call(body, in_specs=[pl.BlockSpec(memory_space=pltpu.SMEM), pl....  7.27 us
    ppermute x10, waiting for transfers between devices, swap(): lax.ppermute(x, 'mp', [(i, i ^ 1) for i in range(lax.axis_size('mp'))])  5.53 us
    pallas_call x5, Pallas kernels, talker_product(): pl.pallas_call(body, in_specs=[pl.BlockSpec(memory_space=pltpu.SMEM), vme...  5.27 us
    ppermute x5, starting transfers between devices, onward(): lax.ppermute(x, 'mp', [(i, (i + 2 - 4 * (i % 2)) % count) for i in range(...  3.1 us
  transfers between devices with their start and end apart: 18, of which 13 were waited for; matrix products, arithmetic and copies ran while one was open for 2% of the time, Pallas kernels for 11%

profile of v6, /device:TPU:0, one launch (start us, length us, event | category | flops | bytes accessed | tf_op | source)
XLA Modules:
  0.0 109.4 jit_solution(10727902395051077542)
XLA Ops:
  0.7 0.1 pad_add_fusion.blocks_ref
  0.7 10.2 %shard_map.131 = (bf16[320,1024]{1,0:T(8,128)(2,1)S(1)}, bf16[320,1024]{1,0:T(8,128)(2,1)S(1)}, bf16[320,1024]{1,0:T(8,128)(2,1)S(1)}) custom-call(s32[2]{0:T(128)S(1)} %pad_add_fusion.blocks_ref, s32[80]{0:T(128)} %len_ref.1, bf16[4,80,1024]{2,1,0:T(8,128)(2,1)} %q_ref.1, bf16[4,80,128]{2,1,0:T(8,128)(2,1)} %tk_ref.1, bf16[4,80,128]{2,1,0:T(8,128)(2,1)} %tv_ref.1, ...), custom_call_target="tpu_custom_call" | custom-call | flops 1342177280 | bytes 33554432 | tf_op jit(solution)/shard_map/pallas_call | solution.py:105
  10.9 0.1 collective-permute-start
  11.1 0.1 stack.53.blocks_ref
  11.2 1.9 %collective-permute-done = bf16[320,1024]{1,0:T(8,128)(2,1)S(1)} collective-permute-done((bf16[320,1024]{1,0:T(8,128)(2,1)S(1)}, bf16[320,1024]{1,0:T(8,128)(2,1)S(1)}, u32[]{:S(2)}, u32[]{:S(2)}) %collective-permute-start) | collective-permute-done | bytes 655392 | tf_op jit(solution)/shard_map/ppermute | solution.py:247
  13.1 0.2 add_convert_fusion.3
  13.3 0.0 slice-start.1
  13.3 1.7 %collective-permute-start.1 = (bf16[320,1024]{1,0:T(8,128)(2,1)S(1)}, bf16[320,1024]{1,0:T(8,128)(2,1)S(1)}, u32[]{:S(2)}, u32[]{:S(2)}) collective-permute-start(bf16[320,1024]{1,0:T(8,128)(2,1)S(1)} %add_convert_fusion.3), channel_id=1, source_target_pairs={{0,2},{1,7},{2,4},{3,1},{4,6},{5,3},{6,0},{7,5},{8,10},{9,15},{10,... | collective-permute-start | bytes 1966088 | tf_op jit(solution)/shard_map/ppermute | solution.py:237
  15.1 7.3 %shard_map.132 = (bf16[320,1024]{1,0:T(8,128)(2,1)S(1)}, bf16[320,1024]{1,0:T(8,128)(2,1)S(1)}, bf16[320,1024]{1,0:T(8,128)(2,1)S(1)}, bf16[320,1024]{1,0:T(8,12...) custom-call(s32[6]{0:T(128)S(1)} %stack.53.blocks_ref, ...), custom_call_target="tpu_custom_call" | custom-call | flops 4026531840 | bytes 16515072 | tf_op jit(solution)/shard_map/pallas_call | solution.py:161
  22.4 1.4 %collective-permute-start.3 = (bf16[320,1024]{1,0:T(8,128)(2,1)S(1)}, bf16[320,1024]{1,0:T(8,128)(2,1)S(1)}, u32[]{:S(2)}, u32[]{:S(2)}) collective-permute-start(bf16[320,1024]{1,0:T(8,128)(2,1)S(1)} %get-tuple-element.26), channel_id=1, source_target_pairs={{0,1},{1,0},{2,3},{3,2},{4,5},{5,4},{6,7},{7,6},{8,9},{9,8},{10,11... | collective-permute-start | bytes 1966088 | tf_op jit(solution)/shard_map/ppermute | solution.py:247
  23.7 0.1 collective-permute-start.5
  23.8 1.4 %collective-permute-done.1 = bf16[320,1024]{1,0:T(8,128)(2,1)S(1)} collective-permute-done((bf16[320,1024]{1,0:T(8,128)(2,1)S(1)}, bf16[320,1024]{1,0:T(8,128)(2,1)S(1)}, u32[]{:S(2)}, u32[]{:S(2)}) %collective-permute-start.1) | collective-permute-done | bytes 655392 | tf_op jit(solution)/shard_map/ppermute | solution.py:237
  25.2 0.0 collective-permute-start.2
  25.2 0.2 collective-permute-done.3
  25.5 0.2 add_convert_fusion.2
  25.7 0.5 collective-permute-start.4
  26.2 0.2 collective-permute-done.5
  26.4 0.3 add_convert_fusion.1
  26.7 1.4 %collective-permute-start.6 = (bf16[320,1024]{1,0:T(8,128)(2,1)S(1)}, bf16[320,1024]{1,0:T(8,128)(2,1)S(1)}, u32[]{:S(2)}, u32[]{:S(2)}) collective-permute-start(bf16[320,1024]{1,0:T(8,128)(2,1)S(1)} %add_convert_fusion.1), channel_id=1, source_target_pairs={{0,2},{1,7},{2,4},{3,1},{4,6},{5,3},{6,0},{7,5},{8,10},{9,15},{10,... | collective-permute-start | bytes 1966088 | tf_op jit(solution)/shard_map/ppermute | solution.py:237
  28.1 0.0 collective-permute-done.2
  28.1 7.7 %collective-permute-done.4 = bf16[320,1024]{1,0:T(8,128)(2,1)S(1)} collective-permute-done((bf16[320,1024]{1,0:T(8,128)(2,1)S(1)}, bf16[320,1024]{1,0:T(8,128)(2,1)S(1)}, u32[]{:S(2)}, u32[]{:S(2)}) %collective-permute-start.4) | collective-permute-done | bytes 655392 | tf_op jit(solution)/shard_map/ppermute | solution.py:243
  35.8 0.5 fusion.1
  36.3 8.3 %collective-permute-done.6 = bf16[320,1024]{1,0:T(8,128)(2,1)S(1)} collective-permute-done((bf16[320,1024]{1,0:T(8,128)(2,1)S(1)}, bf16[320,1024]{1,0:T(8,128)(2,1)S(1)}, u32[]{:S(2)}, u32[]{:S(2)}) %collective-permute-start.6) | collective-permute-done | bytes 655392 | tf_op jit(solution)/shard_map/ppermute | solution.py:237
  44.6 1.2 %bitcast_add_fusion = (bf16[320,1024]{1,0:T(8,128)(2,1)S(1)}, bf16[320,1024]{1,0:T(8,128)(2,1)}) fusion(bf16[4,80,1024]{2,1,0:T(8,128)(2,1)S(1)} %copy-done.1, f32[320,1024]{1,0:T(8,128)S(1)} %fusion.1, bf16[320,1024]{1,0:T(8,128)(2,1)S(1)} %collective-permute-done.6), kind=kLoop, calls=%fused_computation.12 | loop fusion | flops 1310720 | bytes 3932160 | tf_op jit(solution)/shard_map/add | solution.py:320
  45.8 0.0 collective-permute-start.7
  45.8 0.8 collective-permute-start.9
  46.6 0.1 collective-permute-start.12
  46.7 17.4 %collective-permute-done.7.refs_1_ = bf16[320,1024]{1,0:T(8,128)(2,1)S(1)} collective-permute-done((bf16[320,1024]{1,0:T(8,128)(2,1)S(1)}, bf16[320,1024]{1,0:T(8,128)(2,1)S(1)}, u32[]{:S(2)}, u32[]{:S(2)}) %collective-permute-start.7) | collective-permute-done | bytes 655392 | tf_op jit(solution)/shard_map/ppermute | solution.py:237
  64.1 0.0 collective-permute-start.11
  64.1 0.0 collective-permute-done.9.refs_1_
  64.1 0.5 collective-permute-start.10
  64.6 0.0 collective-permute-start.8
  64.6 0.1 pad_add_fusion.3.blocks_ref
  64.7 0.1 pad_add_fusion.2.blocks_ref
  64.8 0.1 pad_add_fusion.1.blocks_ref
  64.8 0.0 collective-permute-done.12.refs_0_
  64.9 1.4 %shard_map.133.refs_2_ = f32[320,448]{1,0:T(8,128)S(1)} custom-call(s32[2]{0:T(128)S(1)} %pad_add_fusion.3.blocks_ref, bf16[448,8192]{1,0:T(8,128)(2,1)S(1)} %bitcast.22, bf16[320,1024]{1,0:T(8,128)(2,1)S(1)} %collective-permute-done.12.refs_0_, bf16[320,1024]{1,0:T(8,128)(2,1)S(1)} %get-tuple-element.32.refs_1_), custom_call_target="tpu_custom_call" | custom-call | flops 587202560 | bytes 3145728 | tf_op jit(solution)/shard_map/pallas_call | solution.py:212
  66.3 1.4 %shard_map.134.refs_2_ = f32[320,448]{1,0:T(8,128)S(1)} custom-call(s32[2]{0:T(128)S(1)} %pad_add_fusion.2.blocks_ref, bf16[448,8192]{1,0:T(8,128)(2,1)S(1)} %bitcast.23, bf16[320,1024]{1,0:T(8,128)(2,1)S(1)} %collective-permute-done.11.refs_0_, bf16[320,1024]{1,0:T(8,128)(2,1)S(1)} %collective-permute-done.7.refs_1_, f32[320,448]{1,0:T(8,128)S(1)} %shard_map.133.refs_2_), custom_call_target="tpu_custom_call" | custom-call | flops 587202560 | bytes 3145728 | tf_op jit(solution)/shard_map/pallas_call | solution.py:212
  67.7 1.4 %shard_map.135.refs_1_ = f32[320,448]{1,0:T(8,128)S(1)} custom-call(s32[2]{0:T(128)S(1)} %pad_add_fusion.1.blocks_ref, bf16[448,8192]{1,0:T(8,128)(2,1)S(1)} %bitcast.24, bf16[320,1024]{1,0:T(8,128)(2,1)S(1)} %collective-permute-done.10.refs_0_, bf16[320,1024]{1,0:T(8,128)(2,1)S(1)} %collective-permute-done.9.refs_1_, f32[320,448]{1,0:T(8,128)S(1)} %shard_map.134.refs_2_), custom_call_target="tpu_custom_call" | custom-call | flops 587202560 | bytes 3145728 | tf_op jit(solution)/shard_map/pallas_call | solution.py:212
  69.1 7.3 %collective-permute-done.8.refs_0_ = bf16[320,1024]{1,0:T(8,128)(2,1)S(1)} collective-permute-done((bf16[320,1024]{1,0:T(8,128)(2,1)S(1)}, bf16[320,1024]{1,0:T(8,128)(2,1)S(1)}, u32[]{:S(2)}, u32[]{:S(2)}) %collective-permute-start.8) | collective-permute-done | bytes 655392 | tf_op jit(solution)/shard_map/ppermute | solution.py:237
  76.4 0.0 collective-permute-start.13
  76.4 0.5 shard_map.136.refs_1_
  77.0 0.0 copy-start.3
  77.0 0.0 copy-start.2
  77.0 1.5 %collective-permute-done.13.refs_0_ = bf16[320,1024]{1,0:T(8,128)(2,1)S(1)} collective-permute-done((bf16[320,1024]{1,0:T(8,128)(2,1)S(1)}, bf16[320,1024]{1,0:T(8,128)(2,1)S(1)}, u32[]{:S(2)}, u32[]{:S(2)}) %collective-permute-start.13) | collective-permute-done | bytes 655392 | tf_op jit(solution)/shard_map/ppermute | solution.py:247
  78.5 0.5 shard_map.137
  79.0 0.1 multiply_reduce_fusion
  79.2 0.2 collective-permute-start.14
  79.4 1.0 collective-permute-done.14
  80.4 0.0 collective-permute-start.16
  80.4 0.2 convert_reduce_fusion
  80.6 1.1 collective-permute-start.15
  81.7 3.5 %collective-permute-done.16 = f32[320]{0:T(512)S(1)} collective-permute-done((f32[320]{0:T(512)S(1)}, f32[320]{0:T(512)S(1)}, u32[]{:S(2)}, u32[]{:S(2)}) %collective-permute-start.16) | collective-permute-done | bytes 1312 | tf_op jit(solution)/shard_map/ppermute | solution.py:237
  85.2 0.0 collective-permute-start.17
  85.3 0.1 add.233
  85.3 0.1 broadcast_in_dim.7
  85.4 0.3 collective-permute-done.15
  85.8 0.6 collective-permute-done.17
  86.4 0.1 multiply_convert_fusion
  86.5 0.1 broadcast_in_dim.8
  86.6 0.6 fusion.2
  87.2 20.8 %all_to_all.5 = bf16[16,40,512]{2,1,0:T(8,128)(2,1)S(1)} all-to-all(bf16[16,40,512]{2,1,0:T(8,128)(2,1)S(1)} %bitcast.31), channel_id=1, replica_groups=mesh['dp'=16,'mp'=8] {'dp'}, dimensions={0} | all-to-all | bytes 1310720 | tf_op jit(solution)/shard_map/all_to_all | solution.py:364
  108.0 0.2 add_reduce_fusion
  108.2 1.2 %fusion.3 = bf16[320,448]{1,0:T(8,128)(2,1)} fusion(bf16[640,512]{1,0:T(8,128)(2,1)S(1)} %bitcast.30, s32[640]{0:T(1024)S(1)} %fusion.14), kind=kOutput, calls=%fused_computation.10 | convolution fusion | flops 183705600 | bytes 944640 | tf_op jit(solution)/shard_map/dot_general | solution.py:371
  (19 shorter events, 0.1 us)
Async XLA Ops:
  10.9 2.2 %collective-permute-start = (bf16[320,1024]{1,0:T(8,128)(2,1)S(1)}, bf16[320,1024]{1,0:T(8,128)(2,1)S(1)}, u32[]{:S(2)}, u32[]{:S(2)}) collective-permute-start(bf16[320,1024]{1,0:T(8,128)(2,1)S(1)} %get-tuple-element.18), channel_id=1, source_target_pairs={{0,1},{1,0},{2,3},{3,2},{4,5},{5,4},{6,7},{7,6},{8,9},{9,8},{10,11... | collective-permute-start | bytes 1966088 | tf_op jit(solution)/shard_map/ppermute | solution.py:247
  13.1 51.8 %slice-start = ((s8[7340032]{0:T(1024)(128)(4,1)}), s8[4194304]{0:T(1024)(128)(4,1)S(1)}, s32[]{:S(2)}) async-start(s8[7340032]{0:T(1024)(128)(4,1)} %bitcast.20), calls=%async_computation.1 | async-start | bytes 8388608
  13.3 51.5 %slice-start.1 = ((s8[7340032]{0:T(1024)(128)(4,1)}), s8[3145728]{0:T(1024)(128)(4,1)S(1)}, s32[]{:S(2)}) async-start(s8[7340032]{0:T(1024)(128)(4,1)} %bitcast.20), calls=%async_computation.2 | async-start | bytes 6291456
  13.3 11.9 %collective-permute-start.1 = (bf16[320,1024]{1,0:T(8,128)(2,1)S(1)}, bf16[320,1024]{1,0:T(8,128)(2,1)S(1)}, u32[]{:S(2)}, u32[]{:S(2)}) collective-permute-start(bf16[320,1024]{1,0:T(8,128)(2,1)S(1)} %add_convert_fusion.3), channel_id=1, source_target_pairs={{0,2},{1,7},{2,4},{3,1},{4,6},{5,3},{6,0},{7,5},{8,10},{9,15},{10,... | collective-permute-start | bytes 1966088 | tf_op jit(solution)/shard_map/ppermute | solution.py:237
  22.4 3.1 %collective-permute-start.3 = (bf16[320,1024]{1,0:T(8,128)(2,1)S(1)}, bf16[320,1024]{1,0:T(8,128)(2,1)S(1)}, u32[]{:S(2)}, u32[]{:S(2)}) collective-permute-start(bf16[320,1024]{1,0:T(8,128)(2,1)S(1)} %get-tuple-element.26), channel_id=1, source_target_pairs={{0,1},{1,0},{2,3},{3,2},{4,5},{5,4},{6,7},{7,6},{8,9},{9,8},{10,11... | collective-permute-start | bytes 1966088 | tf_op jit(solution)/shard_map/ppermute | solution.py:247
  23.7 2.7 %collective-permute-start.5 = (bf16[320,1024]{1,0:T(8,128)(2,1)S(1)}, bf16[320,1024]{1,0:T(8,128)(2,1)S(1)}, u32[]{:S(2)}, u32[]{:S(2)}) collective-permute-start(bf16[320,1024]{1,0:T(8,128)(2,1)S(1)} %get-tuple-element.28), channel_id=1, source_target_pairs={{0,1},{1,0},{2,3},{3,2},{4,5},{5,4},{6,7},{7,6},{8,9},{9,8},{10,11... | collective-permute-start | bytes 1966088 | tf_op jit(solution)/shard_map/ppermute | solution.py:247
  25.2 2.9 %collective-permute-start.2 = (bf16[320,1024]{1,0:T(8,128)(2,1)S(1)}, bf16[320,1024]{1,0:T(8,128)(2,1)S(1)}, u32[]{:S(2)}, u32[]{:S(2)}) collective-permute-start(bf16[320,1024]{1,0:T(8,128)(2,1)S(1)} %get-tuple-element.24), channel_id=1, source_target_pairs={{0,1},{1,0},{2,3},{3,2},{4,5},{5,4},{6,7},{7,6},{8,9},{9,8},{10,11... | collective-permute-start | bytes 1966088 | tf_op jit(solution)/shard_map/ppermute | solution.py:247
  25.7 10.1 %collective-permute-start.4 = (bf16[320,1024]{1,0:T(8,128)(2,1)S(1)}, bf16[320,1024]{1,0:T(8,128)(2,1)S(1)}, u32[]{:S(2)}, u32[]{:S(2)}) collective-permute-start(bf16[320,1024]{1,0:T(8,128)(2,1)S(1)} %add_convert_fusion.2), channel_id=1, source_target_pairs={{0,3},{1,6},{2,5},{3,0},{4,7},{5,2},{6,1},{7,4},{8,11},{9,14},{10,... | collective-permute-start | bytes 1966088 | tf_op jit(solution)/shard_map/ppermute | solution.py:243
  26.4 9.4 %copy-start = (bf16[4,80,1024]{2,1,0:T(8,128)(2,1)S(1)}, bf16[4,80,1024]{2,1,0:T(8,128)(2,1)}, u32[]{:S(2)}) copy-start(bf16[4,80,1024]{2,1,0:T(8,128)(2,1)} %param.19) | copy-start | bytes 1966084
  26.7 17.8 %collective-permute-start.6 = (bf16[320,1024]{1,0:T(8,128)(2,1)S(1)}, bf16[320,1024]{1,0:T(8,128)(2,1)S(1)}, u32[]{:S(2)}, u32[]{:S(2)}) collective-permute-start(bf16[320,1024]{1,0:T(8,128)(2,1)S(1)} %add_convert_fusion.1), channel_id=1, source_target_pairs={{0,2},{1,7},{2,4},{3,1},{4,6},{5,3},{6,0},{7,5},{8,10},{9,15},{10,... | collective-permute-start | bytes 1966088 | tf_op jit(solution)/shard_map/ppermute | solution.py:237
  35.8 8.8 %copy-start.1 = (bf16[4,80,1024]{2,1,0:T(8,128)(2,1)S(1)}, bf16[4,80,1024]{2,1,0:T(8,128)(2,1)}, u32[]{:S(2)}) copy-start(bf16[4,80,1024]{2,1,0:T(8,128)(2,1)} %param.20) | copy-start | bytes 1966084
  45.8 18.3 %collective-permute-start.7 = (bf16[320,1024]{1,0:T(8,128)(2,1)S(1)}, bf16[320,1024]{1,0:T(8,128)(2,1)S(1)}, u32[]{:S(2)}, u32[]{:S(2)}) collective-permute-start(bf16[320,1024]{1,0:T(8,128)(2,1)S(1)} %get-tuple-element.32.refs_1_), channel_id=1, source_target_pairs={{0,2},{1,7},{2,4},{3,1},{4,6},{5,3},{6,0},{7,5},{8,10},{9,15},{10,... | collective-permute-start | bytes 1966088 | tf_op jit(solution)/shard_map/ppermute | solution.py:237
  45.8 18.3 %collective-permute-start.9 = (bf16[320,1024]{1,0:T(8,128)(2,1)S(1)}, bf16[320,1024]{1,0:T(8,128)(2,1)S(1)}, u32[]{:S(2)}, u32[]{:S(2)}) collective-permute-start(bf16[320,1024]{1,0:T(8,128)(2,1)S(1)} %get-tuple-element.32.refs_1_), channel_id=1, source_target_pairs={{0,7},{1,2},{2,1},{3,4},{4,3},{5,6},{6,5},{7,0},{8,15},{9,10},{10,... | collective-permute-start | bytes 1966088 | tf_op jit(solution)/shard_map/ppermute | solution.py:243
  46.6 18.3 %collective-permute-start.12 = (bf16[320,1024]{1,0:T(8,128)(2,1)S(1)}, bf16[320,1024]{1,0:T(8,128)(2,1)S(1)}, u32[]{:S(2)}, u32[]{:S(2)}) collective-permute-start(bf16[320,1024]{1,0:T(8,128)(2,1)S(1)} %get-tuple-element.32.refs_1_), channel_id=1, source_target_pairs={{0,1},{1,0},{2,3},{3,2},{4,5},{5,4},{6,7},{7,6},{8,9},{9,8},{10,11... | collective-permute-start | bytes 1966088 | tf_op jit(solution)/shard_map/ppermute | solution.py:247
  64.1 2.2 %collective-permute-start.11 = (bf16[320,1024]{1,0:T(8,128)(2,1)S(1)}, bf16[320,1024]{1,0:T(8,128)(2,1)S(1)}, u32[]{:S(2)}, u32[]{:S(2)}) collective-permute-start(bf16[320,1024]{1,0:T(8,128)(2,1)S(1)} %collective-permute-done.7.refs_1_), channel_id=1, source_target_pairs={{0,1},{1,0},{2,3},{3,2},{4,5},{5,4},{6,7},{7,6},{8,9},{9,8},{10,11... | collective-permute-start | bytes 1966088 | tf_op jit(solution)/shard_map/ppermute | solution.py:247
  64.1 3.6 %collective-permute-start.10 = (bf16[320,1024]{1,0:T(8,128)(2,1)S(1)}, bf16[320,1024]{1,0:T(8,128)(2,1)S(1)}, u32[]{:S(2)}, u32[]{:S(2)}) collective-permute-start(bf16[320,1024]{1,0:T(8,128)(2,1)S(1)} %collective-permute-done.9.refs_1_), channel_id=1, source_target_pairs={{0,1},{1,0},{2,3},{3,2},{4,5},{5,4},{6,7},{7,6},{8,9},{9,8},{10,11... | collective-permute-start | bytes 1966088 | tf_op jit(solution)/shard_map/ppermute | solution.py:247
  64.6 11.8 %collective-permute-start.8 = (bf16[320,1024]{1,0:T(8,128)(2,1)S(1)}, bf16[320,1024]{1,0:T(8,128)(2,1)S(1)}, u32[]{:S(2)}, u32[]{:S(2)}) collective-permute-start(bf16[320,1024]{1,0:T(8,128)(2,1)S(1)} %collective-permute-done.7.refs_1_), channel_id=1, source_target_pairs={{0,2},{1,7},{2,4},{3,1},{4,6},{5,3},{6,0},{7,5},{8,10},{9,15},{10,... | collective-permute-start | bytes 1966088 | tf_op jit(solution)/shard_map/ppermute | solution.py:237
  76.4 2.1 %collective-permute-start.13 = (bf16[320,1024]{1,0:T(8,128)(2,1)S(1)}, bf16[320,1024]{1,0:T(8,128)(2,1)S(1)}, u32[]{:S(2)}, u32[]{:S(2)}) collective-permute-start(bf16[320,1024]{1,0:T(8,128)(2,1)S(1)} %collective-permute-done.8.refs_0_), channel_id=1, source_target_pairs={{0,1},{1,0},{2,3},{3,2},{4,5},{5,4},{6,7},{7,6},{8,9},{9,8},{10,11... | collective-permute-start | bytes 1966088 | tf_op jit(solution)/shard_map/ppermute | solution.py:247
  77.0 2.5 %copy-start.3 = (s32[80]{0:T(128)S(1)}, s32[80]{0:T(128)}, u32[]{:S(2)}) copy-start(s32[80]{0:T(128)} %param.18) | copy-start | bytes 964
  77.0 8.3 %copy-start.2 = (bf16[448]{0:T(512)(128)(2,1)S(1)}, bf16[448]{0:T(512)(128)(2,1)}, u32[]{:S(2)}) copy-start(bf16[448]{0:T(512)(128)(2,1)} %param.23) | copy-start | bytes 2692
  79.2 1.2 %collective-permute-start.14 = (f32[320]{0:T(512)S(1)}, f32[320]{0:T(512)S(1)}, u32[]{:S(2)}, u32[]{:S(2)}) collective-permute-start(f32[320]{0:T(512)S(1)} %multiply_reduce_fusion), channel_id=1, source_target_pairs={{0,1},{1,0},{2,3},{3,2},{4,5},{5,4},{6,7},{7,6},{8,9},{9,8},{10,11... | collective-permute-start | bytes 3848 | tf_op jit(solution)/shard_map/ppermute | solution.py:247
  80.4 4.8 %collective-permute-start.16 = (f32[320]{0:T(512)S(1)}, f32[320]{0:T(512)S(1)}, u32[]{:S(2)}, u32[]{:S(2)}) collective-permute-start(f32[320]{0:T(512)S(1)} %add.235), channel_id=1, source_target_pairs={{0,2},{1,7},{2,4},{3,1},{4,6},{5,3},{6,0},{7,5},{8,10},{9,15},{10,... | collective-permute-start | bytes 3848 | tf_op jit(solution)/shard_map/ppermute | solution.py:237
  80.6 5.2 %collective-permute-start.15 = (f32[320]{0:T(512)S(1)}, f32[320]{0:T(512)S(1)}, u32[]{:S(2)}, u32[]{:S(2)}) collective-permute-start(f32[320]{0:T(512)S(1)} %add.235), channel_id=1, source_target_pairs={{0,4},{1,5},{2,6},{3,7},{4,0},{5,1},{6,2},{7,3},{8,12},{9,13},{10,... | collective-permute-start | bytes 3848 | tf_op jit(solution)/shard_map/ppermute | solution.py:232
  85.2 1.2 %collective-permute-start.17 = (f32[320]{0:T(512)S(1)}, f32[320]{0:T(512)S(1)}, u32[]{:S(2)}, u32[]{:S(2)}) collective-permute-start(f32[320]{0:T(512)S(1)} %collective-permute-done.16), channel_id=1, source_target_pairs={{0,1},{1,0},{2,3},{3,2},{4,5},{5,4},{6,7},{7,6},{8,9},{9,8},{10,11... | collective-permute-start | bytes 3848 | tf_op jit(solution)/shard_map/ppermute | solution.py:247

commit v7 on v6

--- a/solution.py
+++ b/solution.py
@@ -32,7 +32,7 @@
             at = pl.ds(pl.multiple_of(blocks_ref[k] * cols, cols), cols)
             return pltpu.make_async_copy(w_ref.at[:, at], w_buf.at[k], sems.at[k])
 
-        @pl.when(chunk == 0)
+        @pl.when(chunk == 1)
         def _():
             for k in range(count):
                 load(k).start()

time: 110 us -> 109 us (level)
  no operation moved by 1% of the time
where the time goes in v7:
time: 109 us
  waiting for transfers between devices  51.5 us (47%)
  Pallas kernels  22.4 us (21%)
  blocking collectives  20.8 us (19%)
  starting transfers between devices  7.79 us (7%)
  other arithmetic  3.57 us (3%)
  matrix products  1.71 us (2%)
    ppermute x5, waiting for transfers between devices, onward(): lax.ppermute(x, 'mp', [(i, (i + 2 - 4 * (i % 2)) % count) for i in range(...  38 us
    all_to_all x1, blocking collectives, local(): lax.all_to_all(sent.reshape(n_dp, slots // n_dp, -1), 'dp', 0, 0, tiled=T...  20.8 us
    pallas_call x1, Pallas kernels, attend_and_project(): pl.pallas_call(body, grid_spec=pltpu.PrefetchScalarGridSpec(num_scalar_pr...  9.87 us
    ppermute x2, waiting for transfers between devices, across(): return lax.ppermute(x, 'mp', moves)  7.69 us
    pallas_call x1, Pallas kernels, head_product(): pl.pallas_call(body, in_specs=[pl.BlockSpec(memory_space=pltpu.SMEM), pl....  7.27 us
    ppermute x10, waiting for transfers between devices, swap(): lax.ppermute(x, 'mp', [(i, i ^ 1) for i in range(lax.axis_size('mp'))])  5.53 us
    pallas_call x5, Pallas kernels, talker_product(): pl.pallas_call(body, in_specs=[pl.BlockSpec(memory_space=pltpu.SMEM), vme...  5.27 us
    ppermute x5, starting transfers between devices, onward(): lax.ppermute(x, 'mp', [(i, (i + 2 - 4 * (i % 2)) % count) for i in range(...  3.1 us
  transfers between devices with their start and end apart: 18, of which 13 were waited for; matrix products, arithmetic and copies ran while one was open for 2% of the time, Pallas kernels for 11%

profile of v7, /device:TPU:0, one launch (start us, length us, event | category | flops | bytes accessed | tf_op | source)
XLA Modules:
  0.0 109.1 jit_solution(2906550757883016757)
XLA Ops:
  0.7 0.1 pad_add_fusion.blocks_ref
  0.7 9.9 %shard_map.131 = (bf16[320,1024]{1,0:T(8,128)(2,1)S(1)}, bf16[320,1024]{1,0:T(8,128)(2,1)S(1)}, bf16[320,1024]{1,0:T(8,128)(2,1)S(1)}) custom-call(s32[2]{0:T(128)S(1)} %pad_add_fusion.blocks_ref, s32[80]{0:T(128)} %len_ref.1, bf16[4,80,1024]{2,1,0:T(8,128)(2,1)} %q_ref.1, bf16[4,80,128]{2,1,0:T(8,128)(2,1)} %tk_ref.1, bf16[4,80,128]{2,1,0:T(8,128)(2,1)} %tv_ref.1, ...), custom_call_target="tpu_custom_call" | custom-call | flops 1342177280 | bytes 33554432 | tf_op jit(solution)/shard_map/pallas_call | solution.py:105
  10.6 0.1 collective-permute-start
  10.8 0.1 stack.53.blocks_ref
  10.9 1.9 %collective-permute-done = bf16[320,1024]{1,0:T(8,128)(2,1)S(1)} collective-permute-done((bf16[320,1024]{1,0:T(8,128)(2,1)S(1)}, bf16[320,1024]{1,0:T(8,128)(2,1)S(1)}, u32[]{:S(2)}, u32[]{:S(2)}) %collective-permute-start) | collective-permute-done | bytes 655392 | tf_op jit(solution)/shard_map/ppermute | solution.py:247
  12.8 0.2 add_convert_fusion.3
  13.0 0.0 slice-start.1
  13.1 1.7 %collective-permute-start.1 = (bf16[320,1024]{1,0:T(8,128)(2,1)S(1)}, bf16[320,1024]{1,0:T(8,128)(2,1)S(1)}, u32[]{:S(2)}, u32[]{:S(2)}) collective-permute-start(bf16[320,1024]{1,0:T(8,128)(2,1)S(1)} %add_convert_fusion.3), channel_id=1, source_target_pairs={{0,2},{1,7},{2,4},{3,1},{4,6},{5,3},{6,0},{7,5},{8,10},{9,15},{10,... | collective-permute-start | bytes 1966088 | tf_op jit(solution)/shard_map/ppermute | solution.py:237
  14.8 7.3 %shard_map.132 = (bf16[320,1024]{1,0:T(8,128)(2,1)S(1)}, bf16[320,1024]{1,0:T(8,128)(2,1)S(1)}, bf16[320,1024]{1,0:T(8,128)(2,1)S(1)}, bf16[320,1024]{1,0:T(8,12...) custom-call(s32[6]{0:T(128)S(1)} %stack.53.blocks_ref, ...), custom_call_target="tpu_custom_call" | custom-call | flops 4026531840 | bytes 16515072 | tf_op jit(solution)/shard_map/pallas_call | solution.py:161
  22.1 1.4 %collective-permute-start.3 = (bf16[320,1024]{1,0:T(8,128)(2,1)S(1)}, bf16[320,1024]{1,0:T(8,128)(2,1)S(1)}, u32[]{:S(2)}, u32[]{:S(2)}) collective-permute-start(bf16[320,1024]{1,0:T(8,128)(2,1)S(1)} %get-tuple-element.26), channel_id=1, source_target_pairs={{0,1},{1,0},{2,3},{3,2},{4,5},{5,4},{6,7},{7,6},{8,9},{9,8},{10,11... | collective-permute-start | bytes 1966088 | tf_op jit(solution)/shard_map/ppermute | solution.py:247
  23.4 0.1 collective-permute-start.5
  23.5 1.4 %collective-permute-done.1 = bf16[320,1024]{1,0:T(8,128)(2,1)S(1)} collective-permute-done((bf16[320,1024]{1,0:T(8,128)(2,1)S(1)}, bf16[320,1024]{1,0:T(8,128)(2,1)S(1)}, u32[]{:S(2)}, u32[]{:S(2)}) %collective-permute-start.1) | collective-permute-done | bytes 655392 | tf_op jit(solution)/shard_map/ppermute | solution.py:237
  24.9 0.0 collective-permute-start.2
  24.9 0.2 collective-permute-done.3
  25.2 0.2 add_convert_fusion.2
  25.4 0.5 collective-permute-start.4
  25.9 0.2 collective-permute-done.5
  26.1 0.3 add_convert_fusion.1
  26.4 1.4 %collective-permute-start.6 = (bf16[320,1024]{1,0:T(8,128)(2,1)S(1)}, bf16[320,1024]{1,0:T(8,128)(2,1)S(1)}, u32[]{:S(2)}, u32[]{:S(2)}) collective-permute-start(bf16[320,1024]{1,0:T(8,128)(2,1)S(1)} %add_convert_fusion.1), channel_id=1, source_target_pairs={{0,2},{1,7},{2,4},{3,1},{4,6},{5,3},{6,0},{7,5},{8,10},{9,15},{10,... | collective-permute-start | bytes 1966088 | tf_op jit(solution)/shard_map/ppermute | solution.py:237
  27.8 0.0 collective-permute-done.2
  27.8 7.7 %collective-permute-done.4 = bf16[320,1024]{1,0:T(8,128)(2,1)S(1)} collective-permute-done((bf16[320,1024]{1,0:T(8,128)(2,1)S(1)}, bf16[320,1024]{1,0:T(8,128)(2,1)S(1)}, u32[]{:S(2)}, u32[]{:S(2)}) %collective-permute-start.4) | collective-permute-done | bytes 655392 | tf_op jit(solution)/shard_map/ppermute | solution.py:243
  35.5 0.5 fusion.1
  36.0 8.3 %collective-permute-done.6 = bf16[320,1024]{1,0:T(8,128)(2,1)S(1)} collective-permute-done((bf16[320,1024]{1,0:T(8,128)(2,1)S(1)}, bf16[320,1024]{1,0:T(8,128)(2,1)S(1)}, u32[]{:S(2)}, u32[]{:S(2)}) %collective-permute-start.6) | collective-permute-done | bytes 655392 | tf_op jit(solution)/shard_map/ppermute | solution.py:237
  44.3 1.2 %bitcast_add_fusion = (bf16[320,1024]{1,0:T(8,128)(2,1)S(1)}, bf16[320,1024]{1,0:T(8,128)(2,1)}) fusion(bf16[4,80,1024]{2,1,0:T(8,128)(2,1)S(1)} %copy-done.1, f32[320,1024]{1,0:T(8,128)S(1)} %fusion.1, bf16[320,1024]{1,0:T(8,128)(2,1)S(1)} %collective-permute-done.6), kind=kLoop, calls=%fused_computation.12 | loop fusion | flops 1310720 | bytes 3932160 | tf_op jit(solution)/shard_map/add | solution.py:320
  45.5 0.0 collective-permute-start.7
  45.5 0.8 collective-permute-start.9
  46.3 0.1 collective-permute-start.12
  46.4 17.4 %collective-permute-done.7.refs_1_ = bf16[320,1024]{1,0:T(8,128)(2,1)S(1)} collective-permute-done((bf16[320,1024]{1,0:T(8,128)(2,1)S(1)}, bf16[320,1024]{1,0:T(8,128)(2,1)S(1)}, u32[]{:S(2)}, u32[]{:S(2)}) %collective-permute-start.7) | collective-permute-done | bytes 655392 | tf_op jit(solution)/shard_map/ppermute | solution.py:237
  63.8 0.0 collective-permute-start.11
  63.8 0.0 collective-permute-done.9.refs_1_
  63.8 0.5 collective-permute-start.10
  64.3 0.0 collective-permute-start.8
  64.3 0.1 pad_add_fusion.3.blocks_ref
  64.4 0.1 pad_add_fusion.2.blocks_ref
  64.5 0.1 pad_add_fusion.1.blocks_ref
  64.6 0.0 collective-permute-done.12.refs_0_
  64.6 1.4 %shard_map.133.refs_2_ = f32[320,448]{1,0:T(8,128)S(1)} custom-call(s32[2]{0:T(128)S(1)} %pad_add_fusion.3.blocks_ref, bf16[448,8192]{1,0:T(8,128)(2,1)S(1)} %bitcast.22, bf16[320,1024]{1,0:T(8,128)(2,1)S(1)} %collective-permute-done.12.refs_0_, bf16[320,1024]{1,0:T(8,128)(2,1)S(1)} %get-tuple-element.32.refs_1_), custom_call_target="tpu_custom_call" | custom-call | flops 587202560 | bytes 3145728 | tf_op jit(solution)/shard_map/pallas_call | solution.py:212
  66.0 1.4 %shard_map.134.refs_2_ = f32[320,448]{1,0:T(8,128)S(1)} custom-call(s32[2]{0:T(128)S(1)} %pad_add_fusion.2.blocks_ref, bf16[448,8192]{1,0:T(8,128)(2,1)S(1)} %bitcast.23, bf16[320,1024]{1,0:T(8,128)(2,1)S(1)} %collective-permute-done.11.refs_0_, bf16[320,1024]{1,0:T(8,128)(2,1)S(1)} %collective-permute-done.7.refs_1_, f32[320,448]{1,0:T(8,128)S(1)} %shard_map.133.refs_2_), custom_call_target="tpu_custom_call" | custom-call | flops 587202560 | bytes 3145728 | tf_op jit(solution)/shard_map/pallas_call | solution.py:212
  67.4 1.4 %shard_map.135.refs_1_ = f32[320,448]{1,0:T(8,128)S(1)} custom-call(s32[2]{0:T(128)S(1)} %pad_add_fusion.1.blocks_ref, bf16[448,8192]{1,0:T(8,128)(2,1)S(1)} %bitcast.24, bf16[320,1024]{1,0:T(8,128)(2,1)S(1)} %collective-permute-done.10.refs_0_, bf16[320,1024]{1,0:T(8,128)(2,1)S(1)} %collective-permute-done.9.refs_1_, f32[320,448]{1,0:T(8,128)S(1)} %shard_map.134.refs_2_), custom_call_target="tpu_custom_call" | custom-call | flops 587202560 | bytes 3145728 | tf_op jit(solution)/shard_map/pallas_call | solution.py:212
  68.8 7.3 %collective-permute-done.8.refs_0_ = bf16[320,1024]{1,0:T(8,128)(2,1)S(1)} collective-permute-done((bf16[320,1024]{1,0:T(8,128)(2,1)S(1)}, bf16[320,1024]{1,0:T(8,128)(2,1)S(1)}, u32[]{:S(2)}, u32[]{:S(2)}) %collective-permute-start.8) | collective-permute-done | bytes 655392 | tf_op jit(solution)/shard_map/ppermute | solution.py:237
  76.1 0.0 collective-permute-start.13
  76.1 0.5 shard_map.136.refs_1_
  76.7 0.0 copy-start.3
  76.7 0.0 copy-start.2
  76.7 1.5 %collective-permute-done.13.refs_0_ = bf16[320,1024]{1,0:T(8,128)(2,1)S(1)} collective-permute-done((bf16[320,1024]{1,0:T(8,128)(2,1)S(1)}, bf16[320,1024]{1,0:T(8,128)(2,1)S(1)}, u32[]{:S(2)}, u32[]{:S(2)}) %collective-permute-start.13) | collective-permute-done | bytes 655392 | tf_op jit(solution)/shard_map/ppermute | solution.py:247
  78.2 0.5 shard_map.137
  78.8 0.1 multiply_reduce_fusion
  78.9 0.2 collective-permute-start.14
  79.1 1.0 collective-permute-done.14
  80.1 0.0 collective-permute-start.16
  80.1 0.2 convert_reduce_fusion
  80.3 1.1 collective-permute-start.15
  81.4 3.5 %collective-permute-done.16 = f32[320]{0:T(512)S(1)} collective-permute-done((f32[320]{0:T(512)S(1)}, f32[320]{0:T(512)S(1)}, u32[]{:S(2)}, u32[]{:S(2)}) %collective-permute-start.16) | collective-permute-done | bytes 1312 | tf_op jit(solution)/shard_map/ppermute | solution.py:237
  84.9 0.0 collective-permute-start.17
  85.0 0.1 add.233
  85.1 0.1 broadcast_in_dim.7
  85.1 0.3 collective-permute-done.15
  85.5 0.6 collective-permute-done.17
  86.1 0.1 multiply_convert_fusion
  86.2 0.1 broadcast_in_dim.8
  86.4 0.6 fusion.2
  86.9 20.8 %all_to_all.5 = bf16[16,40,512]{2,1,0:T(8,128)(2,1)S(1)} all-to-all(bf16[16,40,512]{2,1,0:T(8,128)(2,1)S(1)} %bitcast.31), channel_id=1, replica_groups=mesh['dp'=16,'mp'=8] {'dp'}, dimensions={0} | all-to-all | bytes 1310720 | tf_op jit(solution)/shard_map/all_to_all | solution.py:364
  107.7 0.2 add_reduce_fusion
  108.0 1.2 %fusion.3 = bf16[320,448]{1,0:T(8,128)(2,1)} fusion(bf16[640,512]{1,0:T(8,128)(2,1)S(1)} %bitcast.30, s32[640]{0:T(1024)S(1)} %fusion.14), kind=kOutput, calls=%fused_computation.10 | convolution fusion | flops 183705600 | bytes 944640 | tf_op jit(solution)/shard_map/dot_general | solution.py:371
  (19 shorter events, 0.1 us)
Async XLA Ops:
  10.6 2.2 %collective-permute-start = (bf16[320,1024]{1,0:T(8,128)(2,1)S(1)}, bf16[320,1024]{1,0:T(8,128)(2,1)S(1)}, u32[]{:S(2)}, u32[]{:S(2)}) collective-permute-start(bf16[320,1024]{1,0:T(8,128)(2,1)S(1)} %get-tuple-element.18), channel_id=1, source_target_pairs={{0,1},{1,0},{2,3},{3,2},{4,5},{5,4},{6,7},{7,6},{8,9},{9,8},{10,11... | collective-permute-start | bytes 1966088 | tf_op jit(solution)/shard_map/ppermute | solution.py:247
  12.8 51.8 %slice-start = ((s8[7340032]{0:T(1024)(128)(4,1)}), s8[4194304]{0:T(1024)(128)(4,1)S(1)}, s32[]{:S(2)}) async-start(s8[7340032]{0:T(1024)(128)(4,1)} %bitcast.20), calls=%async_computation.1 | async-start | bytes 8388608
  13.0 51.5 %slice-start.1 = ((s8[7340032]{0:T(1024)(128)(4,1)}), s8[3145728]{0:T(1024)(128)(4,1)S(1)}, s32[]{:S(2)}) async-start(s8[7340032]{0:T(1024)(128)(4,1)} %bitcast.20), calls=%async_computation.2 | async-start | bytes 6291456
  13.1 11.9 %collective-permute-start.1 = (bf16[320,1024]{1,0:T(8,128)(2,1)S(1)}, bf16[320,1024]{1,0:T(8,128)(2,1)S(1)}, u32[]{:S(2)}, u32[]{:S(2)}) collective-permute-start(bf16[320,1024]{1,0:T(8,128)(2,1)S(1)} %add_convert_fusion.3), channel_id=1, source_target_pairs={{0,2},{1,7},{2,4},{3,1},{4,6},{5,3},{6,0},{7,5},{8,10},{9,15},{10,... | collective-permute-start | bytes 1966088 | tf_op jit(solution)/shard_map/ppermute | solution.py:237
  22.1 3.1 %collective-permute-start.3 = (bf16[320,1024]{1,0:T(8,128)(2,1)S(1)}, bf16[320,1024]{1,0:T(8,128)(2,1)S(1)}, u32[]{:S(2)}, u32[]{:S(2)}) collective-permute-start(bf16[320,1024]{1,0:T(8,128)(2,1)S(1)} %get-tuple-element.26), channel_id=1, source_target_pairs={{0,1},{1,0},{2,3},{3,2},{4,5},{5,4},{6,7},{7,6},{8,9},{9,8},{10,11... | collective-permute-start | bytes 1966088 | tf_op jit(solution)/shard_map/ppermute | solution.py:247
  23.4 2.7 %collective-permute-start.5 = (bf16[320,1024]{1,0:T(8,128)(2,1)S(1)}, bf16[320,1024]{1,0:T(8,128)(2,1)S(1)}, u32[]{:S(2)}, u32[]{:S(2)}) collective-permute-start(bf16[320,1024]{1,0:T(8,128)(2,1)S(1)} %get-tuple-element.28), channel_id=1, source_target_pairs={{0,1},{1,0},{2,3},{3,2},{4,5},{5,4},{6,7},{7,6},{8,9},{9,8},{10,11... | collective-permute-start | bytes 1966088 | tf_op jit(solution)/shard_map/ppermute | solution.py:247
  24.9 2.9 %collective-permute-start.2 = (bf16[320,1024]{1,0:T(8,128)(2,1)S(1)}, bf16[320,1024]{1,0:T(8,128)(2,1)S(1)}, u32[]{:S(2)}, u32[]{:S(2)}) collective-permute-start(bf16[320,1024]{1,0:T(8,128)(2,1)S(1)} %get-tuple-element.24), channel_id=1, source_target_pairs={{0,1},{1,0},{2,3},{3,2},{4,5},{5,4},{6,7},{7,6},{8,9},{9,8},{10,11... | collective-permute-start | bytes 1966088 | tf_op jit(solution)/shard_map/ppermute | solution.py:247
  25.4 10.1 %collective-permute-start.4 = (bf16[320,1024]{1,0:T(8,128)(2,1)S(1)}, bf16[320,1024]{1,0:T(8,128)(2,1)S(1)}, u32[]{:S(2)}, u32[]{:S(2)}) collective-permute-start(bf16[320,1024]{1,0:T(8,128)(2,1)S(1)} %add_convert_fusion.2), channel_id=1, source_target_pairs={{0,3},{1,6},{2,5},{3,0},{4,7},{5,2},{6,1},{7,4},{8,11},{9,14},{10,... | collective-permute-start | bytes 1966088 | tf_op jit(solution)/shard_map/ppermute | solution.py:243
  26.1 9.4 %copy-start = (bf16[4,80,1024]{2,1,0:T(8,128)(2,1)S(1)}, bf16[4,80,1024]{2,1,0:T(8,128)(2,1)}, u32[]{:S(2)}) copy-start(bf16[4,80,1024]{2,1,0:T(8,128)(2,1)} %param.19) | copy-start | bytes 1966084
  26.4 17.8 %collective-permute-start.6 = (bf16[320,1024]{1,0:T(8,128)(2,1)S(1)}, bf16[320,1024]{1,0:T(8,128)(2,1)S(1)}, u32[]{:S(2)}, u32[]{:S(2)}) collective-permute-start(bf16[320,1024]{1,0:T(8,128)(2,1)S(1)} %add_convert_fusion.1), channel_id=1, source_target_pairs={{0,2},{1,7},{2,4},{3,1},{4,6},{5,3},{6,0},{7,5},{8,10},{9,15},{10,... | collective-permute-start | bytes 1966088 | tf_op jit(solution)/shard_map/ppermute | solution.py:237
  35.5 8.8 %copy-start.1 = (bf16[4,80,1024]{2,1,0:T(8,128)(2,1)S(1)}, bf16[4,80,1024]{2,1,0:T(8,128)(2,1)}, u32[]{:S(2)}) copy-start(bf16[4,80,1024]{2,1,0:T(8,128)(2,1)} %param.20) | copy-start | bytes 1966084
  45.5 18.3 %collective-permute-start.7 = (bf16[320,1024]{1,0:T(8,128)(2,1)S(1)}, bf16[320,1024]{1,0:T(8,128)(2,1)S(1)}, u32[]{:S(2)}, u32[]{:S(2)}) collective-permute-start(bf16[320,1024]{1,0:T(8,128)(2,1)S(1)} %get-tuple-element.32.refs_1_), channel_id=1, source_target_pairs={{0,2},{1,7},{2,4},{3,1},{4,6},{5,3},{6,0},{7,5},{8,10},{9,15},{10,... | collective-permute-start | bytes 1966088 | tf_op jit(solution)/shard_map/ppermute | solution.py:237
  45.5 18.3 %collective-permute-start.9 = (bf16[320,1024]{1,0:T(8,128)(2,1)S(1)}, bf16[320,1024]{1,0:T(8,128)(2,1)S(1)}, u32[]{:S(2)}, u32[]{:S(2)}) collective-permute-start(bf16[320,1024]{1,0:T(8,128)(2,1)S(1)} %get-tuple-element.32.refs_1_), channel_id=1, source_target_pairs={{0,7},{1,2},{2,1},{3,4},{4,3},{5,6},{6,5},{7,0},{8,15},{9,10},{10,... | collective-permute-start | bytes 1966088 | tf_op jit(solution)/shard_map/ppermute | solution.py:243
  46.3 18.3 %collective-permute-start.12 = (bf16[320,1024]{1,0:T(8,128)(2,1)S(1)}, bf16[320,1024]{1,0:T(8,128)(2,1)S(1)}, u32[]{:S(2)}, u32[]{:S(2)}) collective-permute-start(bf16[320,1024]{1,0:T(8,128)(2,1)S(1)} %get-tuple-element.32.refs_1_), channel_id=1, source_target_pairs={{0,1},{1,0},{2,3},{3,2},{4,5},{5,4},{6,7},{7,6},{8,9},{9,8},{10,11... | collective-permute-start | bytes 1966088 | tf_op jit(solution)/shard_map/ppermute | solution.py:247
  63.8 2.2 %collective-permute-start.11 = (bf16[320,1024]{1,0:T(8,128)(2,1)S(1)}, bf16[320,1024]{1,0:T(8,128)(2,1)S(1)}, u32[]{:S(2)}, u32[]{:S(2)}) collective-permute-start(bf16[320,1024]{1,0:T(8,128)(2,1)S(1)} %collective-permute-done.7.refs_1_), channel_id=1, source_target_pairs={{0,1},{1,0},{2,3},{3,2},{4,5},{5,4},{6,7},{7,6},{8,9},{9,8},{10,11... | collective-permute-start | bytes 1966088 | tf_op jit(solution)/shard_map/ppermute | solution.py:247
  63.8 3.6 %collective-permute-start.10 = (bf16[320,1024]{1,0:T(8,128)(2,1)S(1)}, bf16[320,1024]{1,0:T(8,128)(2,1)S(1)}, u32[]{:S(2)}, u32[]{:S(2)}) collective-permute-start(bf16[320,1024]{1,0:T(8,128)(2,1)S(1)} %collective-permute-done.9.refs_1_), channel_id=1, source_target_pairs={{0,1},{1,0},{2,3},{3,2},{4,5},{5,4},{6,7},{7,6},{8,9},{9,8},{10,11... | collective-permute-start | bytes 1966088 | tf_op jit(solution)/shard_map/ppermute | solution.py:247
  64.3 11.8 %collective-permute-start.8 = (bf16[320,1024]{1,0:T(8,128)(2,1)S(1)}, bf16[320,1024]{1,0:T(8,128)(2,1)S(1)}, u32[]{:S(2)}, u32[]{:S(2)}) collective-permute-start(bf16[320,1024]{1,0:T(8,128)(2,1)S(1)} %collective-permute-done.7.refs_1_), channel_id=1, source_target_pairs={{0,2},{1,7},{2,4},{3,1},{4,6},{5,3},{6,0},{7,5},{8,10},{9,15},{10,... | collective-permute-start | bytes 1966088 | tf_op jit(solution)/shard_map/ppermute | solution.py:237
  76.1 2.1 %collective-permute-start.13 = (bf16[320,1024]{1,0:T(8,128)(2,1)S(1)}, bf16[320,1024]{1,0:T(8,128)(2,1)S(1)}, u32[]{:S(2)}, u32[]{:S(2)}) collective-permute-start(bf16[320,1024]{1,0:T(8,128)(2,1)S(1)} %collective-permute-done.8.refs_0_), channel_id=1, source_target_pairs={{0,1},{1,0},{2,3},{3,2},{4,5},{5,4},{6,7},{7,6},{8,9},{9,8},{10,11... | collective-permute-start | bytes 1966088 | tf_op jit(solution)/shard_map/ppermute | solution.py:247
  76.7 2.5 %copy-start.3 = (s32[80]{0:T(128)S(1)}, s32[80]{0:T(128)}, u32[]{:S(2)}) copy-start(s32[80]{0:T(128)} %param.18) | copy-start | bytes 964
  76.7 8.3 %copy-start.2 = (bf16[448]{0:T(512)(128)(2,1)S(1)}, bf16[448]{0:T(512)(128)(2,1)}, u32[]{:S(2)}) copy-start(bf16[448]{0:T(512)(128)(2,1)} %param.23) | copy-start | bytes 2692
  78.9 1.2 %collective-permute-start.14 = (f32[320]{0:T(512)S(1)}, f32[320]{0:T(512)S(1)}, u32[]{:S(2)}, u32[]{:S(2)}) collective-permute-start(f32[320]{0:T(512)S(1)} %multiply_reduce_fusion), channel_id=1, source_target_pairs={{0,1},{1,0},{2,3},{3,2},{4,5},{5,4},{6,7},{7,6},{8,9},{9,8},{10,11... | collective-permute-start | bytes 3848 | tf_op jit(solution)/shard_map/ppermute | solution.py:247
  80.1 4.8 %collective-permute-start.16 = (f32[320]{0:T(512)S(1)}, f32[320]{0:T(512)S(1)}, u32[]{:S(2)}, u32[]{:S(2)}) collective-permute-start(f32[320]{0:T(512)S(1)} %add.235), channel_id=1, source_target_pairs={{0,2},{1,7},{2,4},{3,1},{4,6},{5,3},{6,0},{7,5},{8,10},{9,15},{10,... | collective-permute-start | bytes 3848 | tf_op jit(solution)/shard_map/ppermute | solution.py:237
  80.3 5.2 %collective-permute-start.15 = (f32[320]{0:T(512)S(1)}, f32[320]{0:T(512)S(1)}, u32[]{:S(2)}, u32[]{:S(2)}) collective-permute-start(f32[320]{0:T(512)S(1)} %add.235), channel_id=1, source_target_pairs={{0,4},{1,5},{2,6},{3,7},{4,0},{5,1},{6,2},{7,3},{8,12},{9,13},{10,... | collective-permute-start | bytes 3848 | tf_op jit(solution)/shard_map/ppermute | solution.py:232
  84.9 1.2 %collective-permute-start.17 = (f32[320]{0:T(512)S(1)}, f32[320]{0:T(512)S(1)}, u32[]{:S(2)}, u32[]{:S(2)}) collective-permute-start(f32[320]{0:T(512)S(1)} %collective-permute-done.16), channel_id=1, source_target_pairs={{0,1},{1,0},{2,3},{3,2},{4,5},{5,4},{6,7},{7,6},{8,9},{9,8},{10,11... | collective-permute-start | bytes 3848 | tf_op jit(solution)/shard_map/ppermute | solution.py:247
